TPU v7x, 128 devices: a whole 4x4x4 slice. The times are simulated.
128 devices in a mesh: ch: 4 (over z_lo, core), seq: 32 (over x, z_hi, y).
Axes of the slice: x: 4, y: 4, z: 4 (z_hi: 2, z_lo: 2; z = z_hi * 2 + z_lo), core: 2. Of those that a mesh axis runs over, the one named last changes fastest.
Arguments:
- gate_proj: bfloat16 [12288, 8192], P('seq', 'ch'), may hold values from -120 to 120
- key_proj: bfloat16 [12288, 8192], P('seq', 'ch'), may hold values from -6 to 6
- value_proj: bfloat16 [12288, 8192], P('seq', 'ch'), may hold values from -6 to 6
- rates: float32 [16, 8192], P(None, 'ch'), may hold values from 0 to 1, as said below
- residues: float32 [16, 8192], P(None, 'ch'), may hold values from -1 to 1
- skip_gain: float32 [8192], P('ch'), may hold values from -3 to 3
- norm_gain: float32 [8192], P('ch'), may hold values from 0.1 to 1.9
Outputs:
- output: bfloat16 [12288, 8192], P('seq', 'ch')
Inputs may be any that keep to these rules, and one draw needn't show every extreme that they name: `rates`: each rate lies either in a slow band, between 0.1 / 12288 and 200 / 12288, or in a fast band, between 1/50 and 1/30; which modes lie in which band varies from channel to channel.
All inputs are finite; a program needn't handle non-finite values.
Results may differ from a plain program's by a relative error of at most 0.001.
Values sent between devices are 32-bit elements; how exact they have to be, the bound alone decides.
No kernel may reach another device: no remote copies, remote signals or barrier semaphores. Data moves between devices by JAX's collectives and lax.ppermute only.
A program may use at most 192 MiB of HBM per device.

v0:
```python
import jax
import jax.numpy as jnp
import numpy as np
from jax import lax
from jax.sharding import PartitionSpec as P

D = 8192


block_len = 16


def from_behind(shard, axis, by):
    size = lax.axis_size(axis)
    pairs = [(i, i + by) for i in range(size) if 0 <= i + by < size]
    return lax.ppermute(shard, axis, pairs)


def make_tables(rate_part, residue_part, span_len):
    lag_steps = jnp.arange(block_len, dtype=jnp.float32)[:, None, None]
    read_weights = residue_part[None] * jnp.exp(-rate_part[None] * lag_steps)
    short_filter = jnp.sum(read_weights, axis=1)
    end_weights = jnp.exp(-rate_part[None] * (block_len - lag_steps))
    span_decay = jnp.exp(-rate_part * span_len)
    block_decay = jnp.exp(-rate_part * float(block_len))
    return (short_filter, end_weights, read_weights, span_decay, block_decay)


def combine_pairs(earlier, later):
    return (earlier[0] * later[0], earlier[1] * later[0] + later[1])


def body(gate_proj, key_proj, value_proj, rates, residues, skip_gain, norm_gain):
    size_tokens, channels = gate_proj.shape
    num_blocks = size_tokens // block_len
    highest = lax.Precision.HIGHEST
    share = channels // lax.axis_size("seq")
    first_channel = lax.axis_index("seq") * share
    rate_part = lax.dynamic_slice_in_dim(rates, first_channel, share, 1)
    residue_part = lax.dynamic_slice_in_dim(residues, first_channel, share, 1)
    pieces = make_tables(rate_part, residue_part, float(size_tokens))
    short_filter, end_weights, read_weights, span_decay, block_decay = (
        lax.all_gather(pieces[0], "seq", axis=1, tiled=True),
        lax.all_gather(pieces[1], "seq", axis=2, tiled=True),
        lax.all_gather(pieces[2], "seq", axis=2, tiled=True),
        lax.all_gather(pieces[3], "seq", axis=1, tiled=True),
        lax.all_gather(pieces[4], "seq", axis=1, tiled=True),
    )
    offsets = np.arange(block_len)[:, None] - np.arange(block_len)[None, :]
    lower = (offsets >= 0).astype(np.float32)[:, :, None]
    toeplitz = short_filter[np.maximum(offsets, 0)] * lower
    signal = key_proj.astype(jnp.float32) * value_proj.astype(jnp.float32)
    signal_blocks = signal.reshape(num_blocks, block_len, channels)
    inner_part = jnp.einsum("hgc,bgc->bhc", toeplitz, signal_blocks, precision=highest)
    block_ends = jnp.einsum("gnc,bgc->bnc", end_weights, signal_blocks, precision=highest)
    decays = jnp.broadcast_to(block_decay[None], block_ends.shape)
    powers, running = lax.associative_scan(combine_pairs, (decays, block_ends), axis=0)
    start_local = jnp.concatenate([jnp.zeros_like(running[:1]), running[:-1]], axis=0)
    start_power = jnp.concatenate([jnp.ones_like(powers[:1]), powers[:-1]], axis=0)
    local_end = running[-1]

    def pass_state(turn_index, carry):
        state_out, incoming = carry
        incoming = from_behind(state_out, "seq", 1)
        return (span_decay * incoming + local_end, incoming)

    carried = lax.fori_loop(
        0, lax.axis_size("seq") - 1, pass_state, (local_end, jnp.zeros_like(local_end))
    )
    state_in = carried[1]
    states = start_local + start_power * state_in[None]
    outer_part = jnp.einsum("hnc,bnc->bhc", read_weights, states, precision=highest)
    conv = (inner_part + outer_part).reshape(size_tokens, channels)
    gated_mix = gate_proj.astype(jnp.float32) * (conv + skip_gain[None, :] * signal)
    token_power = lax.psum(jnp.sum(gated_mix * gated_mix, axis=1), "ch") / D
    output = gated_mix * lax.rsqrt(token_power + 1e-06)[:, None] * norm_gain[None, :]
    return output.astype(jnp.bfloat16)


def solution(mesh):
    placed = (
        P("seq", "ch"),
        P("seq", "ch"),
        P("seq", "ch"),
        P(None, "ch"),
        P(None, "ch"),
        P("ch"),
        P("ch"),
    )
    return jax.shard_map(
        body, mesh=mesh, in_specs=placed, out_specs=P("seq", "ch"), check_vma=False
    )
```

profile of v0, /device:TPU:3, one launch (start us, length us, event | category | flops | bytes accessed | tf_op | source)
XLA Modules:
  0.0 938.5 jit_solution(12385076184783368435)
XLA Ops:
  13.3 12.4 %copy.293 = f32[24,16,2048]{0,1,2:T(8,128)} copy(f32[24,16,2048]{2,1,0:T(8,128)} %bitcast.79) | data formatting | bytes 6291456 | tf_op jit(solution)/shard_map/reshape | solution.py:53
  25.7 72.1 %all-gather.1 = f32[32,64,16]{1,2,0:T(8,128)S(1)} all-gather(f32[1,64,16]{1,2,0:T(8,128)S(1)} %exponential_bitcast_fusion.1), channel_id=1, replica_groups=mesh['ch'=4,'seq'=32] {'seq'}, dimensions={0}, use_global_device_ids=true | all-gather | bytes 135168 | tf_op jit(solution)/shard_map/all_gather | solution.py:47
  98.9 71.5 %all-gather.2 = f32[32,64,16]{1,2,0:T(8,128)S(1)} all-gather(f32[1,64,16]{1,2,0:T(8,128)S(1)} %get-tuple-element.47), channel_id=1, replica_groups=mesh['ch'=4,'seq'=32] {'seq'}, dimensions={0}, use_global_device_ids=true | all-gather | bytes 135168 | tf_op jit(solution)/shard_map/all_gather | solution.py:46
  170.6 76.7 %all-gather = f32[32,64,16]{1,2,0:T(8,128)S(1)} all-gather(f32[1,64,16]{1,2,0:T(8,128)S(1)} %copy.290), channel_id=1, replica_groups=mesh['ch'=4,'seq'=32] {'seq'}, dimensions={0}, use_global_device_ids=true | all-gather | bytes 135168 | tf_op jit(solution)/shard_map/all_gather | solution.py:43
  249.0 11.4 %copy.292 = f32[16,16,2048]{1,0,2:T(8,128)} copy(f32[16,16,2048]{2,1,0:T(8,128)S(1)} %bitcast.80) | data formatting | bytes 4194304 | tf_op jit(solution)/shard_map/gather | solution.py:51
  261.9 23.7 %fusion = f32[2048,24,16]{1,2,0:T(8,128)} fusion(f32[24,16,2048]{0,1,2:T(8,128)} %copy.293, f32[16,16,2048]{1,0,2:T(8,128)} %copy.292, f32[16,16]{1,0:T(8,128)S(1)} %copy-done.20), kind=kOutput, calls=%fused_computation.3 | convolution fusion | flops 151519232 | bytes 8389632 | tf_op jit(solution)/shard_map/hgc,bgc->bhc/dot_general | solution.py:54
  285.6 32.2 %fusion.16 = f32[2048,24,16]{1,2,0:T(8,128)} fusion(f32[24,16,2048]{0,1,2:T(8,128)} %copy.293, f32[16,16,2048]{1,0,2:T(8,128)} %all-gather.6.cloned.1.call-done), kind=kOutput, calls=%fused_computation.61 | convolution fusion | flops 150994944 | bytes 8388608 | tf_op jit(solution)/shard_map/gnc,bgc->bnc/dot_general | solution.py:55
  317.8 10.7 %copy.296 = f32[2048,24,16]{0,2,1:T(8,128)S(1)} copy(f32[2048,24,16]{1,2,0:T(8,128)} %fusion.16) | data formatting | bytes 6291456 | tf_op jit(solution)/shard_map/gnc,bgc->bnc/dot_general | solution.py:55
  378.0 9.0 pad.122
  387.0 9.0 pad.59
  429.4 8.9 pad.85
  444.8 344.9 %while.12 = (s32[]{:T(128)}, f32[16,2048]{1,0:T(8,128)S(1)}, f32[16,2048]{1,0:T(8,128)}, f32[16,2048]{1,0:T(8,128)S(1)}, f32[16,2048]{1,0:T(8,128)S(1)}, /*index=5*/s32[]{:T(128)}) while((s32[]{:T(128)}, f32[16,2048]{1,0:T(8,128)S(1)}, f32[16,2048]{1,0:T(8,128)}, f32[16,2048]{1,0:T(8,128)S(1)}, f32[16,2048]{1,0:T(8,128)S(1)}, ...), condition=%wide.region_2.0_spmd, body=%wide.region_1.0_spmd.sunk | while | flops 65538 | bytes 1573001 | solution.py:67
  501.2 9.4 %collective-permute-done = f32[16,2048]{1,0:T(8,128)S(1)} collective-permute-done((f32[16,2048]{1,0:T(8,128)S(1)}, f32[16,2048]{1,0:T(8,128)S(1)}, u32[]{:S(2)}, u32[]{:S(2)}) %collective-permute-start) | collective-permute-done | bytes 131104 | tf_op jit(solution)/shard_map/while/body/eval_jaxpr/ppermute | solution.py:16
  513.1 9.2 collective-permute-done
  611.9 8.6 collective-permute-done
  623.1 10.0 %collective-permute-done = f32[16,2048]{1,0:T(8,128)S(1)} collective-permute-done((f32[16,2048]{1,0:T(8,128)S(1)}, f32[16,2048]{1,0:T(8,128)S(1)}, u32[]{:S(2)}, u32[]{:S(2)}) %collective-permute-start) | collective-permute-done | bytes 131104 | tf_op jit(solution)/shard_map/while/body/eval_jaxpr/ppermute | solution.py:16
  635.6 9.2 collective-permute-done
  734.4 8.6 collective-permute-done
  745.6 10.0 %collective-permute-done = f32[16,2048]{1,0:T(8,128)S(1)} collective-permute-done((f32[16,2048]{1,0:T(8,128)S(1)}, f32[16,2048]{1,0:T(8,128)S(1)}, u32[]{:S(2)}, u32[]{:S(2)}) %collective-permute-start) | collective-permute-done | bytes 131104 | tf_op jit(solution)/shard_map/while/body/eval_jaxpr/ppermute | solution.py:16
  758.1 9.2 collective-permute-done
  793.0 11.5 %copy.299 = f32[24,16,2048]{0,1,2:T(8,128)} copy(f32[24,16,2048]{2,1,0:T(8,128)S(1)} %multiply_add_fusion.1) | data formatting | bytes 6291456 | tf_op jit(solution)/shard_map/add | solution.py:71
  804.5 27.3 %add_bitcast_fusion = f32[24,16,2048]{0,1,2:T(8,128)} fusion(f32[2048,24,16]{1,2,0:T(8,128)} %fusion, f32[24,16,2048]{0,1,2:T(8,128)} %copy.299, f32[16,16,2048]{1,0,2:T(8,128)} %all-gather.8.cloned.1.call-done), kind=kOutput, calls=%fused_computation.2 | convolution fusion | flops 151781376 | bytes 11534336 | tf_op jit(solution)/shard_map/hnc,bnc->bhc/dot_general | solution.py:72
  831.8 10.8 %copy.300 = f32[24,16,2048]{2,1,0:T(8,128)S(1)} copy(f32[24,16,2048]{0,1,2:T(8,128)} %add_bitcast_fusion) | data formatting | bytes 6291456 | tf_op jit(solution)/shard_map/add | solution.py:73
  846.1 80.7 %psum.7 = f32[384]{0:T(512)S(1)} all-reduce(f32[384]{0:T(512)S(1)} %multiply_reduce_fusion), channel_id=1, replica_groups=mesh['ch'=4,'seq'=32] {'ch'}, use_global_device_ids=true, to_apply=%region_4.0 | all-reduce | flops 384 | bytes 3072 | tf_op jit(solution)/shard_map/psum | solution.py:75
  (261 shorter events, 382.7 us)
Async XLA Ops:
  6.5 279.1 %all-gather.6.cloned.1.call-start = ((), (), s32[]{:S(2)}) async-start(), calls=%async_computation | async-start | bytes 17301504 | tf_op jit(solution)/shard_map/all_gather | solution.py:44
  8.9 795.7 %all-gather.8.cloned.1.call-start = ((), (), s32[]{:S(2)}) async-start(), calls=%async_computation.1 | async-start | bytes 17301504 | tf_op jit(solution)/shard_map/all_gather | solution.py:45
  444.8 10.2 %collective-permute-start = (f32[16,2048]{1,0:T(8,128)S(1)}, f32[16,2048]{1,0:T(8,128)S(1)}, u32[]{:S(2)}, u32[]{:S(2)}) collective-permute-start(f32[16,2048]{1,0:T(8,128)S(1)} %get-tuple-element.106), channel_id=1, source_target_pairs={{0,1},{1,2},{2,3},{3,4},{4,5},{5,6},{6,7},{7,8},{8,9},{9,10},{10,1... | collective-permute-start | bytes 393224 | tf_op jit(solution)/shard_map/while/body/eval_jaxpr/ppermute | solution.py:16
  455.7 10.2 %collective-permute-start = (f32[16,2048]{1,0:T(8,128)S(1)}, f32[16,2048]{1,0:T(8,128)S(1)}, u32[]{:S(2)}, u32[]{:S(2)}) collective-permute-start(f32[16,2048]{1,0:T(8,128)S(1)} %get-tuple-element.106), channel_id=1, source_target_pairs={{0,1},{1,2},{2,3},{3,4},{4,5},{5,6},{6,7},{7,8},{8,9},{9,10},{10,1... | collective-permute-start | bytes 393224 | tf_op jit(solution)/shard_map/while/body/eval_jaxpr/ppermute | solution.py:16
  477.5 10.2 %collective-permute-start = (f32[16,2048]{1,0:T(8,128)S(1)}, f32[16,2048]{1,0:T(8,128)S(1)}, u32[]{:S(2)}, u32[]{:S(2)}) collective-permute-start(f32[16,2048]{1,0:T(8,128)S(1)} %get-tuple-element.106), channel_id=1, source_target_pairs={{0,1},{1,2},{2,3},{3,4},{4,5},{5,6},{6,7},{7,8},{8,9},{9,10},{10,1... | collective-permute-start | bytes 393224 | tf_op jit(solution)/shard_map/while/body/eval_jaxpr/ppermute | solution.py:16
  488.4 10.2 %collective-permute-start = (f32[16,2048]{1,0:T(8,128)S(1)}, f32[16,2048]{1,0:T(8,128)S(1)}, u32[]{:S(2)}, u32[]{:S(2)}) collective-permute-start(f32[16,2048]{1,0:T(8,128)S(1)} %get-tuple-element.106), channel_id=1, source_target_pairs={{0,1},{1,2},{2,3},{3,4},{4,5},{5,6},{6,7},{7,8},{8,9},{9,10},{10,1... | collective-permute-start | bytes 393224 | tf_op jit(solution)/shard_map/while/body/eval_jaxpr/ppermute | solution.py:16
  499.2 11.3 %collective-permute-start = (f32[16,2048]{1,0:T(8,128)S(1)}, f32[16,2048]{1,0:T(8,128)S(1)}, u32[]{:S(2)}, u32[]{:S(2)}) collective-permute-start(f32[16,2048]{1,0:T(8,128)S(1)} %get-tuple-element.106), channel_id=1, source_target_pairs={{0,1},{1,2},{2,3},{3,4},{4,5},{5,6},{6,7},{7,8},{8,9},{9,10},{10,1... | collective-permute-start | bytes 393224 | tf_op jit(solution)/shard_map/while/body/eval_jaxpr/ppermute | solution.py:16
  511.2 11.1 %collective-permute-start = (f32[16,2048]{1,0:T(8,128)S(1)}, f32[16,2048]{1,0:T(8,128)S(1)}, u32[]{:S(2)}, u32[]{:S(2)}) collective-permute-start(f32[16,2048]{1,0:T(8,128)S(1)} %get-tuple-element.106), channel_id=1, source_target_pairs={{0,1},{1,2},{2,3},{3,4},{4,5},{5,6},{6,7},{7,8},{8,9},{9,10},{10,1... | collective-permute-start | bytes 393224 | tf_op jit(solution)/shard_map/while/body/eval_jaxpr/ppermute | solution.py:16
  523.0 10.2 %collective-permute-start = (f32[16,2048]{1,0:T(8,128)S(1)}, f32[16,2048]{1,0:T(8,128)S(1)}, u32[]{:S(2)}, u32[]{:S(2)}) collective-permute-start(f32[16,2048]{1,0:T(8,128)S(1)} %get-tuple-element.106), channel_id=1, source_target_pairs={{0,1},{1,2},{2,3},{3,4},{4,5},{5,6},{6,7},{7,8},{8,9},{9,10},{10,1... | collective-permute-start | bytes 393224 | tf_op jit(solution)/shard_map/while/body/eval_jaxpr/ppermute | solution.py:16
  544.7 10.2 %collective-permute-start = (f32[16,2048]{1,0:T(8,128)S(1)}, f32[16,2048]{1,0:T(8,128)S(1)}, u32[]{:S(2)}, u32[]{:S(2)}) collective-permute-start(f32[16,2048]{1,0:T(8,128)S(1)} %get-tuple-element.106), channel_id=1, source_target_pairs={{0,1},{1,2},{2,3},{3,4},{4,5},{5,6},{6,7},{7,8},{8,9},{9,10},{10,1... | collective-permute-start | bytes 393224 | tf_op jit(solution)/shard_map/while/body/eval_jaxpr/ppermute | solution.py:16
  555.6 10.2 %collective-permute-start = (f32[16,2048]{1,0:T(8,128)S(1)}, f32[16,2048]{1,0:T(8,128)S(1)}, u32[]{:S(2)}, u32[]{:S(2)}) collective-permute-start(f32[16,2048]{1,0:T(8,128)S(1)} %get-tuple-element.106), channel_id=1, source_target_pairs={{0,1},{1,2},{2,3},{3,4},{4,5},{5,6},{6,7},{7,8},{8,9},{9,10},{10,1... | collective-permute-start | bytes 393224 | tf_op jit(solution)/shard_map/while/body/eval_jaxpr/ppermute | solution.py:16
  588.3 10.2 %collective-permute-start = (f32[16,2048]{1,0:T(8,128)S(1)}, f32[16,2048]{1,0:T(8,128)S(1)}, u32[]{:S(2)}, u32[]{:S(2)}) collective-permute-start(f32[16,2048]{1,0:T(8,128)S(1)} %get-tuple-element.106), channel_id=1, source_target_pairs={{0,1},{1,2},{2,3},{3,4},{4,5},{5,6},{6,7},{7,8},{8,9},{9,10},{10,1... | collective-permute-start | bytes 393224 | tf_op jit(solution)/shard_map/while/body/eval_jaxpr/ppermute | solution.py:16
  599.1 10.2 %collective-permute-start = (f32[16,2048]{1,0:T(8,128)S(1)}, f32[16,2048]{1,0:T(8,128)S(1)}, u32[]{:S(2)}, u32[]{:S(2)}) collective-permute-start(f32[16,2048]{1,0:T(8,128)S(1)} %get-tuple-element.106), channel_id=1, source_target_pairs={{0,1},{1,2},{2,3},{3,4},{4,5},{5,6},{6,7},{7,8},{8,9},{9,10},{10,1... | collective-permute-start | bytes 393224 | tf_op jit(solution)/shard_map/while/body/eval_jaxpr/ppermute | solution.py:16
  610.0 10.5 %collective-permute-start = (f32[16,2048]{1,0:T(8,128)S(1)}, f32[16,2048]{1,0:T(8,128)S(1)}, u32[]{:S(2)}, u32[]{:S(2)}) collective-permute-start(f32[16,2048]{1,0:T(8,128)S(1)} %get-tuple-element.106), channel_id=1, source_target_pairs={{0,1},{1,2},{2,3},{3,4},{4,5},{5,6},{6,7},{7,8},{8,9},{9,10},{10,1... | collective-permute-start | bytes 393224 | tf_op jit(solution)/shard_map/while/body/eval_jaxpr/ppermute | solution.py:16
  621.2 11.9 %collective-permute-start = (f32[16,2048]{1,0:T(8,128)S(1)}, f32[16,2048]{1,0:T(8,128)S(1)}, u32[]{:S(2)}, u32[]{:S(2)}) collective-permute-start(f32[16,2048]{1,0:T(8,128)S(1)} %get-tuple-element.106), channel_id=1, source_target_pairs={{0,1},{1,2},{2,3},{3,4},{4,5},{5,6},{6,7},{7,8},{8,9},{9,10},{10,1... | collective-permute-start | bytes 393224 | tf_op jit(solution)/shard_map/while/body/eval_jaxpr/ppermute | solution.py:16
  633.7 11.1 %collective-permute-start = (f32[16,2048]{1,0:T(8,128)S(1)}, f32[16,2048]{1,0:T(8,128)S(1)}, u32[]{:S(2)}, u32[]{:S(2)}) collective-permute-start(f32[16,2048]{1,0:T(8,128)S(1)} %get-tuple-element.106), channel_id=1, source_target_pairs={{0,1},{1,2},{2,3},{3,4},{4,5},{5,6},{6,7},{7,8},{8,9},{9,10},{10,1... | collective-permute-start | bytes 393224 | tf_op jit(solution)/shard_map/while/body/eval_jaxpr/ppermute | solution.py:16
  656.3 10.2 %collective-permute-start = (f32[16,2048]{1,0:T(8,128)S(1)}, f32[16,2048]{1,0:T(8,128)S(1)}, u32[]{:S(2)}, u32[]{:S(2)}) collective-permute-start(f32[16,2048]{1,0:T(8,128)S(1)} %get-tuple-element.106), channel_id=1, source_target_pairs={{0,1},{1,2},{2,3},{3,4},{4,5},{5,6},{6,7},{7,8},{8,9},{9,10},{10,1... | collective-permute-start | bytes 393224 | tf_op jit(solution)/shard_map/while/body/eval_jaxpr/ppermute | solution.py:16
  667.2 10.2 %collective-permute-start = (f32[16,2048]{1,0:T(8,128)S(1)}, f32[16,2048]{1,0:T(8,128)S(1)}, u32[]{:S(2)}, u32[]{:S(2)}) collective-permute-start(f32[16,2048]{1,0:T(8,128)S(1)} %get-tuple-element.106), channel_id=1, source_target_pairs={{0,1},{1,2},{2,3},{3,4},{4,5},{5,6},{6,7},{7,8},{8,9},{9,10},{10,1... | collective-permute-start | bytes 393224 | tf_op jit(solution)/shard_map/while/body/eval_jaxpr/ppermute | solution.py:16
  678.1 10.2 %collective-permute-start = (f32[16,2048]{1,0:T(8,128)S(1)}, f32[16,2048]{1,0:T(8,128)S(1)}, u32[]{:S(2)}, u32[]{:S(2)}) collective-permute-start(f32[16,2048]{1,0:T(8,128)S(1)} %get-tuple-element.106), channel_id=1, source_target_pairs={{0,1},{1,2},{2,3},{3,4},{4,5},{5,6},{6,7},{7,8},{8,9},{9,10},{10,1... | collective-permute-start | bytes 393224 | tf_op jit(solution)/shard_map/while/body/eval_jaxpr/ppermute | solution.py:16
  699.9 10.2 %collective-permute-start = (f32[16,2048]{1,0:T(8,128)S(1)}, f32[16,2048]{1,0:T(8,128)S(1)}, u32[]{:S(2)}, u32[]{:S(2)}) collective-permute-start(f32[16,2048]{1,0:T(8,128)S(1)} %get-tuple-element.106), channel_id=1, source_target_pairs={{0,1},{1,2},{2,3},{3,4},{4,5},{5,6},{6,7},{7,8},{8,9},{9,10},{10,1... | collective-permute-start | bytes 393224 | tf_op jit(solution)/shard_map/while/body/eval_jaxpr/ppermute | solution.py:16
  710.7 10.2 %collective-permute-start = (f32[16,2048]{1,0:T(8,128)S(1)}, f32[16,2048]{1,0:T(8,128)S(1)}, u32[]{:S(2)}, u32[]{:S(2)}) collective-permute-start(f32[16,2048]{1,0:T(8,128)S(1)} %get-tuple-element.106), channel_id=1, source_target_pairs={{0,1},{1,2},{2,3},{3,4},{4,5},{5,6},{6,7},{7,8},{8,9},{9,10},{10,1... | collective-permute-start | bytes 393224 | tf_op jit(solution)/shard_map/while/body/eval_jaxpr/ppermute | solution.py:16
  732.5 10.5 %collective-permute-start = (f32[16,2048]{1,0:T(8,128)S(1)}, f32[16,2048]{1,0:T(8,128)S(1)}, u32[]{:S(2)}, u32[]{:S(2)}) collective-permute-start(f32[16,2048]{1,0:T(8,128)S(1)} %get-tuple-element.106), channel_id=1, source_target_pairs={{0,1},{1,2},{2,3},{3,4},{4,5},{5,6},{6,7},{7,8},{8,9},{9,10},{10,1... | collective-permute-start | bytes 393224 | tf_op jit(solution)/shard_map/while/body/eval_jaxpr/ppermute | solution.py:16
  743.6 11.9 %collective-permute-start = (f32[16,2048]{1,0:T(8,128)S(1)}, f32[16,2048]{1,0:T(8,128)S(1)}, u32[]{:S(2)}, u32[]{:S(2)}) collective-permute-start(f32[16,2048]{1,0:T(8,128)S(1)} %get-tuple-element.106), channel_id=1, source_target_pairs={{0,1},{1,2},{2,3},{3,4},{4,5},{5,6},{6,7},{7,8},{8,9},{9,10},{10,1... | collective-permute-start | bytes 393224 | tf_op jit(solution)/shard_map/while/body/eval_jaxpr/ppermute | solution.py:16
  756.2 11.1 %collective-permute-start = (f32[16,2048]{1,0:T(8,128)S(1)}, f32[16,2048]{1,0:T(8,128)S(1)}, u32[]{:S(2)}, u32[]{:S(2)}) collective-permute-start(f32[16,2048]{1,0:T(8,128)S(1)} %get-tuple-element.106), channel_id=1, source_target_pairs={{0,1},{1,2},{2,3},{3,4},{4,5},{5,6},{6,7},{7,8},{8,9},{9,10},{10,1... | collective-permute-start | bytes 393224 | tf_op jit(solution)/shard_map/while/body/eval_jaxpr/ppermute | solution.py:16
  (64 other events, 540.2 us)
Sparse Core Ops, SparseCore 0:
  10.4 162.4 all-gather.5
  176.0 155.4 all-gather.7
where the time goes:
time: 941 us; the launch traced here: 938 us
  blocking collectives  301 us (32%)
  waiting for transfers between devices  265 us (28%)
  local copies, waits for them, and re-layouts  160 us (17%)
  matrix products  83.2 us (9%)
  starting transfers between devices  59.2 us (6%)
  other arithmetic  55.4 us (6%)
  between operations  13.6 us (1%)
    ppermute x31, waiting for transfers between devices, from_behind(): return lax.ppermute(shard, axis, pairs)  265 us
    psum x1, blocking collectives, body(): token_power = lax.psum(jnp.sum(gated_mix * gated_mix, axis=1), 'ch') / D  80.7 us
    all_gather x1, blocking collectives, body(): lax.all_gather(pieces[0], 'seq', axis=1, tiled=True)  76.7 us
    all_gather x1, blocking collectives, body(): lax.all_gather(pieces[4], 'seq', axis=1, tiled=True)  72.1 us
    all_gather x1, blocking collectives, body(): lax.all_gather(pieces[3], 'seq', axis=1, tiled=True)  71.5 us
    ppermute x31, starting transfers between devices, from_behind(): return lax.ppermute(shard, axis, pairs)  59.2 us
    pad x12, local copies, waits for them, and re-layouts, body(): lax.associative_scan(combine_pairs, (decays, block_ends), axis=0)  53.9 us
    dot_general x1, matrix products, body(): jnp.einsum('gnc,bgc->bnc', end_weights, signal_blocks, precision=highest)  32.2 us
  transfers between devices with their start and end apart: 33, of which 31 were waited for; matrix products, arithmetic and copies ran while one was open for 24% of the time, Pallas kernels for 0%

commit v1 on v0

v1 whole, which is shorter than its diff:
```python
import jax
import jax.numpy as jnp
from jax import lax
from jax.experimental import pallas as pl
from jax.experimental.pallas import tpu as pltpu
from jax.sharding import PartitionSpec as P

D = 8192
ORDER = 16
LANES = 128
SUB = 8
RUN = 16
OWNERS = 4
F32 = jnp.float32
BF16 = jnp.bfloat16

IN_HBM = pl.BlockSpec(memory_space=pltpu.HBM)
IN_VMEM = pl.BlockSpec(memory_space=pltpu.VMEM)
PARAMS = pltpu.CompilerParams(vmem_limit_bytes=24 << 20)


def cost(flops, bytes_accessed):
    return pl.CostEstimate(flops=flops, bytes_accessed=bytes_accessed, transcendentals=0)


def spread(table):
    return [jnp.broadcast_to(table[n : n + 1, :], (SUB, LANES)) for n in range(ORDER)]


def add_up(terms):
    terms = list(terms)
    while len(terms) > 1:
        terms = [a + b for a, b in zip(terms[::2], terms[1::2])] + terms[len(terms) & ~1 :]
    return terms[0]


def quarter_of(by):
    return lax.rem(lax.axis_index("seq") + (by + OWNERS), OWNERS)


def lanes_at(first):
    return pl.ds(pl.multiple_of(first, LANES), LANES)


def later(x, by):
    place = lax.broadcasted_iota(jnp.int32, (SUB, LANES), 0)
    return jnp.where(place >= by, pltpu.roll(x, by, 0), 0.0)


def end_of_tile(signal_ref, rates, sent_ref, ends_ref, here):
    span = signal_ref.shape[0] // SUB
    one = spread(jnp.exp(-rates))
    run = spread(jnp.exp(rates * float(-RUN)))
    total = None
    for g in range(span // RUN):
        acc = None
        for i in range(RUN):
            j = g * RUN + i
            signal = signal_ref[pl.ds(j, SUB, stride=span), :]
            sent_ref[pl.ds(j * SUB, SUB), here] = signal
            acc = [signal] * ORDER if acc is None else [a * o + signal for a, o in zip(acc, one)]
        for n in range(ORDER):
            ends_ref[pl.ds((g * ORDER + n) * SUB, SUB), here] = acc[n]
        total = acc if total is None else [t * r + a for t, r, a in zip(total, run, acc)]
    place = lax.broadcasted_iota(jnp.int32, (SUB, LANES), 0).astype(F32)
    return [
        jnp.sum(a * jnp.exp(rates[n : n + 1, :] * ((place - float(SUB - 1)) * float(span))), axis=0, keepdims=True)
        for n, a in enumerate(total)
    ]


def ends_kernel(key_ref, value_ref, rates_ref, *refs):
    outs, (key_own, value_own, key_held, value_held, signal_ref, rates_here, sems, sem) = refs[:9], refs[9:]
    width = key_own.shape[1]
    per = width // LANES
    pieces = [(quarter_of(k), j) for k in (1, 2, 3) for j in range(per)]

    def copies(i):
        quarter, j = pieces[i]
        there = lanes_at(quarter * width + j * LANES)
        return [
            pltpu.make_async_copy(a.at[:, there], b.at[i], sems.at[s, i])
            for s, (a, b) in enumerate(((key_ref, key_held), (value_ref, value_held)))
        ]

    own = pl.ds(pl.multiple_of(quarter_of(0) * width, width), width)
    own_copies = [
        pltpu.make_async_copy(a.at[:, own], b, sems.at[s, len(pieces)])
        for s, (a, b) in enumerate(((key_ref, key_own), (value_ref, value_own)))
    ]
    rates_copy = pltpu.make_async_copy(rates_ref, rates_here, sem)
    rates_copy.start()
    ahead = 4
    for i in range(ahead):
        for c in copies(i):
            c.start()
    rates_copy.wait()
    for i in range(len(pieces)):
        for c in copies(i):
            c.wait()
        if i + ahead < len(pieces):
            for c in copies(i + ahead):
                c.start()
        elif i + ahead == len(pieces):
            for c in own_copies:
                c.start()
        end_ref, sent_ref, ends_ref = outs[i // per :: 3]
        quarter, j = pieces[i]
        here = pl.ds(j * LANES, LANES)
        signal_ref[...] = key_held[i].astype(F32) * value_held[i].astype(F32)
        ends = end_of_tile(signal_ref, rates_here[:, lanes_at(quarter * width + j * LANES)], sent_ref, ends_ref, here)
        for n in range(ORDER):
            end_ref[n : n + 1, here] = ends[n]
    for c in own_copies:
        c.wait()


def far_ends(key, value, rates):
    tokens, channels = key.shape
    width = channels // OWNERS
    pieces = 3 * (width // LANES)
    end = jax.ShapeDtypeStruct((ORDER, width), F32)
    part = jax.ShapeDtypeStruct((tokens, width), F32)
    own = jax.ShapeDtypeStruct((tokens, width), BF16)
    constrained = [pltpu.with_memory_space_constraint(a, pltpu.HBM) for a in (key, value, rates)]
    return pl.pallas_call(
        ends_kernel,
        in_specs=[IN_HBM, IN_HBM, IN_HBM],
        out_specs=[IN_VMEM] * 11,
        out_shape=[end] * 3 + [part] * 6 + [own] * 2,
        scratch_shapes=[
            pltpu.VMEM((pieces, tokens, LANES), BF16),
            pltpu.VMEM((pieces, tokens, LANES), BF16),
            pltpu.VMEM((tokens, LANES), F32),
            pltpu.VMEM((ORDER, channels), F32),
            pltpu.SemaphoreType.DMA((2, pieces + 1)),
            pltpu.SemaphoreType.DMA(()),
        ],
        compiler_params=PARAMS,
        cost_estimate=cost(32 * tokens * channels, 4 * tokens * channels),
        name="far_ends",
    )(*constrained)


ENTRIES = 9


def position():
    place = lax.axis_index("seq")
    return lax.div(place, 8), lax.rem(lax.div(place, 4), 2), lax.rem(place, 4)


def own_end_kernel(key_ref, value_ref, rates_ref, end_ref, sent_ref, ends_ref, tables_ref, signal_ref):
    tokens, width = key_ref.shape
    x, z, _ = position()
    first = quarter_of(0) * width

    def tile(t, _):
        here = lanes_at(t * LANES)
        rates = rates_ref[:, lanes_at(first + t * LANES)]
        signal_ref[...] = key_ref[:, here].astype(F32) * value_ref[:, here].astype(F32)
        ends = end_of_tile(signal_ref, rates, sent_ref, ends_ref, here)
        for n in range(ORDER):
            end_ref[n : n + 1, here] = ends[n]
        rates = rates * float(-tokens)
        tables_ref[0, :, here] = jnp.zeros((ORDER, LANES), F32)
        for m in range(1, 6):
            tables_ref[m, :, here] = jnp.exp(rates * float(m - 1))
        for k in (1, 2, 3):
            spans = (4 * z + jnp.maximum(8 * (k - 1), 0)).astype(F32)
            tables_ref[5 + k, :, here] = jnp.exp(rates * spans) * (x >= k).astype(F32)
        return 0

    lax.fori_loop(0, width // LANES, tile, 0)


def own_end(key, value, rates):
    tokens, width = key.shape
    part = jax.ShapeDtypeStruct((tokens, width), F32)
    return pl.pallas_call(
        own_end_kernel,
        in_specs=[IN_VMEM] * 3,
        out_specs=[IN_VMEM] * 4,
        out_shape=[
            jax.ShapeDtypeStruct((ORDER, width), F32),
            part,
            part,
            jax.ShapeDtypeStruct((ENTRIES, ORDER, width), F32),
        ],
        scratch_shapes=[pltpu.VMEM((tokens, LANES), F32)],
        compiler_params=PARAMS,
        cost_estimate=cost(32 * tokens * width, 12 * tokens * width),
        name="own_end",
    )(key, value, rates)


def sender(y, by):
    return lax.rem(y + (OWNERS - by), OWNERS)


def row_kernel(e0, e1, e2, e3, tables_ref, row_ref):
    _, _, y = position()
    row_ref[...] = add_up([tables_ref[4 - sender(y, k)] * e[...] for k, e in enumerate((e0, e1, e2, e3))])


def plane_kernel(row_ref, other_ref, tables_ref, plane_ref):
    _, z, _ = position()
    plane_ref[...] = tables_ref[5 - 4 * z] * row_ref[...] + tables_ref[1 + 4 * z] * other_ref[...]


def states_kernel(e0, e1, e2, e3, other_ref, p1, p2, p3, tables_ref, *states):
    _, z, y = position()
    head = other_ref[...] * z.astype(F32) + add_up(
        [tables_ref[5 + k] * p[...] for k, p in ((1, p1), (2, p2), (3, p3))]
    )
    for j, state_ref in enumerate(states):
        target = lax.rem(y + j, OWNERS)
        before = [
            tables_ref[jnp.maximum(target - sender(y, k), 0)] * e[...] for k, e in enumerate((e0, e1, e2, e3))
        ]
        state_ref[...] = add_up(before) + tables_ref[1 + target] * head


def small(kernel, count, *args):
    out = jax.ShapeDtypeStruct(args[0].shape, F32)
    return pl.pallas_call(
        kernel,
        in_specs=[IN_VMEM] * len(args),
        out_specs=[IN_VMEM] * count,
        out_shape=[out] * count,
        compiler_params=PARAMS,
        cost_estimate=cost(10 * out.size, 40 * out.size),
        name=kernel.__name__,
    )(*args)


def local_kernel(by, sent_ref, ends_ref, gate_ref, rates_ref, residues_ref, skip_ref,
                 mixed_ref, gate_out, start_ref, reach_ref, enter_ref, gate_held, gate_f32, sems):
    tokens, width = mixed_ref.shape
    span = tokens // SUB
    place = lax.broadcasted_iota(jnp.int32, (SUB, LANES), 0).astype(F32)

    def copy(t):
        there = lanes_at(quarter_of(by) * width + t * LANES)
        return pltpu.make_async_copy(gate_ref.at[:, there], gate_held.at[t], sems.at[t])

    for t in range(width // LANES):
        copy(t).start()

    def tile(t, _):
        lanes = lanes_at(quarter_of(by) * width + t * LANES)
        here = lanes_at(t * LANES)
        rates = rates_ref[:, lanes]
        residues = residues_ref[:, lanes]
        decay = jnp.exp(-rates)

        taps, term = [], residues
        for k in range(RUN):
            tap = term[:SUB] + term[SUB:]
            for shift in (4, 2, 1):
                tap = tap + pltpu.roll(tap, shift, 0)
            taps.append(tap)
            term = term * decay
        taps[0] = taps[0] + skip_ref[:, lanes]

        run = spread(jnp.exp(rates * float(-RUN)))

        def end(g, n):
            return ends_ref[pl.ds((g * ORDER + n) * SUB, SUB), here]

        state = [(end(0, n) * run[n] + end(1, n)) * run[n] + end(2, n) for n in range(ORDER)]
        for step in (1, 2, 4):
            across = spread(jnp.exp(rates * float(-span * step)))
            state = [s + later(s, step) * a for s, a in zip(state, across)]
        first = spread(residues * decay)
        for n in range(ORDER):
            rows = pl.ds(n * SUB, SUB)
            start_ref[rows, here] = first[n] * later(state[n], 1)
            reach_ref[rows, here] = first[n] * jnp.exp(rates[n : n + 1, :] * (place * float(-span)))
            for g in (0, 1):
                enter_ref[pl.ds((g * ORDER + n) * SUB, SUB), here] = first[n] * end(g, n)

        copy(t).wait()
        gate_f32[...] = gate_held[t].astype(F32)

        def group(g, _):
            signal = []
            for i in range(RUN):
                rows = pl.ds(pl.multiple_of((g * RUN + i) * SUB, SUB), SUB)
                signal.append(sent_ref[rows, here])
                gate = gate_f32[pl.ds(g * RUN + i, SUB, stride=span), :]
                conv = add_up([taps[i - m] * signal[m] for m in range(i + 1)])
                mixed_ref[rows, here] = gate * conv
                gate_out[rows, here] = gate
            return 0

        lax.fori_loop(0, span // RUN, group, 0)
        return 0

    lax.fori_loop(0, width // LANES, tile, 0)


def local_part(by, sent, ends, gate, rates, residues, skip):
    tokens, width = sent.shape
    token_part = jax.ShapeDtypeStruct((tokens, width), F32)
    mode_part = jax.ShapeDtypeStruct((ORDER * SUB, width), F32)
    enter_part = jax.ShapeDtypeStruct((2 * ORDER * SUB, width), F32)
    gate = pltpu.with_memory_space_constraint(gate, pltpu.HBM)
    return pl.pallas_call(
        lambda *refs: local_kernel(by, *refs),
        in_specs=[IN_VMEM, IN_VMEM, IN_HBM, IN_VMEM, IN_VMEM, IN_VMEM],
        out_specs=[IN_VMEM] * 5,
        out_shape=[token_part, token_part, mode_part, mode_part, enter_part],
        scratch_shapes=[
            pltpu.VMEM((width // LANES, tokens, LANES), BF16),
            pltpu.VMEM((tokens, LANES), F32),
            pltpu.SemaphoreType.DMA((width // LANES,)),
        ],
        compiler_params=PARAMS,
        cost_estimate=cost(30 * tokens * width, 14 * tokens * width),
        name="local_part",
    )(sent, ends, gate, rates, residues, skip)


def mix_kernel(by, last, mixed_ref, gate_ref, start_ref, reach_ref, enter_ref, state_ref, rates_ref, *rest):
    tokens, width = mixed_ref.shape
    span = tokens // SUB
    gated_ref, sums_ref = rest[-2], rest[-1]
    if by == 0:
        sums_ref[...] = jnp.zeros_like(sums_ref)
    else:
        sums_ref[...] = rest[0][...]
    if last:
        power_ref = rest[1]

    def tile(t, _):
        here = lanes_at(t * LANES)
        step = spread(jnp.exp(-rates_ref[:, lanes_at(quarter_of(-by) * width + t * LANES)]))
        state = state_ref[:, here]
        terms = []
        for n in range(ORDER):
            rows = pl.ds(n * SUB, SUB)
            terms.append(start_ref[rows, here] + reach_ref[rows, here] * state[n : n + 1, :])
        for j in range(span):
            if j > 0:
                terms = [a * b for a, b in zip(terms, step)]
            if j > 0 and j % RUN == 0:
                g = j // RUN - 1
                terms = [a + enter_ref[pl.ds((g * ORDER + n) * SUB, SUB), here] for n, a in enumerate(terms)]
            rows = pl.ds(j * SUB, SUB)
            gated = mixed_ref[rows, here] + gate_ref[rows, here] * add_up(terms)
            gated_ref[t, pl.ds(j, SUB, stride=span), :] = gated
            sums_ref[rows, :] += gated * gated
        return 0

    lax.fori_loop(0, width // LANES, tile, 0)
    if last:
        power_ref[...] = lax.dot_general(
            jnp.ones((SUB, LANES), F32),
            sums_ref[...],
            (((1,), (1,)), ((), ())),
            precision=lax.Precision.HIGHEST,
            preferred_element_type=F32,
        )[0:1, :]


def mix(by, last, part, state, rates, sums):
    tokens, width = part[0].shape
    out_sums = jax.ShapeDtypeStruct((tokens, LANES), F32)
    gated = jax.ShapeDtypeStruct((width // LANES, tokens, LANES), F32)
    args = [*part, state, rates] + ([] if sums is None else [sums])
    if last:
        outs, scratch = [jax.ShapeDtypeStruct((1, tokens), F32), gated], [pltpu.VMEM((tokens, LANES), F32)]
    else:
        outs, scratch = [gated, out_sums], []
    return pl.pallas_call(
        lambda *refs: mix_kernel(by, last, *refs),
        in_specs=[IN_VMEM] * len(args),
        out_specs=[IN_VMEM] * 2,
        out_shape=outs,
        scratch_shapes=scratch,
        compiler_params=PARAMS,
        cost_estimate=cost(40 * tokens * width, 12 * tokens * width),
        name="mix",
    )(*args)


def norm_kernel(g0, g1, g2, g3, gain_ref, p0_ref, p1_ref, p2_ref, p3_ref, out_ref, runs_ref, scale_ref, held, sems):
    tiles, tokens, _ = g0.shape
    width = tiles * LANES
    span = tokens // SUB
    total = (p0_ref[...] + p1_ref[...]) + (p2_ref[...] + p3_ref[...])
    first = (lax.broadcasted_iota(jnp.int32, (SUB, LANES), 0) == 0).astype(F32)
    power = lax.dot_general(
        jnp.broadcast_to(total, (SUB, tokens)),
        first,
        (((0,), (0,)), ((), ())),
        precision=lax.Precision.HIGHEST,
        preferred_element_type=F32,
    )
    runs_ref[...] = lax.rsqrt(power * (1.0 / D) + 1e-6)
    for i in range(span):
        scale_ref[pl.ds(i, SUB, stride=span), :] = runs_ref[pl.ds(i * SUB, SUB), :]

    copies = []
    for by, gated_ref in enumerate((g0, g1, g2, g3)):
        first = quarter_of(-by) * width

        def tile(t, _):
            here = lanes_at(t * LANES)
            gain = gain_ref[:, lanes_at(first + t * LANES)]
            held[by, :, here] = (gated_ref[t] * scale_ref[...] * gain).astype(BF16)
            return 0

        lax.fori_loop(0, width // LANES, tile, 0)
        copy = pltpu.make_async_copy(
            held.at[by], out_ref.at[:, pl.ds(pl.multiple_of(first, width), width)], sems.at[by]
        )
        copy.start()
        copies.append(copy)
    for copy in copies:
        copy.wait()


def norm(gated, gain, powers):
    tiles, tokens, _ = gated[0].shape
    width = tiles * LANES
    channels = width * OWNERS
    return pl.pallas_call(
        norm_kernel,
        in_specs=[IN_VMEM] * 9,
        out_specs=IN_HBM,
        out_shape=jax.ShapeDtypeStruct((tokens, channels), BF16),
        scratch_shapes=[
            pltpu.VMEM((tokens, LANES), F32),
            pltpu.VMEM((tokens, LANES), F32),
            pltpu.VMEM((OWNERS, tokens, width), BF16),
            pltpu.SemaphoreType.DMA((OWNERS,)),
        ],
        compiler_params=PARAMS,
        cost_estimate=cost(3 * tokens * channels, 6 * tokens * channels),
        name="norm",
    )(*gated, gain, *powers)


def over_y(x, by):
    return lax.ppermute(x, "seq", [(i, i // 4 * 4 + (i + by) % 4) for i in range(32)])


def over_z(x):
    return lax.ppermute(x, "seq", [(i, i ^ 4) for i in range(32)])


def over_x(x, by):
    return lax.ppermute(x, "seq", [(i, (i + 8 * by) % 32) for i in range(32)])


def over_ch(x, by):
    return lax.ppermute(x, "ch", [(i, (i + by) % 4) for i in range(4)])


def body(gate, key, value, rates, residues, skip_gain, norm_gain):
    skip = skip_gain[None, :]
    tie = lax.optimization_barrier
    parts = [None] * OWNERS

    def local(by, rates):
        parts[by] = local_part(-by, sent[-by], inner[-by], gate, rates, residues, skip)

    outs = far_ends(key, value, rates)
    ends, sent, inner = [None, *outs[0:3]], [None, *outs[3:6]], [None, *outs[6:9]]
    got = [over_y(ends[k], k) for k in (1, 2, 3)]
    own, sent[0], inner[0], tables = own_end(*outs[9:11], rates)
    local(1, rates)
    own, parts[1] = tie((own, parts[1]))
    ends = [own] + got
    (row,) = small(row_kernel, 1, *ends, tables)

    row, rates1 = tie((row, rates))
    other = over_z(row)
    local(2, rates1)
    local(3, rates1)
    other, parts[2], parts[3] = tie((other, parts[2], parts[3]))
    (plane,) = small(plane_kernel, 1, row, other, tables)

    plane, rates2 = tie((plane, rates))
    got = [over_x(plane, k) for k in (1, 2, 3)]
    local(0, rates2)
    got[0], parts[0] = tie((got[0], parts[0]))
    states = list(small(states_kernel, OWNERS, *ends, other, *got, tables))

    states = [states[0]] + [over_y(s, k) for k, s in zip((1, 2, 3), states[1:])]
    gated, sums = [], None
    for by in range(OWNERS):
        first, second = mix(by, by == OWNERS - 1, parts[by], states[by], rates, sums)
        if by < OWNERS - 1:
            gated.append(first)
            sums = second
        else:
            gated.append(second)
            power = first
    powers = [power] + [over_ch(power, k) for k in (1, 2, 3)]
    return norm(gated, norm_gain[None, :], powers)


def solution(mesh):
    placed = (
        P("seq", "ch"),
        P("seq", "ch"),
        P("seq", "ch"),
        P(None, "ch"),
        P(None, "ch"),
        P("ch"),
        P("ch"),
    )
    return jax.shard_map(
        body, mesh=mesh, in_specs=placed, out_specs=P("seq", "ch"), check_vma=False
    )
```

time: 941 us -> 47.3 us (0.05)
  the two profiles are of different devices: /device:TPU:3 before, /device:TPU:1 now
where the time goes in v1:
time: 47.3 us; the launch traced here: 47 us
  starting transfers between devices  23 us (49%)
  Pallas kernels  20.8 us (44%)
  waiting for transfers between devices  3.03 us (6%)
    ppermute x6, starting transfers between devices, over_y(): lax.ppermute(x, 'seq', [(i, i // 4 * 4 + (i + by) % 4) for i in range(32)])  8.83 us
    pallas_call x4, Pallas kernels, local_part(): pl.pallas_call(lambda *refs: local_kernel(by, *refs), in_specs=[IN_VMEM,...  7.79 us
    ppermute x3, starting transfers between devices, over_ch(): return lax.ppermute(x, 'ch', [(i, (i + by) % 4) for i in range(4)])  5.63 us
    pallas_call x1, Pallas kernels, far_ends(): pl.pallas_call(ends_kernel, in_specs=[IN_HBM, IN_HBM, IN_HBM], out_specs=...  5.18 us
    ppermute x3, starting transfers between devices, over_x(): return lax.ppermute(x, 'seq', [(i, (i + 8 * by) % 32) for i in range(32)])  4.88 us
    pallas_call x4, Pallas kernels, mix(): pl.pallas_call(lambda *refs: mix_kernel(by, last, *refs), in_specs=[IN_VM...  4.71 us
    ppermute x1, starting transfers between devices, over_z(): return lax.ppermute(x, 'seq', [(i, i ^ 4) for i in range(32)])  3.68 us
    ppermute x3, waiting for transfers between devices, over_ch(): return lax.ppermute(x, 'ch', [(i, (i + by) % 4) for i in range(4)])  3 us
  transfers between devices with their start and end apart: 13, of which 2 were waited for; matrix products, arithmetic and copies ran while one was open for 0% of the time, Pallas kernels for 26%

profile of v1, /device:TPU:1, one launch (start us, length us, event | category | flops | bytes accessed | tf_op | source)
XLA Modules:
  0.0 47.0 jit_solution(8331922863515405101)
XLA Ops:
  0.0 5.2 %far_ends.1 = (f32[16,512]{1,0:T(8,128)S(1)}, f32[16,512]{1,0:T(8,128)S(1)}, f32[16,512]{1,0:T(8,128)S(1)}, f32[384,512]{1,0:T(8,128)S(1)}, f32[384,512]{1,0:T(8...) custom-call(bf16[384,2048]{1,0:T(8,128)(2,1)} %key_ref.1, ...), custom_call_target="tpu_custom_call" | custom-call | flops 25165824 | bytes 3145728 | tf_op jit(solution)/shard_map/far_ends/pallas_call | solution.py:126
  5.2 2.2 %collective-permute-start = (f32[16,512]{1,0:T(8,128)S(1)}, f32[16,512]{1,0:T(8,128)S(1)}, u32[]{:S(2)}, u32[]{:S(2)}) collective-permute-start(f32[16,512]{1,0:T(8,128)S(1)} %get-tuple-element.90), channel_id=1, source_target_pairs={{0,1},{1,2},{2,3},{3,0},{4,5},{5,6},{6,7},{7,4},{8,9},{9,10},{10,1... | collective-permute-start | bytes 98312 | tf_op jit(solution)/shard_map/ppermute | solution.py:447
  7.4 2.6 %collective-permute-start.1 = (f32[16,512]{1,0:T(8,128)S(1)}, f32[16,512]{1,0:T(8,128)S(1)}, u32[]{:S(2)}, u32[]{:S(2)}) collective-permute-start(f32[16,512]{1,0:T(8,128)S(1)} %get-tuple-element.91), channel_id=1, source_target_pairs={{0,2},{1,3},{2,0},{3,1},{4,6},{5,7},{6,4},{7,5},{8,10},{9,11},{10,... | collective-permute-start | bytes 98312 | tf_op jit(solution)/shard_map/ppermute | solution.py:447
  10.0 1.1 %collective-permute-start.2 = (f32[16,512]{1,0:T(8,128)S(1)}, f32[16,512]{1,0:T(8,128)S(1)}, u32[]{:S(2)}, u32[]{:S(2)}) collective-permute-start(f32[16,512]{1,0:T(8,128)S(1)} %get-tuple-element.92), channel_id=1, source_target_pairs={{0,3},{1,0},{2,1},{3,2},{4,7},{5,4},{6,5},{7,6},{8,11},{9,8},{10,9... | collective-permute-start | bytes 98312 | tf_op jit(solution)/shard_map/ppermute | solution.py:447
  11.1 1.9 %local_part.4 = (f32[384,512]{1,0:T(8,128)S(1)}, f32[384,512]{1,0:T(8,128)S(1)}, f32[128,512]{1,0:T(8,128)S(1)}, f32[128,512]{1,0:T(8,128)S(1)}, f32[256,512]{1,0:T(8,128)S(1)}) custom-call(f32[384,512]{1,0:T(8,128)S(1)} %get-tuple-element.82.refs_0_, f32[384,512]{1,0:T(8,128)S(1)} %get-tuple-element.83.refs_1_, bf16[384,2048]{1,0:T(8,128)(2,1)} %refs_2_.7, ...), custom_call_target="tpu_custom_call" | custom-call | flops 5898240 | bytes 2752512 | tf_op jit(solution)/shard_map/local_part/pallas_call | solution.py:309
  13.1 1.3 %own_end.1 = (f32[16,512]{1,0:T(8,128)S(1)}, f32[384,512]{1,0:T(8,128)S(1)}, f32[384,512]{1,0:T(8,128)S(1)}, f32[9,16,512]{2,1,0:T(8,128)S(1)}) custom-call(bf16[384,512]{1,0:T(8,128)(2,1)S(1)} %get-tuple-element.79.key_ref, bf16[384,512]{1,0:T(8,128)(2,1)S(1)} %get-tuple-element.80.value_ref, f32[16,2048]{1,0:T(8,128)S(1)} %copy-done), custom_call_target="tpu_custom_call" | custom-call | flops 6291456 | bytes 2359296 | tf_op jit(solution)/shard_map/own_end/pallas_call | solution.py:180
  14.4 3.7 %collective-permute-start.3 = (f32[16,512]{1,0:T(8,128)S(1)}, f32[16,512]{1,0:T(8,128)S(1)}, u32[]{:S(2)}, u32[]{:S(2)}) collective-permute-start(f32[16,512]{1,0:T(8,128)S(1)} %row_kernel.1.row_ref), channel_id=1, source_target_pairs={{0,4},{1,5},{2,6},{3,7},{4,0},{5,1},{6,2},{7,3},{8,12},{9,13},{10,... | collective-permute-start | bytes 98312 | tf_op jit(solution)/shard_map/ppermute | solution.py:451
  18.1 1.9 %local_part.6 = (f32[384,512]{1,0:T(8,128)S(1)}, f32[384,512]{1,0:T(8,128)S(1)}, f32[128,512]{1,0:T(8,128)S(1)}, f32[128,512]{1,0:T(8,128)S(1)}, f32[256,512]{1,0:T(8,128)S(1)}) custom-call(f32[384,512]{1,0:T(8,128)S(1)} %get-tuple-element.103.refs_0_, f32[384,512]{1,0:T(8,128)S(1)} %get-tuple-element.104.refs_1_, bf16[384,2048]{1,0:T(8,128)(2,1)} %refs_2_.7, ...), custom_call_target="tpu_custom_call" | custom-call | flops 5898240 | bytes 2752512 | tf_op jit(solution)/shard_map/local_part/pallas_call | solution.py:309
  20.0 2.0 %local_part.5 = (f32[384,512]{1,0:T(8,128)S(1)}, f32[384,512]{1,0:T(8,128)S(1)}, f32[128,512]{1,0:T(8,128)S(1)}, f32[128,512]{1,0:T(8,128)S(1)}, f32[256,512]{1,0:T(8,128)S(1)}) custom-call(f32[384,512]{1,0:T(8,128)S(1)} %get-tuple-element.95.refs_0_, f32[384,512]{1,0:T(8,128)S(1)} %get-tuple-element.96.refs_1_, bf16[384,2048]{1,0:T(8,128)(2,1)} %refs_2_.7, ...), custom_call_target="tpu_custom_call" | custom-call | flops 5898240 | bytes 2752512 | tf_op jit(solution)/shard_map/local_part/pallas_call | solution.py:309
  22.0 1.3 %collective-permute-start.4 = (f32[16,512]{1,0:T(8,128)S(1)}, f32[16,512]{1,0:T(8,128)S(1)}, u32[]{:S(2)}, u32[]{:S(2)}) collective-permute-start(f32[16,512]{1,0:T(8,128)S(1)} %plane_kernel.1), channel_id=1, source_target_pairs={{0,8},{1,9},{2,10},{3,11},{4,12},{5,13},{6,14},{7,15},{8,16},{9,17... | collective-permute-start | bytes 98312 | tf_op jit(solution)/shard_map/ppermute | solution.py:455
  23.3 2.5 %collective-permute-start.5 = (f32[16,512]{1,0:T(8,128)S(1)}, f32[16,512]{1,0:T(8,128)S(1)}, u32[]{:S(2)}, u32[]{:S(2)}) collective-permute-start(f32[16,512]{1,0:T(8,128)S(1)} %plane_kernel.1), channel_id=1, source_target_pairs={{0,16},{1,17},{2,18},{3,19},{4,20},{5,21},{6,22},{7,23},{8,24},{9,... | collective-permute-start | bytes 98312 | tf_op jit(solution)/shard_map/ppermute | solution.py:455
  25.8 1.2 %collective-permute-start.6 = (f32[16,512]{1,0:T(8,128)S(1)}, f32[16,512]{1,0:T(8,128)S(1)}, u32[]{:S(2)}, u32[]{:S(2)}) collective-permute-start(f32[16,512]{1,0:T(8,128)S(1)} %plane_kernel.1), channel_id=1, source_target_pairs={{0,24},{1,25},{2,26},{3,27},{4,28},{5,29},{6,30},{7,31},{8,0},{9,1... | collective-permute-start | bytes 98312 | tf_op jit(solution)/shard_map/ppermute | solution.py:455
  26.9 1.9 %local_part.7 = (f32[384,512]{1,0:T(8,128)S(1)}, f32[384,512]{1,0:T(8,128)S(1)}, f32[128,512]{1,0:T(8,128)S(1)}, f32[128,512]{1,0:T(8,128)S(1)}, f32[256,512]{1,0:T(8,128)S(1)}) custom-call(f32[384,512]{1,0:T(8,128)S(1)} %get-tuple-element.112.refs_0_, f32[384,512]{1,0:T(8,128)S(1)} %get-tuple-element.113.refs_1_, bf16[384,2048]{1,0:T(8,128)(2,1)} %refs_2_.7, ...), custom_call_target="tpu_custom_call" | custom-call | flops 5898240 | bytes 2752512 | tf_op jit(solution)/shard_map/local_part/pallas_call | solution.py:309
  29.5 1.5 %collective-permute-start.8 = (f32[16,512]{1,0:T(8,128)S(1)}, f32[16,512]{1,0:T(8,128)S(1)}, u32[]{:S(2)}, u32[]{:S(2)}) collective-permute-start(f32[16,512]{1,0:T(8,128)S(1)} %get-tuple-element.141), channel_id=1, source_target_pairs={{0,2},{1,3},{2,0},{3,1},{4,6},{5,7},{6,4},{7,5},{8,10},{9,11},{10,... | collective-permute-start | bytes 98312 | tf_op jit(solution)/shard_map/ppermute | solution.py:447
  30.9 1.0 %collective-permute-start.9 = (f32[16,512]{1,0:T(8,128)S(1)}, f32[16,512]{1,0:T(8,128)S(1)}, u32[]{:S(2)}, u32[]{:S(2)}) collective-permute-start(f32[16,512]{1,0:T(8,128)S(1)} %get-tuple-element.149), channel_id=1, source_target_pairs={{0,3},{1,0},{2,1},{3,2},{4,7},{5,4},{6,5},{7,6},{8,11},{9,8},{10,9... | collective-permute-start | bytes 98312 | tf_op jit(solution)/shard_map/ppermute | solution.py:447
  31.9 1.1 %mix.4 = (f32[4,384,128]{2,1,0:T(8,128)S(1)}, f32[384,128]{1,0:T(8,128)S(1)}) custom-call(f32[384,512]{1,0:T(8,128)S(1)} %get-tuple-element.120.refs_0_, f32[384,512]{1,0:T(8,128)S(1)} %get-tuple-element.121.refs_1_, f32[128,512]{1,0:T(8,128)S(1)} %get-tuple-element.122.refs_2_, f32[128,512]{1,0:T(8,128)S(1)} %get-tuple-element.123.refs_3_, ...), custom_call_target="tpu_custom_call" | custom-call | flops 7864320 | bytes 2359296 | tf_op jit(solution)/shard_map/mix/pallas_call | solution.py:376
  33.1 1.1 %mix.5 = (f32[4,384,128]{2,1,0:T(8,128)S(1)}, f32[384,128]{1,0:T(8,128)S(1)}) custom-call(f32[384,512]{1,0:T(8,128)S(1)} %get-tuple-element.128.refs_0_, f32[384,512]{1,0:T(8,128)S(1)} %get-tuple-element.129.refs_1_, f32[128,512]{1,0:T(8,128)S(1)} %get-tuple-element.130.refs_2_, f32[128,512]{1,0:T(8,128)S(1)} %get-tuple-element.131.refs_3_, ...), custom_call_target="tpu_custom_call" | custom-call | flops 7864320 | bytes 2359296 | tf_op jit(solution)/shard_map/mix/pallas_call | solution.py:376
  34.2 1.1 %mix.6 = (f32[4,384,128]{2,1,0:T(8,128)S(1)}, f32[384,128]{1,0:T(8,128)S(1)}) custom-call(f32[384,512]{1,0:T(8,128)S(1)} %get-tuple-element.136.refs_0_, f32[384,512]{1,0:T(8,128)S(1)} %get-tuple-element.137.refs_1_, f32[128,512]{1,0:T(8,128)S(1)} %get-tuple-element.138.refs_2_, f32[128,512]{1,0:T(8,128)S(1)} %get-tuple-element.139.refs_3_, ...), custom_call_target="tpu_custom_call" | custom-call | flops 7864320 | bytes 2359296 | tf_op jit(solution)/shard_map/mix/pallas_call | solution.py:376
  35.3 1.4 %mix.7 = (f32[1,384]{1,0:T(1,128)S(1)}, f32[4,384,128]{2,1,0:T(8,128)S(1)}) custom-call(f32[384,512]{1,0:T(8,128)S(1)} %get-tuple-element.144.refs_0_, f32[384,512]{1,0:T(8,128)S(1)} %get-tuple-element.145.refs_1_, f32[128,512]{1,0:T(8,128)S(1)} %get-tuple-element.146.refs_2_, f32[128,512]{1,0:T(8,128)S(1)} %get-tuple-element.147.refs_3_, ...), custom_call_target="tpu_custom_call" | custom-call | flops 7864320 | bytes 2359296 | tf_op jit(solution)/shard_map/mix/pallas_call | solution.py:376
  36.7 4.9 %collective-permute-start.10 = (f32[1,384]{1,0:T(1,128)S(1)}, f32[1,384]{1,0:T(1,128)S(1)}, u32[]{:S(2)}, u32[]{:S(2)}) collective-permute-start(f32[1,384]{1,0:T(1,128)S(1)} %get-tuple-element.152.p0_ref), channel_id=1, source_target_pairs={{0,32},{32,64},{64,96},{96,0},{1,33},{33,65},{65,97},{97,1},{2,34}... | collective-permute-start | bytes 4616 | tf_op jit(solution)/shard_map/ppermute | solution.py:459
  41.6 0.7 %collective-permute-start.11 = (f32[1,384]{1,0:T(1,128)S(1)}, f32[1,384]{1,0:T(1,128)S(1)}, u32[]{:S(2)}, u32[]{:S(2)}) collective-permute-start(f32[1,384]{1,0:T(1,128)S(1)} %get-tuple-element.152.p0_ref), channel_id=1, source_target_pairs={{0,64},{32,96},{64,0},{96,32},{1,65},{33,97},{65,1},{97,33},{2,66}... | collective-permute-start | bytes 4616 | tf_op jit(solution)/shard_map/ppermute | solution.py:459
  42.3 1.9 %collective-permute-done.11.p2_ref = f32[1,384]{1,0:T(1,128)S(1)} collective-permute-done((f32[1,384]{1,0:T(1,128)S(1)}, f32[1,384]{1,0:T(1,128)S(1)}, u32[]{:S(2)}, u32[]{:S(2)}) %collective-permute-start.11) | collective-permute-done | bytes 1568 | tf_op jit(solution)/shard_map/ppermute | solution.py:459
  44.2 1.1 %collective-permute-done.12.p3_ref = f32[1,384]{1,0:T(1,128)S(1)} collective-permute-done((f32[1,384]{1,0:T(1,128)S(1)}, f32[1,384]{1,0:T(1,128)S(1)}, u32[]{:S(2)}, u32[]{:S(2)}) %collective-permute-start.12) | collective-permute-done | bytes 1568 | tf_op jit(solution)/shard_map/ppermute | solution.py:459
  45.3 1.7 %norm.1 = bf16[384,2048]{1,0:T(8,128)(2,1)} custom-call(f32[4,384,128]{2,1,0:T(8,128)S(1)} %get-tuple-element.127.g0, f32[4,384,128]{2,1,0:T(8,128)S(1)} %get-tuple-element.135.g1, f32[4,384,128]{2,1,0:T(8,128)S(1)} %get-tuple-element.143.g2, f32[4,384,128]{2,1,0:T(8,128)S(1)} %get-tuple-element.151.g3, f32[1,2048]{1,0:T(1,128)S(1)} %bitcast.6, ...), custom_call_target="tpu_custom_call" | custom-call | flops 2359296 | bytes 4718592 | tf_op jit(solution)/shard_map/norm/pallas_call | solution.py:429
  (24 shorter events, 0.7 us)
Async XLA Ops:
  0.0 11.1 %copy-start = (f32[16,2048]{1,0:T(8,128)S(1)}, f32[16,2048]{1,0:T(8,128)}, u32[]{:S(2)}) copy-start(f32[16,2048]{1,0:T(8,128)} %refs_6_.7) | copy-start | bytes 393220
  0.0 11.1 %copy-start.2 = (f32[2048]{0:T(1024)S(1)}, f32[2048]{0:T(1024)}, u32[]{:S(2)}) copy-start(f32[2048]{0:T(1024)} %param.12) | copy-start | bytes 24580
  0.0 11.1 %copy-start.1 = (f32[16,2048]{1,0:T(8,128)S(1)}, f32[16,2048]{1,0:T(8,128)}, u32[]{:S(2)}) copy-start(f32[16,2048]{1,0:T(8,128)} %refs_4_.7) | copy-start | bytes 393220
  5.2 9.1 %collective-permute-start = (f32[16,512]{1,0:T(8,128)S(1)}, f32[16,512]{1,0:T(8,128)S(1)}, u32[]{:S(2)}, u32[]{:S(2)}) collective-permute-start(f32[16,512]{1,0:T(8,128)S(1)} %get-tuple-element.90), channel_id=1, source_target_pairs={{0,1},{1,2},{2,3},{3,0},{4,5},{5,6},{6,7},{7,4},{8,9},{9,10},{10,1... | collective-permute-start | bytes 98312 | tf_op jit(solution)/shard_map/ppermute | solution.py:447
  7.4 7.0 %collective-permute-start.1 = (f32[16,512]{1,0:T(8,128)S(1)}, f32[16,512]{1,0:T(8,128)S(1)}, u32[]{:S(2)}, u32[]{:S(2)}) collective-permute-start(f32[16,512]{1,0:T(8,128)S(1)} %get-tuple-element.91), channel_id=1, source_target_pairs={{0,2},{1,3},{2,0},{3,1},{4,6},{5,7},{6,4},{7,5},{8,10},{9,11},{10,... | collective-permute-start | bytes 98312 | tf_op jit(solution)/shard_map/ppermute | solution.py:447
  10.0 4.3 %collective-permute-start.2 = (f32[16,512]{1,0:T(8,128)S(1)}, f32[16,512]{1,0:T(8,128)S(1)}, u32[]{:S(2)}, u32[]{:S(2)}) collective-permute-start(f32[16,512]{1,0:T(8,128)S(1)} %get-tuple-element.92), channel_id=1, source_target_pairs={{0,3},{1,0},{2,1},{3,2},{4,7},{5,4},{6,5},{7,6},{8,11},{9,8},{10,9... | collective-permute-start | bytes 98312 | tf_op jit(solution)/shard_map/ppermute | solution.py:447
  14.4 7.6 %collective-permute-start.3 = (f32[16,512]{1,0:T(8,128)S(1)}, f32[16,512]{1,0:T(8,128)S(1)}, u32[]{:S(2)}, u32[]{:S(2)}) collective-permute-start(f32[16,512]{1,0:T(8,128)S(1)} %row_kernel.1.row_ref), channel_id=1, source_target_pairs={{0,4},{1,5},{2,6},{3,7},{4,0},{5,1},{6,2},{7,3},{8,12},{9,13},{10,... | collective-permute-start | bytes 98312 | tf_op jit(solution)/shard_map/ppermute | solution.py:451
  22.0 6.8 %collective-permute-start.4 = (f32[16,512]{1,0:T(8,128)S(1)}, f32[16,512]{1,0:T(8,128)S(1)}, u32[]{:S(2)}, u32[]{:S(2)}) collective-permute-start(f32[16,512]{1,0:T(8,128)S(1)} %plane_kernel.1), channel_id=1, source_target_pairs={{0,8},{1,9},{2,10},{3,11},{4,12},{5,13},{6,14},{7,15},{8,16},{9,17... | collective-permute-start | bytes 98312 | tf_op jit(solution)/shard_map/ppermute | solution.py:455
  23.3 5.6 %collective-permute-start.5 = (f32[16,512]{1,0:T(8,128)S(1)}, f32[16,512]{1,0:T(8,128)S(1)}, u32[]{:S(2)}, u32[]{:S(2)}) collective-permute-start(f32[16,512]{1,0:T(8,128)S(1)} %plane_kernel.1), channel_id=1, source_target_pairs={{0,16},{1,17},{2,18},{3,19},{4,20},{5,21},{6,22},{7,23},{8,24},{9,... | collective-permute-start | bytes 98312 | tf_op jit(solution)/shard_map/ppermute | solution.py:455
  25.8 3.1 %collective-permute-start.6 = (f32[16,512]{1,0:T(8,128)S(1)}, f32[16,512]{1,0:T(8,128)S(1)}, u32[]{:S(2)}, u32[]{:S(2)}) collective-permute-start(f32[16,512]{1,0:T(8,128)S(1)} %plane_kernel.1), channel_id=1, source_target_pairs={{0,24},{1,25},{2,26},{3,27},{4,28},{5,29},{6,30},{7,31},{8,0},{9,1... | collective-permute-start | bytes 98312 | tf_op jit(solution)/shard_map/ppermute | solution.py:455
  29.0 4.1 %collective-permute-start.7 = (f32[16,512]{1,0:T(8,128)S(1)}, f32[16,512]{1,0:T(8,128)S(1)}, u32[]{:S(2)}, u32[]{:S(2)}) collective-permute-start(f32[16,512]{1,0:T(8,128)S(1)} %get-tuple-element.133), channel_id=1, source_target_pairs={{0,1},{1,2},{2,3},{3,0},{4,5},{5,6},{6,7},{7,4},{8,9},{9,10},{10,1... | collective-permute-start | bytes 98312 | tf_op jit(solution)/shard_map/ppermute | solution.py:447
  29.5 4.7 %collective-permute-start.8 = (f32[16,512]{1,0:T(8,128)S(1)}, f32[16,512]{1,0:T(8,128)S(1)}, u32[]{:S(2)}, u32[]{:S(2)}) collective-permute-start(f32[16,512]{1,0:T(8,128)S(1)} %get-tuple-element.141), channel_id=1, source_target_pairs={{0,2},{1,3},{2,0},{3,1},{4,6},{5,7},{6,4},{7,5},{8,10},{9,11},{10,... | collective-permute-start | bytes 98312 | tf_op jit(solution)/shard_map/ppermute | solution.py:447
  30.9 4.4 %collective-permute-start.9 = (f32[16,512]{1,0:T(8,128)S(1)}, f32[16,512]{1,0:T(8,128)S(1)}, u32[]{:S(2)}, u32[]{:S(2)}) collective-permute-start(f32[16,512]{1,0:T(8,128)S(1)} %get-tuple-element.149), channel_id=1, source_target_pairs={{0,3},{1,0},{2,1},{3,2},{4,7},{5,4},{6,5},{7,6},{8,11},{9,8},{10,9... | collective-permute-start | bytes 98312 | tf_op jit(solution)/shard_map/ppermute | solution.py:447
  35.3 10.1 %copy-start.3 = (f32[2048]{0:T(1024)S(1)}, f32[2048]{0:T(1024)}, u32[]{:S(2)}) copy-start(f32[2048]{0:T(1024)} %param.13) | copy-start | bytes 24580
  36.7 5.6 %collective-permute-start.10 = (f32[1,384]{1,0:T(1,128)S(1)}, f32[1,384]{1,0:T(1,128)S(1)}, u32[]{:S(2)}, u32[]{:S(2)}) collective-permute-start(f32[1,384]{1,0:T(1,128)S(1)} %get-tuple-element.152.p0_ref), channel_id=1, source_target_pairs={{0,32},{32,64},{64,96},{96,0},{1,33},{33,65},{65,97},{97,1},{2,34}... | collective-permute-start | bytes 4616 | tf_op jit(solution)/shard_map/ppermute | solution.py:459
  41.6 2.6 %collective-permute-start.11 = (f32[1,384]{1,0:T(1,128)S(1)}, f32[1,384]{1,0:T(1,128)S(1)}, u32[]{:S(2)}, u32[]{:S(2)}) collective-permute-start(f32[1,384]{1,0:T(1,128)S(1)} %get-tuple-element.152.p0_ref), channel_id=1, source_target_pairs={{0,64},{32,96},{64,0},{96,32},{1,65},{33,97},{65,1},{97,33},{2,66}... | collective-permute-start | bytes 4616 | tf_op jit(solution)/shard_map/ppermute | solution.py:459
  42.3 3.0 %collective-permute-start.12 = (f32[1,384]{1,0:T(1,128)S(1)}, f32[1,384]{1,0:T(1,128)S(1)}, u32[]{:S(2)}, u32[]{:S(2)}) collective-permute-start(f32[1,384]{1,0:T(1,128)S(1)} %get-tuple-element.152.p0_ref), channel_id=1, source_target_pairs={{0,96},{32,0},{64,32},{96,64},{1,97},{33,1},{65,33},{97,65},{2,98}... | collective-permute-start | bytes 4616 | tf_op jit(solution)/shard_map/ppermute | solution.py:459

commit v2 on v1

--- a/solution.py
+++ b/solution.py
@@ -10,6 +10,8 @@
 LANES = 128
 SUB = 8
 RUN = 16
+PITCH = 52
+OUT_PITCH = 50
 OWNERS = 4
 F32 = jnp.float32
 BF16 = jnp.bfloat16
@@ -19,8 +21,8 @@
 PARAMS = pltpu.CompilerParams(vmem_limit_bytes=24 << 20)
 
 
-def cost(flops, bytes_accessed):
-    return pl.CostEstimate(flops=flops, bytes_accessed=bytes_accessed, transcendentals=0)
+def cost(us):
+    return pl.CostEstimate(flops=int(us * 1.15e9), bytes_accessed=int(us * 3.69e6), transcendentals=0)
 
 
 def spread(table):
@@ -47,8 +49,7 @@
     return jnp.where(place >= by, pltpu.roll(x, by, 0), 0.0)
 
 
-def end_of_tile(signal_ref, rates, sent_ref, ends_ref, here):
-    span = signal_ref.shape[0] // SUB
+def end_of_tile(span, signal_ref, rates, sent_ref, ends_ref, here):
     one = spread(jnp.exp(-rates))
     run = spread(jnp.exp(rates * float(-RUN)))
     total = None
@@ -56,90 +57,108 @@
         acc = None
         for i in range(RUN):
             j = g * RUN + i
-            signal = signal_ref[pl.ds(j, SUB, stride=span), :]
+            signal = signal_ref[pl.ds(j, SUB, stride=PITCH), :]
             sent_ref[pl.ds(j * SUB, SUB), here] = signal
             acc = [signal] * ORDER if acc is None else [a * o + signal for a, o in zip(acc, one)]
         for n in range(ORDER):
             ends_ref[pl.ds((g * ORDER + n) * SUB, SUB), here] = acc[n]
         total = acc if total is None else [t * r + a for t, r, a in zip(total, run, acc)]
-    place = lax.broadcasted_iota(jnp.int32, (SUB, LANES), 0).astype(F32)
+    for by in (1, 2, 4):
+        across = spread(jnp.exp(rates * float(-span * by)))
+        total = [t + pltpu.roll(t, by, 0) * a for t, a in zip(total, across)]
+    return [t[SUB - 1 :, :] for t in total]
+
+
+def end_of_piece(key_ref, value_ref, rates_ref, first, signal_ref, sent_ref, ends_ref, end_ref, at):
+    span = key_ref.shape[0] // SUB
+
+    def tile(t, _):
+        there, here = lanes_at(t * LANES), lanes_at(at + t * LANES)
+        for s in range(SUB):
+            rows = pl.ds(s * span, span)
+            signal_ref[pl.ds(s * PITCH, span), :] = key_ref[rows, there].astype(F32) * value_ref[rows, there].astype(F32)
+        ends = end_of_tile(span, signal_ref, rates_ref[:, lanes_at(first + t * LANES)], sent_ref, ends_ref, here)
+        for n in range(ORDER):
+            end_ref[n : n + 1, here] = ends[n]
+        return 0
+
+    lax.fori_loop(0, key_ref.shape[1] // LANES, tile, 0)
+
+
+def quarter_copies(by, sources, targets, sems, cuts):
+    width = targets[0].shape[1]
+    step = width // cuts
     return [
-        jnp.sum(a * jnp.exp(rates[n : n + 1, :] * ((place - float(SUB - 1)) * float(span))), axis=0, keepdims=True)
-        for n, a in enumerate(total)
+        [
+            pltpu.make_async_copy(
+                a.at[:, pl.ds(pl.multiple_of(quarter_of(by) * width + j * step, step), step)],
+                b.at[:, pl.ds(j * step, step)],
+                sems.at[s, j],
+            )
+            for s, (a, b) in enumerate(zip(sources, targets))
+        ]
+        for j in range(cuts)
     ]
 
 
-def ends_kernel(key_ref, value_ref, rates_ref, *refs):
-    outs, (key_own, value_own, key_held, value_held, signal_ref, rates_here, sems, sem) = refs[:9], refs[9:]
-    width = key_own.shape[1]
-    per = width // LANES
-    pieces = [(quarter_of(k), j) for k in (1, 2, 3) for j in range(per)]
-
-    def copies(i):
-        quarter, j = pieces[i]
-        there = lanes_at(quarter * width + j * LANES)
-        return [
-            pltpu.make_async_copy(a.at[:, there], b.at[i], sems.at[s, i])
-            for s, (a, b) in enumerate(((key_ref, key_held), (value_ref, value_held)))
-        ]
-
-    own = pl.ds(pl.multiple_of(quarter_of(0) * width, width), width)
-    own_copies = [
-        pltpu.make_async_copy(a.at[:, own], b, sems.at[s, len(pieces)])
-        for s, (a, b) in enumerate(((key_ref, key_own), (value_ref, value_own)))
-    ]
+def far_ends_kernel(key_ref, value_ref, rates_ref, *refs):
+    results, (key_held, value_held, signal_ref, rates_here, sems, sem) = refs[:9], refs[9:]
+    width = key_held.shape[2]
+    cuts = 2
+    step = width // cuts
+    sources = (key_ref, value_ref)
+    pieces = []
+    for by in (1, 2, 3):
+        pieces += quarter_copies(by, sources, (key_held.at[by - 1], value_held.at[by - 1]), sems.at[by - 1], cuts)
     rates_copy = pltpu.make_async_copy(rates_ref, rates_here, sem)
     rates_copy.start()
-    ahead = 4
+    ahead = 3
     for i in range(ahead):
-        for c in copies(i):
+        for c in pieces[i]:
             c.start()
     rates_copy.wait()
-    for i in range(len(pieces)):
-        for c in copies(i):
+    for i in range(3 * cuts):
+        for c in pieces[i]:
             c.wait()
         if i + ahead < len(pieces):
-            for c in copies(i + ahead):
+            for c in pieces[i + ahead]:
                 c.start()
-        elif i + ahead == len(pieces):
-            for c in own_copies:
-                c.start()
-        end_ref, sent_ref, ends_ref = outs[i // per :: 3]
-        quarter, j = pieces[i]
-        here = pl.ds(j * LANES, LANES)
-        signal_ref[...] = key_held[i].astype(F32) * value_held[i].astype(F32)
-        ends = end_of_tile(signal_ref, rates_here[:, lanes_at(quarter * width + j * LANES)], sent_ref, ends_ref, here)
-        for n in range(ORDER):
-            end_ref[n : n + 1, here] = ends[n]
-    for c in own_copies:
-        c.wait()
+        by, at = i // cuts, i % cuts * step
+        end_ref, sent_ref, ends_ref = results[3 * by : 3 * by + 3]
+        part = pl.ds(at, step)
+        end_of_piece(key_held.at[by, :, part], value_held.at[by, :, part], rates_here,
+                     quarter_of(by + 1) * width + at, signal_ref, sent_ref, ends_ref, end_ref, at)
+
+
+def end_shapes(tokens, width):
+    part = jax.ShapeDtypeStruct((tokens, width), F32)
+    return [jax.ShapeDtypeStruct((ORDER, width), F32), part, part]
+
+
+def in_hbm(*arrays):
+    return [pltpu.with_memory_space_constraint(a, pltpu.HBM) for a in arrays]
 
 
 def far_ends(key, value, rates):
     tokens, channels = key.shape
     width = channels // OWNERS
-    pieces = 3 * (width // LANES)
-    end = jax.ShapeDtypeStruct((ORDER, width), F32)
-    part = jax.ShapeDtypeStruct((tokens, width), F32)
-    own = jax.ShapeDtypeStruct((tokens, width), BF16)
-    constrained = [pltpu.with_memory_space_constraint(a, pltpu.HBM) for a in (key, value, rates)]
     return pl.pallas_call(
-        ends_kernel,
-        in_specs=[IN_HBM, IN_HBM, IN_HBM],
-        out_specs=[IN_VMEM] * 11,
-        out_shape=[end] * 3 + [part] * 6 + [own] * 2,
+        far_ends_kernel,
+        in_specs=[IN_HBM] * 3,
+        out_specs=[IN_VMEM] * 9,
+        out_shape=end_shapes(tokens, width) * 3,
         scratch_shapes=[
-            pltpu.VMEM((pieces, tokens, LANES), BF16),
-            pltpu.VMEM((pieces, tokens, LANES), BF16),
-            pltpu.VMEM((tokens, LANES), F32),
+            pltpu.VMEM((3, tokens, width), BF16),
+            pltpu.VMEM((3, tokens, width), BF16),
+            pltpu.VMEM((SUB * PITCH, LANES), F32),
             pltpu.VMEM((ORDER, channels), F32),
-            pltpu.SemaphoreType.DMA((2, pieces + 1)),
+            pltpu.SemaphoreType.DMA((3, 2, 2)),
             pltpu.SemaphoreType.DMA(()),
         ],
         compiler_params=PARAMS,
-        cost_estimate=cost(32 * tokens * channels, 4 * tokens * channels),
+        cost_estimate=cost(4.6),
         name="far_ends",
-    )(*constrained)
+    )(*in_hbm(key, value, rates))
 
 
 ENTRIES = 9
@@ -150,48 +169,50 @@
     return lax.div(place, 8), lax.rem(lax.div(place, 4), 2), lax.rem(place, 4)
 
 
-def own_end_kernel(key_ref, value_ref, rates_ref, end_ref, sent_ref, ends_ref, tables_ref, signal_ref):
-    tokens, width = key_ref.shape
+def own_end_kernel(key_ref, value_ref, rates_ref, end_ref, sent_ref, ends_ref, tables_ref,
+                   key_held, value_held, signal_ref, sems):
+    tokens, width = key_held.shape
     x, z, _ = position()
     first = quarter_of(0) * width
-
-    def tile(t, _):
+    (copies,) = quarter_copies(0, (key_ref, value_ref), (key_held, value_held), sems, 1)
+    for c in copies:
+        c.start()
+
+    def table(t, _):
         here = lanes_at(t * LANES)
-        rates = rates_ref[:, lanes_at(first + t * LANES)]
-        signal_ref[...] = key_ref[:, here].astype(F32) * value_ref[:, here].astype(F32)
-        ends = end_of_tile(signal_ref, rates, sent_ref, ends_ref, here)
-        for n in range(ORDER):
-            end_ref[n : n + 1, here] = ends[n]
-        rates = rates * float(-tokens)
+        rates = rates_ref[:, lanes_at(first + t * LANES)] * float(-tokens)
         tables_ref[0, :, here] = jnp.zeros((ORDER, LANES), F32)
         for m in range(1, 6):
             tables_ref[m, :, here] = jnp.exp(rates * float(m - 1))
         for k in (1, 2, 3):
-            spans = (4 * z + jnp.maximum(8 * (k - 1), 0)).astype(F32)
+            spans = (4 * z + 8 * (k - 1)).astype(F32)
             tables_ref[5 + k, :, here] = jnp.exp(rates * spans) * (x >= k).astype(F32)
         return 0
 
-    lax.fori_loop(0, width // LANES, tile, 0)
+    lax.fori_loop(0, width // LANES, table, 0)
+    for c in copies:
+        c.wait()
+    end_of_piece(key_held, value_held, rates_ref, first, signal_ref, sent_ref, ends_ref, end_ref, 0)
 
 
 def own_end(key, value, rates):
-    tokens, width = key.shape
-    part = jax.ShapeDtypeStruct((tokens, width), F32)
+    tokens, channels = key.shape
+    width = channels // OWNERS
     return pl.pallas_call(
         own_end_kernel,
-        in_specs=[IN_VMEM] * 3,
+        in_specs=[IN_HBM, IN_HBM, IN_VMEM],
         out_specs=[IN_VMEM] * 4,
-        out_shape=[
-            jax.ShapeDtypeStruct((ORDER, width), F32),
-            part,
-            part,
-            jax.ShapeDtypeStruct((ENTRIES, ORDER, width), F32),
+        out_shape=end_shapes(tokens, width) + [jax.ShapeDtypeStruct((ENTRIES, ORDER, width), F32)],
+        scratch_shapes=[
+            pltpu.VMEM((tokens, width), BF16),
+            pltpu.VMEM((tokens, width), BF16),
+            pltpu.VMEM((SUB * PITCH, LANES), F32),
+            pltpu.SemaphoreType.DMA((2, 1)),
         ],
-        scratch_shapes=[pltpu.VMEM((tokens, LANES), F32)],
         compiler_params=PARAMS,
-        cost_estimate=cost(32 * tokens * width, 12 * tokens * width),
+        cost_estimate=cost(2.3),
         name="own_end",
-    )(key, value, rates)
+    )(*in_hbm(key, value), rates)
 
 
 def sender(y, by):
@@ -229,7 +250,7 @@
         out_specs=[IN_VMEM] * count,
         out_shape=[out] * count,
         compiler_params=PARAMS,
-        cost_estimate=cost(10 * out.size, 40 * out.size),
+        cost_estimate=cost(0.05),
         name=kernel.__name__,
     )(*args)
 
@@ -241,14 +262,14 @@
     place = lax.broadcasted_iota(jnp.int32, (SUB, LANES), 0).astype(F32)
 
     def copy(t):
-        there = lanes_at(quarter_of(by) * width + t * LANES)
+        there = lanes_at(quarter_of(-by) * width + t * LANES)
         return pltpu.make_async_copy(gate_ref.at[:, there], gate_held.at[t], sems.at[t])
 
     for t in range(width // LANES):
         copy(t).start()
 
     def tile(t, _):
-        lanes = lanes_at(quarter_of(by) * width + t * LANES)
+        lanes = lanes_at(quarter_of(-by) * width + t * LANES)
         here = lanes_at(t * LANES)
         rates = rates_ref[:, lanes]
         residues = residues_ref[:, lanes]
@@ -280,24 +301,31 @@
             for g in (0, 1):
                 enter_ref[pl.ds((g * ORDER + n) * SUB, SUB), here] = first[n] * end(g, n)
 
-        copy(t).wait()
-        gate_f32[...] = gate_held[t].astype(F32)
-
         def group(g, _):
             signal = []
             for i in range(RUN):
                 rows = pl.ds(pl.multiple_of((g * RUN + i) * SUB, SUB), SUB)
                 signal.append(sent_ref[rows, here])
-                gate = gate_f32[pl.ds(g * RUN + i, SUB, stride=span), :]
-                conv = add_up([taps[i - m] * signal[m] for m in range(i + 1)])
-                mixed_ref[rows, here] = gate * conv
-                gate_out[rows, here] = gate
+                mixed_ref[rows, here] = add_up([taps[i - m] * signal[m] for m in range(i + 1)])
             return 0
 
         lax.fori_loop(0, span // RUN, group, 0)
         return 0
 
+    def gating(t, _):
+        here = lanes_at(t * LANES)
+        copy(t).wait()
+        for s in range(SUB):
+            gate_f32[pl.ds(s * PITCH, span), :] = gate_held[t, pl.ds(s * span, span), :].astype(F32)
+        for j in range(span):
+            rows = pl.ds(j * SUB, SUB)
+            gate = gate_f32[pl.ds(j, SUB, stride=PITCH), :]
+            mixed_ref[rows, here] = gate * mixed_ref[rows, here]
+            gate_out[rows, here] = gate
+        return 0
+
     lax.fori_loop(0, width // LANES, tile, 0)
+    lax.fori_loop(0, width // LANES, gating, 0)
 
 
 def local_part(by, sent, ends, gate, rates, residues, skip):
@@ -313,11 +341,11 @@
         out_shape=[token_part, token_part, mode_part, mode_part, enter_part],
         scratch_shapes=[
             pltpu.VMEM((width // LANES, tokens, LANES), BF16),
-            pltpu.VMEM((tokens, LANES), F32),
+            pltpu.VMEM((SUB * PITCH, LANES), F32),
             pltpu.SemaphoreType.DMA((width // LANES,)),
         ],
         compiler_params=PARAMS,
-        cost_estimate=cost(30 * tokens * width, 14 * tokens * width),
+        cost_estimate=cost(1.4),
         name="local_part",
     )(sent, ends, gate, rates, residues, skip)
 
@@ -349,7 +377,7 @@
                 terms = [a + enter_ref[pl.ds((g * ORDER + n) * SUB, SUB), here] for n, a in enumerate(terms)]
             rows = pl.ds(j * SUB, SUB)
             gated = mixed_ref[rows, here] + gate_ref[rows, here] * add_up(terms)
-            gated_ref[t, pl.ds(j, SUB, stride=span), :] = gated
+            gated_ref[t, pl.ds(j, SUB, stride=OUT_PITCH), :] = gated
             sums_ref[rows, :] += gated * gated
         return 0
 
@@ -367,7 +395,7 @@
 def mix(by, last, part, state, rates, sums):
     tokens, width = part[0].shape
     out_sums = jax.ShapeDtypeStruct((tokens, LANES), F32)
-    gated = jax.ShapeDtypeStruct((width // LANES, tokens, LANES), F32)
+    gated = jax.ShapeDtypeStruct((width // LANES, SUB * OUT_PITCH, LANES), F32)
     args = [*part, state, rates] + ([] if sums is None else [sums])
     if last:
         outs, scratch = [jax.ShapeDtypeStruct((1, tokens), F32), gated], [pltpu.VMEM((tokens, LANES), F32)]
@@ -380,13 +408,13 @@
         out_shape=outs,
         scratch_shapes=scratch,
         compiler_params=PARAMS,
-        cost_estimate=cost(40 * tokens * width, 12 * tokens * width),
+        cost_estimate=cost(1.1),
         name="mix",
     )(*args)
 
 
 def norm_kernel(g0, g1, g2, g3, gain_ref, p0_ref, p1_ref, p2_ref, p3_ref, out_ref, runs_ref, scale_ref, held, sems):
-    tiles, tokens, _ = g0.shape
+    tiles, tokens = g0.shape[0], scale_ref.shape[0]
     width = tiles * LANES
     span = tokens // SUB
     total = (p0_ref[...] + p1_ref[...]) + (p2_ref[...] + p3_ref[...])
@@ -409,7 +437,10 @@
         def tile(t, _):
             here = lanes_at(t * LANES)
             gain = gain_ref[:, lanes_at(first + t * LANES)]
-            held[by, :, here] = (gated_ref[t] * scale_ref[...] * gain).astype(BF16)
+            for s in range(SUB):
+                rows = pl.ds(s * span, span)
+                gated = gated_ref[t, pl.ds(s * OUT_PITCH, span), :]
+                held[by, rows, here] = (gated * scale_ref[rows, :] * gain).astype(BF16)
             return 0
 
         lax.fori_loop(0, width // LANES, tile, 0)
@@ -423,7 +454,7 @@
 
 
 def norm(gated, gain, powers):
-    tiles, tokens, _ = gated[0].shape
+    tiles, tokens = gated[0].shape[0], powers[0].shape[1]
     width = tiles * LANES
     channels = width * OWNERS
     return pl.pallas_call(
@@ -438,7 +469,7 @@
             pltpu.SemaphoreType.DMA((OWNERS,)),
         ],
         compiler_params=PARAMS,
-        cost_estimate=cost(3 * tokens * channels, 6 * tokens * channels),
+        cost_estimate=cost(1.7),
         name="norm",
     )(*gated, gain, *powers)
 
@@ -465,31 +496,33 @@
     parts = [None] * OWNERS
 
     def local(by, rates):
-        parts[by] = local_part(-by, sent[-by], inner[-by], gate, rates, residues, skip)
-
+        parts[by] = local_part(by, sent[-by], inner[-by], gate, rates, residues, skip)
+
+    ends, sent, inner = ([None] * OWNERS for _ in range(3))
     outs = far_ends(key, value, rates)
-    ends, sent, inner = [None, *outs[0:3]], [None, *outs[3:6]], [None, *outs[6:9]]
-    got = [over_y(ends[k], k) for k in (1, 2, 3)]
-    own, sent[0], inner[0], tables = own_end(*outs[9:11], rates)
-    local(1, rates)
-    own, parts[1] = tie((own, parts[1]))
-    ends = [own] + got
+    ends[1:], sent[1:], inner[1:] = outs[0::3], outs[1::3], outs[2::3]
+    ends[1], rates0 = tie((ends[1], rates))
+    for k in (2, 1, 3):
+        ends[k] = over_y(ends[k], k)
+    ends[0], sent[0], inner[0], tables = own_end(key, value, rates0)
     (row,) = small(row_kernel, 1, *ends, tables)
 
     row, rates1 = tie((row, rates))
     other = over_z(row)
-    local(2, rates1)
-    local(3, rates1)
-    other, parts[2], parts[3] = tie((other, parts[2], parts[3]))
+    for by in (1, 2, 3):
+        local(by, rates1)
+    other, *parts[1:] = tie((other, *parts[1:]))
     (plane,) = small(plane_kernel, 1, row, other, tables)
 
     plane, rates2 = tie((plane, rates))
-    got = [over_x(plane, k) for k in (1, 2, 3)]
+    got = {k: over_x(plane, k) for k in (2, 1, 3)}
+    got = [got[k] for k in (1, 2, 3)]
     local(0, rates2)
     got[0], parts[0] = tie((got[0], parts[0]))
     states = list(small(states_kernel, OWNERS, *ends, other, *got, tables))
 
-    states = [states[0]] + [over_y(s, k) for k, s in zip((1, 2, 3), states[1:])]
+    for k in (2, 1, 3):
+        states[k] = over_y(states[k], k)
     gated, sums = [], None
     for by in range(OWNERS):
         first, second = mix(by, by == OWNERS - 1, parts[by], states[by], rates, sums)

time: 47.3 us -> 46.8 us (0.989)
  Pallas kernels: 20.8 us -> 18.8 us
  starting transfers between devices: 23 us -> 24 us
  waiting for transfers between devices: 3.03 us -> 3.62 us
    pallas_call x4, Pallas kernels: 7.79 us -> 5.16 us  [local_part(): pl.pallas_call(lambda *refs: local_kernel(by, *refs), in_specs=[IN_VMEM,...]
    ppermute x3, starting transfers between devices: 5.63 us -> 6.56 us  [over_ch(): return lax.ppermute(x, 'ch', [(i, (i + by) % 4) for i in range(4)])]
    pallas_call x2, Pallas kernels: 6.46 us -> 7.19 us  [the longest x1 4.91 us: far_ends(): pl.pallas_call(far_ends_kernel, in_specs=[IN_HBM] * 3, out_specs=[IN_VMEM...]
    ppermute x3, waiting for transfers between devices: 0.01 us -> 0.6 us  [over_x(): return lax.ppermute(x, 'seq', [(i, (i + 8 * by) % 32) for i in range(32)])]
  transfers between devices with their start and end apart: 13 -> 13, of which waited for: 2 -> 3; matrix products, arithmetic and copies ran while one was open for 0% -> 0% of each run, Pallas kernels for 26% -> 23%
where the time goes in v2:
time: 46.8 us; the launch traced here: 46.6 us
  starting transfers between devices  24 us (51%)
  Pallas kernels  18.8 us (40%)
  waiting for transfers between devices  3.62 us (8%)
    ppermute x6, starting transfers between devices, over_y(): lax.ppermute(x, 'seq', [(i, i // 4 * 4 + (i + by) % 4) for i in range(32)])  8.9 us
    ppermute x3, starting transfers between devices, over_ch(): return lax.ppermute(x, 'ch', [(i, (i + by) % 4) for i in range(4)])  6.56 us
    pallas_call x4, Pallas kernels, local_part(): pl.pallas_call(lambda *refs: local_kernel(by, *refs), in_specs=[IN_VMEM,...  5.16 us
    pallas_call x1, Pallas kernels, far_ends(): pl.pallas_call(far_ends_kernel, in_specs=[IN_HBM] * 3, out_specs=[IN_VMEM...  4.91 us
    ppermute x3, starting transfers between devices, over_x(): return lax.ppermute(x, 'seq', [(i, (i + 8 * by) % 32) for i in range(32)])  4.88 us
    pallas_call x4, Pallas kernels, mix(): pl.pallas_call(lambda *refs: mix_kernel(by, last, *refs), in_specs=[IN_VM...  4.55 us
    ppermute x1, starting transfers between devices, over_z(): return lax.ppermute(x, 'seq', [(i, i ^ 4) for i in range(32)])  3.68 us
    ppermute x3, waiting for transfers between devices, over_ch(): return lax.ppermute(x, 'ch', [(i, (i + by) % 4) for i in range(4)])  3 us
  transfers between devices with their start and end apart: 13, of which 3 were waited for; matrix products, arithmetic and copies ran while one was open for 0% of the time, Pallas kernels for 23%

profile of v2, /device:TPU:1, one launch (start us, length us, event | category | flops | bytes accessed | tf_op | source)
XLA Modules:
  0.0 46.6 jit_solution(15940917792435855426)
XLA Ops:
  0.0 4.9 %far_ends.1 = (f32[16,512]{1,0:T(8,128)S(1)}, f32[384,512]{1,0:T(8,128)S(1)}, f32[384,512]{1,0:T(8,128)S(1)}, f32[16,512]{1,0:T(8,128)S(1)}, f32[384,512]{1,0:T(...) custom-call(bf16[384,2048]{1,0:T(8,128)(2,1)} %key_ref.3, ...), custom_call_target="tpu_custom_call" | custom-call | flops 5289999872 | bytes 16974000 | tf_op jit(solution)/shard_map/far_ends/pallas_call | solution.py:145
  4.9 2.2 %collective-permute-start = (f32[16,512]{1,0:T(8,128)S(1)}, f32[16,512]{1,0:T(8,128)S(1)}, u32[]{:S(2)}, u32[]{:S(2)}) collective-permute-start(f32[16,512]{1,0:T(8,128)S(1)} %get-tuple-element.81), channel_id=1, source_target_pairs={{0,1},{1,2},{2,3},{3,0},{4,5},{5,6},{6,7},{7,4},{8,9},{9,10},{10,1... | collective-permute-start | bytes 98312 | tf_op jit(solution)/shard_map/ppermute | solution.py:478
  7.1 2.6 %collective-permute-start.1 = (f32[16,512]{1,0:T(8,128)S(1)}, f32[16,512]{1,0:T(8,128)S(1)}, u32[]{:S(2)}, u32[]{:S(2)}) collective-permute-start(f32[16,512]{1,0:T(8,128)S(1)} %get-tuple-element.82), channel_id=1, source_target_pairs={{0,2},{1,3},{2,0},{3,1},{4,6},{5,7},{6,4},{7,5},{8,10},{9,11},{10,... | collective-permute-start | bytes 98312 | tf_op jit(solution)/shard_map/ppermute | solution.py:478
  9.7 1.1 %collective-permute-start.2 = (f32[16,512]{1,0:T(8,128)S(1)}, f32[16,512]{1,0:T(8,128)S(1)}, u32[]{:S(2)}, u32[]{:S(2)}) collective-permute-start(f32[16,512]{1,0:T(8,128)S(1)} %get-tuple-element.83), channel_id=1, source_target_pairs={{0,3},{1,0},{2,1},{3,2},{4,7},{5,4},{6,5},{7,6},{8,11},{9,8},{10,9... | collective-permute-start | bytes 98312 | tf_op jit(solution)/shard_map/ppermute | solution.py:478
  10.8 2.3 %own_end.1 = (f32[16,512]{1,0:T(8,128)S(1)}, f32[384,512]{1,0:T(8,128)S(1)}, f32[384,512]{1,0:T(8,128)S(1)}, f32[9,16,512]{2,1,0:T(8,128)S(1)}) custom-call(bf16[384,2048]{1,0:T(8,128)(2,1)} %key_ref.3, bf16[384,2048]{1,0:T(8,128)(2,1)} %value_ref.3, f32[16,2048]{1,0:T(8,128)S(1)} %copy-done.1), custom_call_target="tpu_custom_call" | custom-call | flops 2644999936 | bytes 8487000 | tf_op jit(solution)/shard_map/own_end/pallas_call | solution.py:201
  13.2 3.7 %collective-permute-start.3 = (f32[16,512]{1,0:T(8,128)S(1)}, f32[16,512]{1,0:T(8,128)S(1)}, u32[]{:S(2)}, u32[]{:S(2)}) collective-permute-start(f32[16,512]{1,0:T(8,128)S(1)} %row_kernel.1.row_ref), channel_id=1, source_target_pairs={{0,4},{1,5},{2,6},{3,7},{4,0},{5,1},{6,2},{7,3},{8,12},{9,13},{10,... | collective-permute-start | bytes 98312 | tf_op jit(solution)/shard_map/ppermute | solution.py:482
  16.9 1.3 %local_part.6 = (f32[384,512]{1,0:T(8,128)S(1)}, f32[384,512]{1,0:T(8,128)S(1)}, f32[128,512]{1,0:T(8,128)S(1)}, f32[128,512]{1,0:T(8,128)S(1)}, f32[256,512]{1,0:T(8,128)S(1)}) custom-call(f32[384,512]{1,0:T(8,128)S(1)} %get-tuple-element.101.refs_0_, f32[384,512]{1,0:T(8,128)S(1)} %get-tuple-element.102.refs_1_, bf16[384,2048]{1,0:T(8,128)(2,1)} %refs_2_.7, ...), custom_call_target="tpu_custom_call" | custom-call | flops 1610000000 | bytes 5166000 | tf_op jit(solution)/shard_map/local_part/pallas_call | solution.py:337
  18.1 1.3 %local_part.5 = (f32[384,512]{1,0:T(8,128)S(1)}, f32[384,512]{1,0:T(8,128)S(1)}, f32[128,512]{1,0:T(8,128)S(1)}, f32[128,512]{1,0:T(8,128)S(1)}, f32[256,512]{1,0:T(8,128)S(1)}) custom-call(f32[384,512]{1,0:T(8,128)S(1)} %get-tuple-element.94.refs_0_, f32[384,512]{1,0:T(8,128)S(1)} %get-tuple-element.95.refs_1_, bf16[384,2048]{1,0:T(8,128)(2,1)} %refs_2_.7, ...), custom_call_target="tpu_custom_call" | custom-call | flops 1610000000 | bytes 5166000 | tf_op jit(solution)/shard_map/local_part/pallas_call | solution.py:337
  19.4 1.3 %local_part.4 = (f32[384,512]{1,0:T(8,128)S(1)}, f32[384,512]{1,0:T(8,128)S(1)}, f32[128,512]{1,0:T(8,128)S(1)}, f32[128,512]{1,0:T(8,128)S(1)}, f32[256,512]{1,0:T(8,128)S(1)}) custom-call(f32[384,512]{1,0:T(8,128)S(1)} %get-tuple-element.86.refs_0_, f32[384,512]{1,0:T(8,128)S(1)} %get-tuple-element.87.refs_1_, bf16[384,2048]{1,0:T(8,128)(2,1)} %refs_2_.7, ...), custom_call_target="tpu_custom_call" | custom-call | flops 1610000000 | bytes 5166000 | tf_op jit(solution)/shard_map/local_part/pallas_call | solution.py:337
  20.8 1.3 %collective-permute-start.4 = (f32[16,512]{1,0:T(8,128)S(1)}, f32[16,512]{1,0:T(8,128)S(1)}, u32[]{:S(2)}, u32[]{:S(2)}) collective-permute-start(f32[16,512]{1,0:T(8,128)S(1)} %plane_kernel.1), channel_id=1, source_target_pairs={{0,8},{1,9},{2,10},{3,11},{4,12},{5,13},{6,14},{7,15},{8,16},{9,17... | collective-permute-start | bytes 98312 | tf_op jit(solution)/shard_map/ppermute | solution.py:486
  22.1 2.5 %collective-permute-start.5 = (f32[16,512]{1,0:T(8,128)S(1)}, f32[16,512]{1,0:T(8,128)S(1)}, u32[]{:S(2)}, u32[]{:S(2)}) collective-permute-start(f32[16,512]{1,0:T(8,128)S(1)} %plane_kernel.1), channel_id=1, source_target_pairs={{0,16},{1,17},{2,18},{3,19},{4,20},{5,21},{6,22},{7,23},{8,24},{9,... | collective-permute-start | bytes 98312 | tf_op jit(solution)/shard_map/ppermute | solution.py:486
  24.5 1.2 %collective-permute-start.6 = (f32[16,512]{1,0:T(8,128)S(1)}, f32[16,512]{1,0:T(8,128)S(1)}, u32[]{:S(2)}, u32[]{:S(2)}) collective-permute-start(f32[16,512]{1,0:T(8,128)S(1)} %plane_kernel.1), channel_id=1, source_target_pairs={{0,24},{1,25},{2,26},{3,27},{4,28},{5,29},{6,30},{7,31},{8,0},{9,1... | collective-permute-start | bytes 98312 | tf_op jit(solution)/shard_map/ppermute | solution.py:486
  25.7 1.3 %local_part.7 = (f32[384,512]{1,0:T(8,128)S(1)}, f32[384,512]{1,0:T(8,128)S(1)}, f32[128,512]{1,0:T(8,128)S(1)}, f32[128,512]{1,0:T(8,128)S(1)}, f32[256,512]{1,0:T(8,128)S(1)}) custom-call(f32[384,512]{1,0:T(8,128)S(1)} %get-tuple-element.110.refs_0_, f32[384,512]{1,0:T(8,128)S(1)} %get-tuple-element.111.refs_1_, bf16[384,2048]{1,0:T(8,128)(2,1)} %refs_2_.7, ...), custom_call_target="tpu_custom_call" | custom-call | flops 1610000000 | bytes 5166000 | tf_op jit(solution)/shard_map/local_part/pallas_call | solution.py:337
  27.0 0.6 %collective-permute-done.6.p3 = f32[16,512]{1,0:T(8,128)S(1)} collective-permute-done((f32[16,512]{1,0:T(8,128)S(1)}, f32[16,512]{1,0:T(8,128)S(1)}, u32[]{:S(2)}, u32[]{:S(2)}) %collective-permute-start.6) | collective-permute-done | bytes 32800 | tf_op jit(solution)/shard_map/ppermute | solution.py:486
  27.9 2.3 %collective-permute-start.8 = (f32[16,512]{1,0:T(8,128)S(1)}, f32[16,512]{1,0:T(8,128)S(1)}, u32[]{:S(2)}, u32[]{:S(2)}) collective-permute-start(f32[16,512]{1,0:T(8,128)S(1)} %get-tuple-element.139), channel_id=1, source_target_pairs={{0,2},{1,3},{2,0},{3,1},{4,6},{5,7},{6,4},{7,5},{8,10},{9,11},{10,... | collective-permute-start | bytes 98312 | tf_op jit(solution)/shard_map/ppermute | solution.py:478
  30.7 1.1 %mix.4 = (f32[4,400,128]{2,1,0:T(8,128)S(1)}, f32[384,128]{1,0:T(8,128)S(1)}) custom-call(f32[384,512]{1,0:T(8,128)S(1)} %get-tuple-element.118.refs_0_, f32[384,512]{1,0:T(8,128)S(1)} %get-tuple-element.119.refs_1_, f32[128,512]{1,0:T(8,128)S(1)} %get-tuple-element.120.refs_2_, f32[128,512]{1,0:T(8,128)S(1)} %get-tuple-element.121.refs_3_, ...), custom_call_target="tpu_custom_call" | custom-call | flops 1264999936 | bytes 4059000 | tf_op jit(solution)/shard_map/mix/pallas_call | solution.py:404
  31.8 1.1 %mix.5 = (f32[4,400,128]{2,1,0:T(8,128)S(1)}, f32[384,128]{1,0:T(8,128)S(1)}) custom-call(f32[384,512]{1,0:T(8,128)S(1)} %get-tuple-element.126.refs_0_, f32[384,512]{1,0:T(8,128)S(1)} %get-tuple-element.127.refs_1_, f32[128,512]{1,0:T(8,128)S(1)} %get-tuple-element.128.refs_2_, f32[128,512]{1,0:T(8,128)S(1)} %get-tuple-element.129.refs_3_, ...), custom_call_target="tpu_custom_call" | custom-call | flops 1264999936 | bytes 4059000 | tf_op jit(solution)/shard_map/mix/pallas_call | solution.py:404
  32.8 1.1 %mix.6 = (f32[4,400,128]{2,1,0:T(8,128)S(1)}, f32[384,128]{1,0:T(8,128)S(1)}) custom-call(f32[384,512]{1,0:T(8,128)S(1)} %get-tuple-element.134.refs_0_, f32[384,512]{1,0:T(8,128)S(1)} %get-tuple-element.135.refs_1_, f32[128,512]{1,0:T(8,128)S(1)} %get-tuple-element.136.refs_2_, f32[128,512]{1,0:T(8,128)S(1)} %get-tuple-element.137.refs_3_, ...), custom_call_target="tpu_custom_call" | custom-call | flops 1264999936 | bytes 4059000 | tf_op jit(solution)/shard_map/mix/pallas_call | solution.py:404
  33.9 1.4 %mix.7 = (f32[1,384]{1,0:T(1,128)S(1)}, f32[4,400,128]{2,1,0:T(8,128)S(1)}) custom-call(f32[384,512]{1,0:T(8,128)S(1)} %get-tuple-element.142.refs_0_, f32[384,512]{1,0:T(8,128)S(1)} %get-tuple-element.143.refs_1_, f32[128,512]{1,0:T(8,128)S(1)} %get-tuple-element.144.refs_2_, f32[128,512]{1,0:T(8,128)S(1)} %get-tuple-element.145.refs_3_, ...), custom_call_target="tpu_custom_call" | custom-call | flops 1264999936 | bytes 4059000 | tf_op jit(solution)/shard_map/mix/pallas_call | solution.py:404
  35.3 5.8 %collective-permute-start.10 = (f32[1,384]{1,0:T(1,128)S(1)}, f32[1,384]{1,0:T(1,128)S(1)}, u32[]{:S(2)}, u32[]{:S(2)}) collective-permute-start(f32[1,384]{1,0:T(1,128)S(1)} %get-tuple-element.150.p0_ref), channel_id=1, source_target_pairs={{0,32},{32,64},{64,96},{96,0},{1,33},{33,65},{65,97},{97,1},{2,34}... | collective-permute-start | bytes 4616 | tf_op jit(solution)/shard_map/ppermute | solution.py:490
  41.1 0.7 %collective-permute-start.11 = (f32[1,384]{1,0:T(1,128)S(1)}, f32[1,384]{1,0:T(1,128)S(1)}, u32[]{:S(2)}, u32[]{:S(2)}) collective-permute-start(f32[1,384]{1,0:T(1,128)S(1)} %get-tuple-element.150.p0_ref), channel_id=1, source_target_pairs={{0,64},{32,96},{64,0},{96,32},{1,65},{33,97},{65,1},{97,33},{2,66}... | collective-permute-start | bytes 4616 | tf_op jit(solution)/shard_map/ppermute | solution.py:490
  41.8 1.9 %collective-permute-done.11.p2_ref = f32[1,384]{1,0:T(1,128)S(1)} collective-permute-done((f32[1,384]{1,0:T(1,128)S(1)}, f32[1,384]{1,0:T(1,128)S(1)}, u32[]{:S(2)}, u32[]{:S(2)}) %collective-permute-start.11) | collective-permute-done | bytes 1568 | tf_op jit(solution)/shard_map/ppermute | solution.py:490
  43.7 1.1 %collective-permute-done.12.p3_ref = f32[1,384]{1,0:T(1,128)S(1)} collective-permute-done((f32[1,384]{1,0:T(1,128)S(1)}, f32[1,384]{1,0:T(1,128)S(1)}, u32[]{:S(2)}, u32[]{:S(2)}) %collective-permute-start.12) | collective-permute-done | bytes 1568 | tf_op jit(solution)/shard_map/ppermute | solution.py:490
  44.8 1.7 %norm.1 = bf16[384,2048]{1,0:T(8,128)(2,1)} custom-call(f32[4,400,128]{2,1,0:T(8,128)S(1)} %get-tuple-element.125.g0, f32[4,400,128]{2,1,0:T(8,128)S(1)} %get-tuple-element.133.g1, f32[4,400,128]{2,1,0:T(8,128)S(1)} %get-tuple-element.141.g2, f32[4,400,128]{2,1,0:T(8,128)S(1)} %get-tuple-element.149.g3, f32[1,2048]{1,0:T(1,128)S(1)} %bitcast.6, ...), custom_call_target="tpu_custom_call" | custom-call | flops 1955000064 | bytes 6273000 | tf_op jit(solution)/shard_map/norm/pallas_call | solution.py:460
  (24 shorter events, 0.9 us)
Async XLA Ops:
  0.0 10.8 %copy-start.1 = (f32[16,2048]{1,0:T(8,128)S(1)}, f32[16,2048]{1,0:T(8,128)}, u32[]{:S(2)}) copy-start(f32[16,2048]{1,0:T(8,128)} %refs_6_.7) | copy-start | bytes 393220
  4.9 8.2 %collective-permute-start = (f32[16,512]{1,0:T(8,128)S(1)}, f32[16,512]{1,0:T(8,128)S(1)}, u32[]{:S(2)}, u32[]{:S(2)}) collective-permute-start(f32[16,512]{1,0:T(8,128)S(1)} %get-tuple-element.81), channel_id=1, source_target_pairs={{0,1},{1,2},{2,3},{3,0},{4,5},{5,6},{6,7},{7,4},{8,9},{9,10},{10,1... | collective-permute-start | bytes 98312 | tf_op jit(solution)/shard_map/ppermute | solution.py:478
  7.1 6.0 %collective-permute-start.1 = (f32[16,512]{1,0:T(8,128)S(1)}, f32[16,512]{1,0:T(8,128)S(1)}, u32[]{:S(2)}, u32[]{:S(2)}) collective-permute-start(f32[16,512]{1,0:T(8,128)S(1)} %get-tuple-element.82), channel_id=1, source_target_pairs={{0,2},{1,3},{2,0},{3,1},{4,6},{5,7},{6,4},{7,5},{8,10},{9,11},{10,... | collective-permute-start | bytes 98312 | tf_op jit(solution)/shard_map/ppermute | solution.py:478
  9.7 7.1 %copy-start = (f32[16,2048]{1,0:T(8,128)S(1)}, f32[16,2048]{1,0:T(8,128)}, u32[]{:S(2)}) copy-start(f32[16,2048]{1,0:T(8,128)} %refs_4_.7) | copy-start | bytes 393220
  9.7 7.1 %copy-start.2 = (f32[2048]{0:T(1024)S(1)}, f32[2048]{0:T(1024)}, u32[]{:S(2)}) copy-start(f32[2048]{0:T(1024)} %param.12) | copy-start | bytes 24580
  9.7 3.4 %collective-permute-start.2 = (f32[16,512]{1,0:T(8,128)S(1)}, f32[16,512]{1,0:T(8,128)S(1)}, u32[]{:S(2)}, u32[]{:S(2)}) collective-permute-start(f32[16,512]{1,0:T(8,128)S(1)} %get-tuple-element.83), channel_id=1, source_target_pairs={{0,3},{1,0},{2,1},{3,2},{4,7},{5,4},{6,5},{7,6},{8,11},{9,8},{10,9... | collective-permute-start | bytes 98312 | tf_op jit(solution)/shard_map/ppermute | solution.py:478
  13.2 7.6 %collective-permute-start.3 = (f32[16,512]{1,0:T(8,128)S(1)}, f32[16,512]{1,0:T(8,128)S(1)}, u32[]{:S(2)}, u32[]{:S(2)}) collective-permute-start(f32[16,512]{1,0:T(8,128)S(1)} %row_kernel.1.row_ref), channel_id=1, source_target_pairs={{0,4},{1,5},{2,6},{3,7},{4,0},{5,1},{6,2},{7,3},{8,12},{9,13},{10,... | collective-permute-start | bytes 98312 | tf_op jit(solution)/shard_map/ppermute | solution.py:482
  20.8 6.2 %collective-permute-start.4 = (f32[16,512]{1,0:T(8,128)S(1)}, f32[16,512]{1,0:T(8,128)S(1)}, u32[]{:S(2)}, u32[]{:S(2)}) collective-permute-start(f32[16,512]{1,0:T(8,128)S(1)} %plane_kernel.1), channel_id=1, source_target_pairs={{0,8},{1,9},{2,10},{3,11},{4,12},{5,13},{6,14},{7,15},{8,16},{9,17... | collective-permute-start | bytes 98312 | tf_op jit(solution)/shard_map/ppermute | solution.py:486
  22.1 4.9 %collective-permute-start.5 = (f32[16,512]{1,0:T(8,128)S(1)}, f32[16,512]{1,0:T(8,128)S(1)}, u32[]{:S(2)}, u32[]{:S(2)}) collective-permute-start(f32[16,512]{1,0:T(8,128)S(1)} %plane_kernel.1), channel_id=1, source_target_pairs={{0,16},{1,17},{2,18},{3,19},{4,20},{5,21},{6,22},{7,23},{8,24},{9,... | collective-permute-start | bytes 98312 | tf_op jit(solution)/shard_map/ppermute | solution.py:486
  24.5 3.1 %collective-permute-start.6 = (f32[16,512]{1,0:T(8,128)S(1)}, f32[16,512]{1,0:T(8,128)S(1)}, u32[]{:S(2)}, u32[]{:S(2)}) collective-permute-start(f32[16,512]{1,0:T(8,128)S(1)} %plane_kernel.1), channel_id=1, source_target_pairs={{0,24},{1,25},{2,26},{3,27},{4,28},{5,29},{6,30},{7,31},{8,0},{9,1... | collective-permute-start | bytes 98312 | tf_op jit(solution)/shard_map/ppermute | solution.py:486
  27.7 4.1 %collective-permute-start.7 = (f32[16,512]{1,0:T(8,128)S(1)}, f32[16,512]{1,0:T(8,128)S(1)}, u32[]{:S(2)}, u32[]{:S(2)}) collective-permute-start(f32[16,512]{1,0:T(8,128)S(1)} %get-tuple-element.131), channel_id=1, source_target_pairs={{0,1},{1,2},{2,3},{3,0},{4,5},{5,6},{6,7},{7,4},{8,9},{9,10},{10,1... | collective-permute-start | bytes 98312 | tf_op jit(solution)/shard_map/ppermute | solution.py:478
  27.9 4.9 %collective-permute-start.8 = (f32[16,512]{1,0:T(8,128)S(1)}, f32[16,512]{1,0:T(8,128)S(1)}, u32[]{:S(2)}, u32[]{:S(2)}) collective-permute-start(f32[16,512]{1,0:T(8,128)S(1)} %get-tuple-element.139), channel_id=1, source_target_pairs={{0,2},{1,3},{2,0},{3,1},{4,6},{5,7},{6,4},{7,5},{8,10},{9,11},{10,... | collective-permute-start | bytes 98312 | tf_op jit(solution)/shard_map/ppermute | solution.py:478
  30.3 3.6 %collective-permute-start.9 = (f32[16,512]{1,0:T(8,128)S(1)}, f32[16,512]{1,0:T(8,128)S(1)}, u32[]{:S(2)}, u32[]{:S(2)}) collective-permute-start(f32[16,512]{1,0:T(8,128)S(1)} %get-tuple-element.147), channel_id=1, source_target_pairs={{0,3},{1,0},{2,1},{3,2},{4,7},{5,4},{6,5},{7,6},{8,11},{9,8},{10,9... | collective-permute-start | bytes 98312 | tf_op jit(solution)/shard_map/ppermute | solution.py:478
  33.9 10.9 %copy-start.3 = (f32[2048]{0:T(1024)S(1)}, f32[2048]{0:T(1024)}, u32[]{:S(2)}) copy-start(f32[2048]{0:T(1024)} %param.13) | copy-start | bytes 24580
  35.3 6.6 %collective-permute-start.10 = (f32[1,384]{1,0:T(1,128)S(1)}, f32[1,384]{1,0:T(1,128)S(1)}, u32[]{:S(2)}, u32[]{:S(2)}) collective-permute-start(f32[1,384]{1,0:T(1,128)S(1)} %get-tuple-element.150.p0_ref), channel_id=1, source_target_pairs={{0,32},{32,64},{64,96},{96,0},{1,33},{33,65},{65,97},{97,1},{2,34}... | collective-permute-start | bytes 4616 | tf_op jit(solution)/shard_map/ppermute | solution.py:490
  41.1 2.6 %collective-permute-start.11 = (f32[1,384]{1,0:T(1,128)S(1)}, f32[1,384]{1,0:T(1,128)S(1)}, u32[]{:S(2)}, u32[]{:S(2)}) collective-permute-start(f32[1,384]{1,0:T(1,128)S(1)} %get-tuple-element.150.p0_ref), channel_id=1, source_target_pairs={{0,64},{32,96},{64,0},{96,32},{1,65},{33,97},{65,1},{97,33},{2,66}... | collective-permute-start | bytes 4616 | tf_op jit(solution)/shard_map/ppermute | solution.py:490
  41.8 3.0 %collective-permute-start.12 = (f32[1,384]{1,0:T(1,128)S(1)}, f32[1,384]{1,0:T(1,128)S(1)}, u32[]{:S(2)}, u32[]{:S(2)}) collective-permute-start(f32[1,384]{1,0:T(1,128)S(1)} %get-tuple-element.150.p0_ref), channel_id=1, source_target_pairs={{0,96},{32,0},{64,32},{96,64},{1,97},{33,1},{65,33},{97,65},{2,98}... | collective-permute-start | bytes 4616 | tf_op jit(solution)/shard_map/ppermute | solution.py:490

commit v3 on v2

--- a/solution.py
+++ b/solution.py
@@ -12,7 +12,7 @@
 RUN = 16
 PITCH = 52
 OUT_PITCH = 50
-OWNERS = 4
+OWNERS = 2
 F32 = jnp.float32
 BF16 = jnp.bfloat16
 
@@ -36,8 +36,14 @@
     return terms[0]
 
 
-def quarter_of(by):
-    return lax.rem(lax.axis_index("seq") + (by + OWNERS), OWNERS)
+def position():
+    place = lax.axis_index("seq")
+    return lax.div(place, 8), lax.rem(lax.div(place, 4), 2), lax.rem(lax.div(place, 2), 2), lax.rem(place, 2)
+
+
+def half_of(by):
+    _, _, pair, odd = position()
+    return lax.rem(pair + odd + by, 2)
 
 
 def lanes_at(first):
@@ -85,31 +91,30 @@
     lax.fori_loop(0, key_ref.shape[1] // LANES, tile, 0)
 
 
-def quarter_copies(by, sources, targets, sems, cuts):
-    width = targets[0].shape[1]
+def half_copies(by, sources, targets, sems, cuts, which):
+    width = sources[0].shape[1] // OWNERS
     step = width // cuts
     return [
         [
             pltpu.make_async_copy(
-                a.at[:, pl.ds(pl.multiple_of(quarter_of(by) * width + j * step, step), step)],
+                a.at[:, pl.ds(pl.multiple_of(half_of(by) * width + j * step, step), step)],
                 b.at[:, pl.ds(j * step, step)],
                 sems.at[s, j],
             )
             for s, (a, b) in enumerate(zip(sources, targets))
         ]
-        for j in range(cuts)
+        for j in which
     ]
 
 
-def far_ends_kernel(key_ref, value_ref, rates_ref, *refs):
-    results, (key_held, value_held, signal_ref, rates_here, sems, sem) = refs[:9], refs[9:]
-    width = key_held.shape[2]
-    cuts = 2
+def far_end_kernel(key_ref, value_ref, rates_ref, end_ref, sent_ref, ends_ref, key_own, value_own,
+                   key_held, value_held, signal_ref, rates_here, sems, sem):
+    width = key_held.shape[1]
+    cuts = 4
     step = width // cuts
     sources = (key_ref, value_ref)
-    pieces = []
-    for by in (1, 2, 3):
-        pieces += quarter_copies(by, sources, (key_held.at[by - 1], value_held.at[by - 1]), sems.at[by - 1], cuts)
+    pieces = half_copies(1, sources, (key_held, value_held), sems.at[0], cuts, range(cuts))
+    pieces += half_copies(0, sources, (key_own, value_own), sems.at[1], cuts, range(key_own.shape[1] // step))
     rates_copy = pltpu.make_async_copy(rates_ref, rates_here, sem)
     rates_copy.start()
     ahead = 3
@@ -117,17 +122,18 @@
         for c in pieces[i]:
             c.start()
     rates_copy.wait()
-    for i in range(3 * cuts):
+    for i in range(cuts):
         for c in pieces[i]:
             c.wait()
         if i + ahead < len(pieces):
             for c in pieces[i + ahead]:
                 c.start()
-        by, at = i // cuts, i % cuts * step
-        end_ref, sent_ref, ends_ref = results[3 * by : 3 * by + 3]
-        part = pl.ds(at, step)
-        end_of_piece(key_held.at[by, :, part], value_held.at[by, :, part], rates_here,
-                     quarter_of(by + 1) * width + at, signal_ref, sent_ref, ends_ref, end_ref, at)
+        part = pl.ds(i * step, step)
+        end_of_piece(key_held.at[:, part], value_held.at[:, part], rates_here, half_of(1) * width + i * step,
+                     signal_ref, sent_ref, ends_ref, end_ref, i * step)
+    for p in pieces[cuts:]:
+        for c in p:
+            c.wait()
 
 
 def end_shapes(tokens, width):
@@ -139,107 +145,114 @@
     return [pltpu.with_memory_space_constraint(a, pltpu.HBM) for a in arrays]
 
 
-def far_ends(key, value, rates):
+def far_end(key, value, rates):
     tokens, channels = key.shape
     width = channels // OWNERS
     return pl.pallas_call(
-        far_ends_kernel,
+        far_end_kernel,
         in_specs=[IN_HBM] * 3,
-        out_specs=[IN_VMEM] * 9,
-        out_shape=end_shapes(tokens, width) * 3,
+        out_specs=[IN_VMEM] * 5,
+        out_shape=end_shapes(tokens, width) + [jax.ShapeDtypeStruct((tokens, width // 2), BF16)] * 2,
         scratch_shapes=[
-            pltpu.VMEM((3, tokens, width), BF16),
-            pltpu.VMEM((3, tokens, width), BF16),
+            pltpu.VMEM((tokens, width), BF16),
+            pltpu.VMEM((tokens, width), BF16),
             pltpu.VMEM((SUB * PITCH, LANES), F32),
             pltpu.VMEM((ORDER, channels), F32),
-            pltpu.SemaphoreType.DMA((3, 2, 2)),
+            pltpu.SemaphoreType.DMA((2, 2, 4)),
             pltpu.SemaphoreType.DMA(()),
         ],
         compiler_params=PARAMS,
-        cost_estimate=cost(4.6),
-        name="far_ends",
+        cost_estimate=cost(3.4),
+        name="far_end",
     )(*in_hbm(key, value, rates))
 
 
-ENTRIES = 9
-
-
-def position():
-    place = lax.axis_index("seq")
-    return lax.div(place, 8), lax.rem(lax.div(place, 4), 2), lax.rem(place, 4)
-
-
-def own_end_kernel(key_ref, value_ref, rates_ref, end_ref, sent_ref, ends_ref, tables_ref,
+ENTRIES = 7
+
+
+def own_end_kernel(key_first, value_first, key_ref, value_ref, rates_ref, end_ref, sent_ref, ends_ref, tables_ref,
                    key_held, value_held, signal_ref, sems):
     tokens, width = key_held.shape
-    x, z, _ = position()
-    first = quarter_of(0) * width
-    (copies,) = quarter_copies(0, (key_ref, value_ref), (key_held, value_held), sems, 1)
-    for c in copies:
-        c.start()
+    x, z, _, _ = position()
+    first = half_of(0) * width
+    cuts = 4
+    step = width // cuts
+    brought = key_first.shape[1] // step
+    pieces = half_copies(0, (key_ref, value_ref), (key_held, value_held), sems, cuts, range(brought, cuts))
+    for p in pieces:
+        for c in p:
+            c.start()
 
     def table(t, _):
         here = lanes_at(t * LANES)
         rates = rates_ref[:, lanes_at(first + t * LANES)] * float(-tokens)
-        tables_ref[0, :, here] = jnp.zeros((ORDER, LANES), F32)
-        for m in range(1, 6):
-            tables_ref[m, :, here] = jnp.exp(rates * float(m - 1))
+        tables_ref[0, :, here] = jnp.exp(rates)
+        tables_ref[1, :, here] = jnp.exp(rates * 2.0)
+        tables_ref[2, :, here] = jnp.exp(rates * (4 * (1 - z)).astype(F32))
+        tables_ref[3, :, here] = jnp.exp(rates * (4 * z).astype(F32))
         for k in (1, 2, 3):
             spans = (4 * z + 8 * (k - 1)).astype(F32)
-            tables_ref[5 + k, :, here] = jnp.exp(rates * spans) * (x >= k).astype(F32)
+            tables_ref[3 + k, :, here] = jnp.exp(rates * spans) * (x >= k).astype(F32)
         return 0
 
     lax.fori_loop(0, width // LANES, table, 0)
-    for c in copies:
-        c.wait()
-    end_of_piece(key_held, value_held, rates_ref, first, signal_ref, sent_ref, ends_ref, end_ref, 0)
-
-
-def own_end(key, value, rates):
+    for i in range(cuts):
+        part = pl.ds(i * step, step)
+        if i < brought:
+            key, value = key_first, value_first
+        else:
+            key, value = key_held, value_held
+            for c in pieces[i - brought]:
+                c.wait()
+        end_of_piece(key.at[:, part], value.at[:, part], rates_ref, first + i * step,
+                     signal_ref, sent_ref, ends_ref, end_ref, i * step)
+
+
+def own_end(key_first, value_first, key, value, rates):
     tokens, channels = key.shape
     width = channels // OWNERS
     return pl.pallas_call(
         own_end_kernel,
-        in_specs=[IN_HBM, IN_HBM, IN_VMEM],
+        in_specs=[IN_VMEM, IN_VMEM, IN_HBM, IN_HBM, IN_VMEM],
         out_specs=[IN_VMEM] * 4,
         out_shape=end_shapes(tokens, width) + [jax.ShapeDtypeStruct((ENTRIES, ORDER, width), F32)],
         scratch_shapes=[
             pltpu.VMEM((tokens, width), BF16),
             pltpu.VMEM((tokens, width), BF16),
             pltpu.VMEM((SUB * PITCH, LANES), F32),
-            pltpu.SemaphoreType.DMA((2, 1)),
+            pltpu.SemaphoreType.DMA((2, 4)),
         ],
         compiler_params=PARAMS,
-        cost_estimate=cost(2.3),
+        cost_estimate=cost(2.7),
         name="own_end",
-    )(*in_hbm(key, value), rates)
-
-
-def sender(y, by):
-    return lax.rem(y + (OWNERS - by), OWNERS)
-
-
-def row_kernel(e0, e1, e2, e3, tables_ref, row_ref):
-    _, _, y = position()
-    row_ref[...] = add_up([tables_ref[4 - sender(y, k)] * e[...] for k, e in enumerate((e0, e1, e2, e3))])
-
-
-def plane_kernel(row_ref, other_ref, tables_ref, plane_ref):
-    _, z, _ = position()
-    plane_ref[...] = tables_ref[5 - 4 * z] * row_ref[...] + tables_ref[1 + 4 * z] * other_ref[...]
-
-
-def states_kernel(e0, e1, e2, e3, other_ref, p1, p2, p3, tables_ref, *states):
-    _, z, y = position()
-    head = other_ref[...] * z.astype(F32) + add_up(
-        [tables_ref[5 + k] * p[...] for k, p in ((1, p1), (2, p2), (3, p3))]
-    )
-    for j, state_ref in enumerate(states):
-        target = lax.rem(y + j, OWNERS)
-        before = [
-            tables_ref[jnp.maximum(target - sender(y, k), 0)] * e[...] for k, e in enumerate((e0, e1, e2, e3))
-        ]
-        state_ref[...] = add_up(before) + tables_ref[1 + target] * head
+    )(key_first, value_first, *in_hbm(key, value), rates)
+
+
+def pair_kernel(own_ref, got_ref, tables_ref, pair_ref):
+    _, _, _, odd = position()
+    own, got = own_ref[...], got_ref[...]
+    earlier, later = jnp.where(odd == 1, got, own), jnp.where(odd == 1, own, got)
+    pair_ref[...] = tables_ref[0] * earlier + later
+
+
+def row_kernel(own_ref, got_ref, tables_ref, row_ref):
+    _, _, pair, _ = position()
+    own, got = own_ref[...], got_ref[...]
+    earlier, later = jnp.where(pair == 1, got, own), jnp.where(pair == 1, own, got)
+    row_ref[...] = tables_ref[1] * earlier + later
+
+
+def plane_kernel(own_ref, got_ref, tables_ref, plane_ref):
+    plane_ref[...] = tables_ref[2] * own_ref[...] + tables_ref[3] * got_ref[...]
+
+
+def states_kernel(own_ref, got_ref, pair_ref, half_ref, p1, p2, p3, tables_ref, mine_ref, other_ref):
+    _, z, pair, odd = position()
+    head = half_ref[...] * z.astype(F32) + add_up([tables_ref[3 + k] * p[...] for k, p in ((1, p1), (2, p2), (3, p3))])
+    earlier = jnp.where(pair == 1, tables_ref[1] * head + pair_ref[...], head)
+    later = tables_ref[0] * earlier + jnp.where(odd == 1, got_ref[...], own_ref[...])
+    mine_ref[...] = jnp.where(odd == 1, later, earlier)
+    other_ref[...] = jnp.where(odd == 1, earlier, later)
 
 
 def small(kernel, count, *args):
@@ -262,14 +275,14 @@
     place = lax.broadcasted_iota(jnp.int32, (SUB, LANES), 0).astype(F32)
 
     def copy(t):
-        there = lanes_at(quarter_of(-by) * width + t * LANES)
+        there = lanes_at(half_of(by) * width + t * LANES)
         return pltpu.make_async_copy(gate_ref.at[:, there], gate_held.at[t], sems.at[t])
 
     for t in range(width // LANES):
         copy(t).start()
 
     def tile(t, _):
-        lanes = lanes_at(quarter_of(-by) * width + t * LANES)
+        lanes = lanes_at(half_of(by) * width + t * LANES)
         here = lanes_at(t * LANES)
         rates = rates_ref[:, lanes]
         residues = residues_ref[:, lanes]
@@ -345,7 +358,7 @@
             pltpu.SemaphoreType.DMA((width // LANES,)),
         ],
         compiler_params=PARAMS,
-        cost_estimate=cost(1.4),
+        cost_estimate=cost(2.6),
         name="local_part",
     )(sent, ends, gate, rates, residues, skip)
 
@@ -363,7 +376,7 @@
 
     def tile(t, _):
         here = lanes_at(t * LANES)
-        step = spread(jnp.exp(-rates_ref[:, lanes_at(quarter_of(-by) * width + t * LANES)]))
+        step = spread(jnp.exp(-rates_ref[:, lanes_at(half_of(by) * width + t * LANES)]))
         state = state_ref[:, here]
         terms = []
         for n in range(ORDER):
@@ -408,12 +421,12 @@
         out_shape=outs,
         scratch_shapes=scratch,
         compiler_params=PARAMS,
-        cost_estimate=cost(1.1),
+        cost_estimate=cost(2.1),
         name="mix",
     )(*args)
 
 
-def norm_kernel(g0, g1, g2, g3, gain_ref, p0_ref, p1_ref, p2_ref, p3_ref, out_ref, runs_ref, scale_ref, held, sems):
+def norm_kernel(g0, g1, gain_ref, p0_ref, p1_ref, p2_ref, p3_ref, out_ref, runs_ref, scale_ref, held, sems):
     tiles, tokens = g0.shape[0], scale_ref.shape[0]
     width = tiles * LANES
     span = tokens // SUB
@@ -431,8 +444,10 @@
         scale_ref[pl.ds(i, SUB, stride=span), :] = runs_ref[pl.ds(i * SUB, SUB), :]
 
     copies = []
-    for by, gated_ref in enumerate((g0, g1, g2, g3)):
-        first = quarter_of(-by) * width
+    cuts = sems.shape[1]
+    step = width // cuts
+    for by, gated_ref in enumerate((g0, g1)):
+        first = half_of(by) * width
 
         def tile(t, _):
             here = lanes_at(t * LANES)
@@ -443,12 +458,15 @@
                 held[by, rows, here] = (gated * scale_ref[rows, :] * gain).astype(BF16)
             return 0
 
-        lax.fori_loop(0, width // LANES, tile, 0)
-        copy = pltpu.make_async_copy(
-            held.at[by], out_ref.at[:, pl.ds(pl.multiple_of(first, width), width)], sems.at[by]
-        )
-        copy.start()
-        copies.append(copy)
+        for cut in range(cuts):
+            lax.fori_loop(cut * tiles // cuts, (cut + 1) * tiles // cuts, tile, 0)
+            copy = pltpu.make_async_copy(
+                held.at[by, :, pl.ds(cut * step, step)],
+                out_ref.at[:, pl.ds(pl.multiple_of(first + cut * step, step), step)],
+                sems.at[by, cut],
+            )
+            copy.start()
+            copies.append(copy)
     for copy in copies:
         copy.wait()
 
@@ -459,14 +477,14 @@
     channels = width * OWNERS
     return pl.pallas_call(
         norm_kernel,
-        in_specs=[IN_VMEM] * 9,
+        in_specs=[IN_VMEM] * 7,
         out_specs=IN_HBM,
         out_shape=jax.ShapeDtypeStruct((tokens, channels), BF16),
         scratch_shapes=[
             pltpu.VMEM((tokens, LANES), F32),
             pltpu.VMEM((tokens, LANES), F32),
             pltpu.VMEM((OWNERS, tokens, width), BF16),
-            pltpu.SemaphoreType.DMA((OWNERS,)),
+            pltpu.SemaphoreType.DMA((OWNERS, 4)),
         ],
         compiler_params=PARAMS,
         cost_estimate=cost(1.7),
@@ -474,12 +492,8 @@
     )(*gated, gain, *powers)
 
 
-def over_y(x, by):
-    return lax.ppermute(x, "seq", [(i, i // 4 * 4 + (i + by) % 4) for i in range(32)])
-
-
-def over_z(x):
-    return lax.ppermute(x, "seq", [(i, i ^ 4) for i in range(32)])
+def with_partner(x, by):
+    return lax.ppermute(x, "seq", [(i, i ^ by) for i in range(32)])
 
 
 def over_x(x, by):
@@ -493,47 +507,33 @@
 def body(gate, key, value, rates, residues, skip_gain, norm_gain):
     skip = skip_gain[None, :]
     tie = lax.optimization_barrier
-    parts = [None] * OWNERS
-
-    def local(by, rates):
-        parts[by] = local_part(by, sent[-by], inner[-by], gate, rates, residues, skip)
-
-    ends, sent, inner = ([None] * OWNERS for _ in range(3))
-    outs = far_ends(key, value, rates)
-    ends[1:], sent[1:], inner[1:] = outs[0::3], outs[1::3], outs[2::3]
-    ends[1], rates0 = tie((ends[1], rates))
-    for k in (2, 1, 3):
-        ends[k] = over_y(ends[k], k)
-    ends[0], sent[0], inner[0], tables = own_end(key, value, rates0)
-    (row,) = small(row_kernel, 1, *ends, tables)
-
-    row, rates1 = tie((row, rates))
-    other = over_z(row)
-    for by in (1, 2, 3):
-        local(by, rates1)
-    other, *parts[1:] = tie((other, *parts[1:]))
-    (plane,) = small(plane_kernel, 1, row, other, tables)
-
-    plane, rates2 = tie((plane, rates))
-    got = {k: over_x(plane, k) for k in (2, 1, 3)}
-    got = [got[k] for k in (1, 2, 3)]
-    local(0, rates2)
-    got[0], parts[0] = tie((got[0], parts[0]))
-    states = list(small(states_kernel, OWNERS, *ends, other, *got, tables))
-
-    for k in (2, 1, 3):
-        states[k] = over_y(states[k], k)
-    gated, sums = [], None
-    for by in range(OWNERS):
-        first, second = mix(by, by == OWNERS - 1, parts[by], states[by], rates, sums)
-        if by < OWNERS - 1:
-            gated.append(first)
-            sums = second
-        else:
-            gated.append(second)
-            power = first
+
+    far, far_sent, far_ends, *first = far_end(key, value, rates)
+    far, rates0 = tie((far, rates))
+    got = with_partner(far, 1)
+    own, own_sent, own_ends, tables = own_end(*first, key, value, rates0)
+    (pair,) = small(pair_kernel, 1, own, got, tables)
+
+    pair, rates1 = tie((pair, rates))
+    other_pair = with_partner(pair, 3)
+    far_part = local_part(1, far_sent, far_ends, gate, rates1, residues, skip)
+    other_pair, *far_part = tie((other_pair, *far_part))
+    (row,) = small(row_kernel, 1, pair, other_pair, tables)
+
+    row, rates2 = tie((row, rates))
+    other_row = with_partner(row, 4)
+    own_part = local_part(0, own_sent, own_ends, gate, rates2, residues, skip)
+    other_row, *own_part = tie((other_row, *own_part))
+    (plane,) = small(plane_kernel, 1, row, other_row, tables)
+
+    planes = [over_x(plane, k) for k in (1, 2, 3)]
+    mine, theirs = small(states_kernel, 2, own, got, other_pair, other_row, *planes, tables)
+
+    theirs = with_partner(theirs, 1)
+    own_gated, sums = mix(0, False, own_part, mine, rates, None)
+    power, far_gated = mix(1, True, far_part, theirs, rates, sums)
     powers = [power] + [over_ch(power, k) for k in (1, 2, 3)]
-    return norm(gated, norm_gain[None, :], powers)
+    return norm([own_gated, far_gated], norm_gain[None, :], powers)
 
 
 def solution(mesh):

time: 46.8 us -> 43.8 us (0.936)
  starting transfers between devices: 24 us -> 19.3 us
  waiting for transfers between devices: 3.62 us -> 6.05 us
  Pallas kernels: 18.8 us -> 18.1 us
    ppermute x7 -> x4, starting transfers between devices: 12.6 us -> 8.28 us  [with_partner(): return lax.ppermute(x, 'seq', [(i, i ^ by) for i in range(32)])]
    ppermute x3, waiting for transfers between devices: 0.6 us -> 2.26 us  [over_x(): return lax.ppermute(x, 'seq', [(i, (i + 8 * by) % 32) for i in range(32)])]
    ppermute x7 -> x4, waiting for transfers between devices: 0.02 us -> 0.8 us  [with_partner(): return lax.ppermute(x, 'seq', [(i, i ^ by) for i in range(32)])]
    pallas_call x3, Pallas kernels: 8.91 us -> 8.22 us  [the longest x1 3.79 us: far_end(): pl.pallas_call(far_end_kernel, in_specs=[IN_HBM] * 3, out_specs=[IN_VMEM]...]
    pallas_call x4 -> x2, Pallas kernels: 5.16 us -> 5.25 us  [local_part(): pl.pallas_call(lambda *refs: local_kernel(by, *refs), in_specs=[IN_VMEM,...]
    pallas_call x4 -> x2, Pallas kernels: 4.55 us -> 4.55 us  [mix(): pl.pallas_call(lambda *refs: mix_kernel(by, last, *refs), in_specs=[IN_VM...]
  transfers between devices with their start and end apart: 13 -> 10, of which waited for: 3 -> 6; matrix products, arithmetic and copies ran while one was open for 0% -> 0% of each run, Pallas kernels for 23% -> 23%
where the time goes in v3:
time: 43.8 us; the launch traced here: 43.7 us
  starting transfers between devices  19.3 us (44%)
  Pallas kernels  18.1 us (41%)
  waiting for transfers between devices  6.05 us (14%)
    ppermute x4, starting transfers between devices, with_partner(): return lax.ppermute(x, 'seq', [(i, i ^ by) for i in range(32)])  8.28 us
    ppermute x3, starting transfers between devices, over_ch(): return lax.ppermute(x, 'ch', [(i, (i + by) % 4) for i in range(4)])  6.18 us
    pallas_call x2, Pallas kernels, local_part(): pl.pallas_call(lambda *refs: local_kernel(by, *refs), in_specs=[IN_VMEM,...  5.25 us
    ppermute x3, starting transfers between devices, over_x(): return lax.ppermute(x, 'seq', [(i, (i + 8 * by) % 32) for i in range(32)])  4.88 us
    pallas_call x2, Pallas kernels, mix(): pl.pallas_call(lambda *refs: mix_kernel(by, last, *refs), in_specs=[IN_VM...  4.55 us
    pallas_call x1, Pallas kernels, far_end(): pl.pallas_call(far_end_kernel, in_specs=[IN_HBM] * 3, out_specs=[IN_VMEM]...  3.79 us
    ppermute x3, waiting for transfers between devices, over_ch(): return lax.ppermute(x, 'ch', [(i, (i + by) % 4) for i in range(4)])  3 us
    pallas_call x1, Pallas kernels, own_end(): pl.pallas_call(own_end_kernel, in_specs=[IN_VMEM, IN_VMEM, IN_HBM, IN_HBM...  2.62 us
  transfers between devices with their start and end apart: 10, of which 6 were waited for; matrix products, arithmetic and copies ran while one was open for 0% of the time, Pallas kernels for 23%

profile of v3, /device:TPU:1, one launch (start us, length us, event | category | flops | bytes accessed | tf_op | source)
XLA Modules:
  0.0 43.7 jit_solution(5834281959888685487)
XLA Ops:
  0.0 3.8 %far_end.1 = (f32[16,1024]{1,0:T(8,128)S(1)}, f32[384,1024]{1,0:T(8,128)S(1)}, f32[384,1024]{1,0:T(8,128)S(1)}, bf16[384,512]{1,0:T(8,128)(2,1)S(1)}, bf16[384,512]{1,0:T(8,128)(2,1)S(1)}) custom-call(bf16[384,2048]{1,0:T(8,128)(2,1)} %key_ref.3, bf16[384,2048]{1,0:T(8,128)(2,1)} %value_ref.3, f32[16,2048]{1,0:T(8,128)} %refs_6_.3), custom_call_target="tpu_custom_call" | custom-call | flops 3910000128 | bytes 12546000 | tf_op jit(solution)/shard_map/far_end/pallas_call | solution.py:151
  3.8 2.2 %collective-permute-start = (f32[16,1024]{1,0:T(8,128)S(1)}, f32[16,1024]{1,0:T(8,128)S(1)}, u32[]{:S(2)}, u32[]{:S(2)}) collective-permute-start(f32[16,1024]{1,0:T(8,128)S(1)} %get-tuple-element.53), channel_id=1, source_target_pairs={{0,1},{1,0},{2,3},{3,2},{4,5},{5,4},{6,7},{7,6},{8,9},{9,8},{10,11... | collective-permute-start | bytes 196616 | tf_op jit(solution)/shard_map/ppermute | solution.py:496
  6.0 2.6 %own_end.1 = (f32[16,1024]{1,0:T(8,128)S(1)}, f32[384,1024]{1,0:T(8,128)S(1)}, f32[384,1024]{1,0:T(8,128)S(1)}, f32[7,16,1024]{2,1,0:T(8,128)S(1)}) custom-call(bf16[384,512]{1,0:T(8,128)(2,1)S(1)} %get-tuple-element.48.key_first, bf16[384,512]{1,0:T(8,128)(2,1)S(1)} %get-tuple-element.49.value_first, bf16[384,2048]{1,0:T(8,128)(2,1)} %key_ref.3, ...), custom_call_target="tpu_custom_call" | custom-call | flops 3104999936 | bytes 9963000 | tf_op jit(solution)/shard_map/own_end/pallas_call | solution.py:214
  8.6 0.0 collective-permute-done.got_ref
  8.7 2.0 %collective-permute-start.1 = (f32[16,1024]{1,0:T(8,128)S(1)}, f32[16,1024]{1,0:T(8,128)S(1)}, u32[]{:S(2)}, u32[]{:S(2)}) collective-permute-start(f32[16,1024]{1,0:T(8,128)S(1)} %pair_kernel.1.own_ref), channel_id=1, source_target_pairs={{0,3},{1,2},{2,1},{3,0},{4,7},{5,6},{6,5},{7,4},{8,11},{9,10},{10,... | collective-permute-start | bytes 196616 | tf_op jit(solution)/shard_map/ppermute | solution.py:496
  10.7 2.6 %local_part.2 = (f32[384,1024]{1,0:T(8,128)S(1)}, f32[384,1024]{1,0:T(8,128)S(1)}, f32[128,1024]{1,0:T(8,128)S(1)}, f32[128,1024]{1,0:T(8,128)S(1)}, f32[256,1024]{1,0:T(8,128)S(1)}) custom-call(f32[384,1024]{1,0:T(8,128)S(1)} %get-tuple-element.56.refs_0_, f32[384,1024]{1,0:T(8,128)S(1)} %get-tuple-element.57.refs_1_, bf16[384,2048]{1,0:T(8,128)(2,1)} %refs_2_.3, ...), custom_call_target="tpu_custom_call" | custom-call | flops 2990000128 | bytes 9594000 | tf_op jit(solution)/shard_map/local_part/pallas_call | solution.py:350
  13.4 3.7 %collective-permute-start.2 = (f32[16,1024]{1,0:T(8,128)S(1)}, f32[16,1024]{1,0:T(8,128)S(1)}, u32[]{:S(2)}, u32[]{:S(2)}) collective-permute-start(f32[16,1024]{1,0:T(8,128)S(1)} %row_kernel.1.own_ref), channel_id=1, source_target_pairs={{0,4},{1,5},{2,6},{3,7},{4,0},{5,1},{6,2},{7,3},{8,12},{9,13},{10,... | collective-permute-start | bytes 196616 | tf_op jit(solution)/shard_map/ppermute | solution.py:496
  17.0 2.6 %local_part.3 = (f32[384,1024]{1,0:T(8,128)S(1)}, f32[384,1024]{1,0:T(8,128)S(1)}, f32[128,1024]{1,0:T(8,128)S(1)}, f32[128,1024]{1,0:T(8,128)S(1)}, f32[256,1024]{1,0:T(8,128)S(1)}) custom-call(f32[384,1024]{1,0:T(8,128)S(1)} %get-tuple-element.66.refs_0_, f32[384,1024]{1,0:T(8,128)S(1)} %get-tuple-element.67.refs_1_, bf16[384,2048]{1,0:T(8,128)(2,1)} %refs_2_.3, ...), custom_call_target="tpu_custom_call" | custom-call | flops 2990000128 | bytes 9594000 | tf_op jit(solution)/shard_map/local_part/pallas_call | solution.py:350
  19.7 1.3 %collective-permute-start.3 = (f32[16,1024]{1,0:T(8,128)S(1)}, f32[16,1024]{1,0:T(8,128)S(1)}, u32[]{:S(2)}, u32[]{:S(2)}) collective-permute-start(f32[16,1024]{1,0:T(8,128)S(1)} %plane_kernel.1), channel_id=1, source_target_pairs={{0,8},{1,9},{2,10},{3,11},{4,12},{5,13},{6,14},{7,15},{8,16},{9,17... | collective-permute-start | bytes 196616 | tf_op jit(solution)/shard_map/ppermute | solution.py:500
  21.0 2.5 %collective-permute-start.4 = (f32[16,1024]{1,0:T(8,128)S(1)}, f32[16,1024]{1,0:T(8,128)S(1)}, u32[]{:S(2)}, u32[]{:S(2)}) collective-permute-start(f32[16,1024]{1,0:T(8,128)S(1)} %plane_kernel.1), channel_id=1, source_target_pairs={{0,16},{1,17},{2,18},{3,19},{4,20},{5,21},{6,22},{7,23},{8,24},{9,... | collective-permute-start | bytes 196616 | tf_op jit(solution)/shard_map/ppermute | solution.py:500
  23.4 1.2 %collective-permute-start.5 = (f32[16,1024]{1,0:T(8,128)S(1)}, f32[16,1024]{1,0:T(8,128)S(1)}, u32[]{:S(2)}, u32[]{:S(2)}) collective-permute-start(f32[16,1024]{1,0:T(8,128)S(1)} %plane_kernel.1), channel_id=1, source_target_pairs={{0,24},{1,25},{2,26},{3,27},{4,28},{5,29},{6,30},{7,31},{8,0},{9,1... | collective-permute-start | bytes 196616 | tf_op jit(solution)/shard_map/ppermute | solution.py:500
  24.6 1.2 %collective-permute-done.4.p2 = f32[16,1024]{1,0:T(8,128)S(1)} collective-permute-done((f32[16,1024]{1,0:T(8,128)S(1)}, f32[16,1024]{1,0:T(8,128)S(1)}, u32[]{:S(2)}, u32[]{:S(2)}) %collective-permute-start.4) | collective-permute-done | bytes 65568 | tf_op jit(solution)/shard_map/ppermute | solution.py:500
  25.8 1.1 %collective-permute-done.5.p3 = f32[16,1024]{1,0:T(8,128)S(1)} collective-permute-done((f32[16,1024]{1,0:T(8,128)S(1)}, f32[16,1024]{1,0:T(8,128)S(1)}, u32[]{:S(2)}, u32[]{:S(2)}) %collective-permute-start.5) | collective-permute-done | bytes 65568 | tf_op jit(solution)/shard_map/ppermute | solution.py:500
  26.8 0.1 states_kernel.1
  26.9 0.4 collective-permute-start.6
  27.3 2.1 %mix.2 = (f32[8,400,128]{2,1,0:T(8,128)S(1)}, f32[384,128]{1,0:T(8,128)S(1)}) custom-call(f32[384,1024]{1,0:T(8,128)S(1)} %get-tuple-element.74.refs_0_, f32[384,1024]{1,0:T(8,128)S(1)} %get-tuple-element.75.refs_1_, f32[128,1024]{1,0:T(8,128)S(1)} %get-tuple-element.76.refs_2_, f32[128,1024]{1,0:T(8,128)S(1)} %get-tuple-element.77.refs_3_, ...), custom_call_target="tpu_custom_call" | custom-call | flops 2415000064 | bytes 7749000 | tf_op jit(solution)/shard_map/mix/pallas_call | solution.py:417
  29.5 0.8 %collective-permute-done.6.refs_5_ = f32[16,1024]{1,0:T(8,128)S(1)} collective-permute-done((f32[16,1024]{1,0:T(8,128)S(1)}, f32[16,1024]{1,0:T(8,128)S(1)}, u32[]{:S(2)}, u32[]{:S(2)}) %collective-permute-start.6) | collective-permute-done | bytes 65568 | tf_op jit(solution)/shard_map/ppermute | solution.py:496
  30.2 2.4 %mix.3 = (f32[1,384]{1,0:T(1,128)S(1)}, f32[8,400,128]{2,1,0:T(8,128)S(1)}) custom-call(f32[384,1024]{1,0:T(8,128)S(1)} %get-tuple-element.82.refs_0_, f32[384,1024]{1,0:T(8,128)S(1)} %get-tuple-element.83.refs_1_, f32[128,1024]{1,0:T(8,128)S(1)} %get-tuple-element.84.refs_2_, f32[128,1024]{1,0:T(8,128)S(1)} %get-tuple-element.85.refs_3_, ...), custom_call_target="tpu_custom_call" | custom-call | flops 2415000064 | bytes 7749000 | tf_op jit(solution)/shard_map/mix/pallas_call | solution.py:417
  32.7 5.6 %collective-permute-start.7 = (f32[1,384]{1,0:T(1,128)S(1)}, f32[1,384]{1,0:T(1,128)S(1)}, u32[]{:S(2)}, u32[]{:S(2)}) collective-permute-start(f32[1,384]{1,0:T(1,128)S(1)} %get-tuple-element.90.p0_ref), channel_id=1, source_target_pairs={{0,32},{32,64},{64,96},{96,0},{1,33},{33,65},{65,97},{97,1},{2,34}... | collective-permute-start | bytes 4616 | tf_op jit(solution)/shard_map/ppermute | solution.py:504
  38.3 0.6 %collective-permute-start.8 = (f32[1,384]{1,0:T(1,128)S(1)}, f32[1,384]{1,0:T(1,128)S(1)}, u32[]{:S(2)}, u32[]{:S(2)}) collective-permute-start(f32[1,384]{1,0:T(1,128)S(1)} %get-tuple-element.90.p0_ref), channel_id=1, source_target_pairs={{0,64},{32,96},{64,0},{96,32},{1,65},{33,97},{65,1},{97,33},{2,66}... | collective-permute-start | bytes 4616 | tf_op jit(solution)/shard_map/ppermute | solution.py:504
  38.8 0.1 collective-permute-done.7.p1_ref
  39.0 1.7 %collective-permute-done.8.p2_ref = f32[1,384]{1,0:T(1,128)S(1)} collective-permute-done((f32[1,384]{1,0:T(1,128)S(1)}, f32[1,384]{1,0:T(1,128)S(1)}, u32[]{:S(2)}, u32[]{:S(2)}) %collective-permute-start.8) | collective-permute-done | bytes 1568 | tf_op jit(solution)/shard_map/ppermute | solution.py:504
  40.7 1.1 %collective-permute-done.9.p3_ref = f32[1,384]{1,0:T(1,128)S(1)} collective-permute-done((f32[1,384]{1,0:T(1,128)S(1)}, f32[1,384]{1,0:T(1,128)S(1)}, u32[]{:S(2)}, u32[]{:S(2)}) %collective-permute-start.9) | collective-permute-done | bytes 1568 | tf_op jit(solution)/shard_map/ppermute | solution.py:504
  41.9 1.8 %norm.1 = bf16[384,2048]{1,0:T(8,128)(2,1)} custom-call(f32[8,400,128]{2,1,0:T(8,128)S(1)} %get-tuple-element.81.g0, f32[8,400,128]{2,1,0:T(8,128)S(1)} %get-tuple-element.89.g1, f32[1,2048]{1,0:T(1,128)S(1)} %bitcast.4, f32[1,384]{1,0:T(1,128)S(1)} %get-tuple-element.90.p0_ref, f32[1,384]{1,0:T(1,128)S(1)} %collective-permute-done.7.p1_ref, ...), custom_call_target="tpu_custom_call" | custom-call | flops 1955000064 | bytes 6273000 | tf_op jit(solution)/shard_map/norm/pallas_call | solution.py:478
  (15 shorter events, 0.1 us)
Async XLA Ops:
  0.0 6.0 %copy-start.1 = (f32[16,2048]{1,0:T(8,128)S(1)}, f32[16,2048]{1,0:T(8,128)}, u32[]{:S(2)}) copy-start(f32[16,2048]{1,0:T(8,128)} %refs_6_.3) | copy-start | bytes 393220
  3.8 4.8 %collective-permute-start = (f32[16,1024]{1,0:T(8,128)S(1)}, f32[16,1024]{1,0:T(8,128)S(1)}, u32[]{:S(2)}, u32[]{:S(2)}) collective-permute-start(f32[16,1024]{1,0:T(8,128)S(1)} %get-tuple-element.53), channel_id=1, source_target_pairs={{0,1},{1,0},{2,3},{3,2},{4,5},{5,4},{6,7},{7,6},{8,9},{9,8},{10,11... | collective-permute-start | bytes 196616 | tf_op jit(solution)/shard_map/ppermute | solution.py:496
  6.0 4.7 %copy-start = (f32[16,2048]{1,0:T(8,128)S(1)}, f32[16,2048]{1,0:T(8,128)}, u32[]{:S(2)}) copy-start(f32[16,2048]{1,0:T(8,128)} %refs_4_.3) | copy-start | bytes 393220
  6.0 4.7 %copy-start.2 = (f32[2048]{0:T(1024)S(1)}, f32[2048]{0:T(1024)}, u32[]{:S(2)}) copy-start(f32[2048]{0:T(1024)} %param.12) | copy-start | bytes 24580
  8.7 4.6 %collective-permute-start.1 = (f32[16,1024]{1,0:T(8,128)S(1)}, f32[16,1024]{1,0:T(8,128)S(1)}, u32[]{:S(2)}, u32[]{:S(2)}) collective-permute-start(f32[16,1024]{1,0:T(8,128)S(1)} %pair_kernel.1.own_ref), channel_id=1, source_target_pairs={{0,3},{1,2},{2,1},{3,0},{4,7},{5,6},{6,5},{7,4},{8,11},{9,10},{10,... | collective-permute-start | bytes 196616 | tf_op jit(solution)/shard_map/ppermute | solution.py:496
  13.4 6.3 %collective-permute-start.2 = (f32[16,1024]{1,0:T(8,128)S(1)}, f32[16,1024]{1,0:T(8,128)S(1)}, u32[]{:S(2)}, u32[]{:S(2)}) collective-permute-start(f32[16,1024]{1,0:T(8,128)S(1)} %row_kernel.1.own_ref), channel_id=1, source_target_pairs={{0,4},{1,5},{2,6},{3,7},{4,0},{5,1},{6,2},{7,3},{8,12},{9,13},{10,... | collective-permute-start | bytes 196616 | tf_op jit(solution)/shard_map/ppermute | solution.py:496
  19.7 4.9 %collective-permute-start.3 = (f32[16,1024]{1,0:T(8,128)S(1)}, f32[16,1024]{1,0:T(8,128)S(1)}, u32[]{:S(2)}, u32[]{:S(2)}) collective-permute-start(f32[16,1024]{1,0:T(8,128)S(1)} %plane_kernel.1), channel_id=1, source_target_pairs={{0,8},{1,9},{2,10},{3,11},{4,12},{5,13},{6,14},{7,15},{8,16},{9,17... | collective-permute-start | bytes 196616 | tf_op jit(solution)/shard_map/ppermute | solution.py:500
  21.0 4.8 %collective-permute-start.4 = (f32[16,1024]{1,0:T(8,128)S(1)}, f32[16,1024]{1,0:T(8,128)S(1)}, u32[]{:S(2)}, u32[]{:S(2)}) collective-permute-start(f32[16,1024]{1,0:T(8,128)S(1)} %plane_kernel.1), channel_id=1, source_target_pairs={{0,16},{1,17},{2,18},{3,19},{4,20},{5,21},{6,22},{7,23},{8,24},{9,... | collective-permute-start | bytes 196616 | tf_op jit(solution)/shard_map/ppermute | solution.py:500
  23.4 3.4 %collective-permute-start.5 = (f32[16,1024]{1,0:T(8,128)S(1)}, f32[16,1024]{1,0:T(8,128)S(1)}, u32[]{:S(2)}, u32[]{:S(2)}) collective-permute-start(f32[16,1024]{1,0:T(8,128)S(1)} %plane_kernel.1), channel_id=1, source_target_pairs={{0,24},{1,25},{2,26},{3,27},{4,28},{5,29},{6,30},{7,31},{8,0},{9,1... | collective-permute-start | bytes 196616 | tf_op jit(solution)/shard_map/ppermute | solution.py:500
  26.9 3.3 %collective-permute-start.6 = (f32[16,1024]{1,0:T(8,128)S(1)}, f32[16,1024]{1,0:T(8,128)S(1)}, u32[]{:S(2)}, u32[]{:S(2)}) collective-permute-start(f32[16,1024]{1,0:T(8,128)S(1)} %get-tuple-element.87), channel_id=1, source_target_pairs={{0,1},{1,0},{2,3},{3,2},{4,5},{5,4},{6,7},{7,6},{8,9},{9,8},{10,11... | collective-permute-start | bytes 196616 | tf_op jit(solution)/shard_map/ppermute | solution.py:496
  30.2 11.6 %copy-start.3 = (f32[2048]{0:T(1024)S(1)}, f32[2048]{0:T(1024)}, u32[]{:S(2)}) copy-start(f32[2048]{0:T(1024)} %param.13) | copy-start | bytes 24580
  32.7 6.3 %collective-permute-start.7 = (f32[1,384]{1,0:T(1,128)S(1)}, f32[1,384]{1,0:T(1,128)S(1)}, u32[]{:S(2)}, u32[]{:S(2)}) collective-permute-start(f32[1,384]{1,0:T(1,128)S(1)} %get-tuple-element.90.p0_ref), channel_id=1, source_target_pairs={{0,32},{32,64},{64,96},{96,0},{1,33},{33,65},{65,97},{97,1},{2,34}... | collective-permute-start | bytes 4616 | tf_op jit(solution)/shard_map/ppermute | solution.py:504
  38.3 2.5 %collective-permute-start.8 = (f32[1,384]{1,0:T(1,128)S(1)}, f32[1,384]{1,0:T(1,128)S(1)}, u32[]{:S(2)}, u32[]{:S(2)}) collective-permute-start(f32[1,384]{1,0:T(1,128)S(1)} %get-tuple-element.90.p0_ref), channel_id=1, source_target_pairs={{0,64},{32,96},{64,0},{96,32},{1,65},{33,97},{65,1},{97,33},{2,66}... | collective-permute-start | bytes 4616 | tf_op jit(solution)/shard_map/ppermute | solution.py:504
  38.8 3.0 %collective-permute-start.9 = (f32[1,384]{1,0:T(1,128)S(1)}, f32[1,384]{1,0:T(1,128)S(1)}, u32[]{:S(2)}, u32[]{:S(2)}) collective-permute-start(f32[1,384]{1,0:T(1,128)S(1)} %get-tuple-element.90.p0_ref), channel_id=1, source_target_pairs={{0,96},{32,0},{64,32},{96,64},{1,97},{33,1},{65,33},{97,65},{2,98}... | collective-permute-start | bytes 4616 | tf_op jit(solution)/shard_map/ppermute | solution.py:504

commit v4 on v3

--- a/solution.py
+++ b/solution.py
@@ -396,13 +396,9 @@
 
     lax.fori_loop(0, width // LANES, tile, 0)
     if last:
-        power_ref[...] = lax.dot_general(
-            jnp.ones((SUB, LANES), F32),
-            sums_ref[...],
-            (((1,), (1,)), ((), ())),
-            precision=lax.Precision.HIGHEST,
-            preferred_element_type=F32,
-        )[0:1, :]
+        for block in range(tokens // LANES):
+            rows = pl.ds(block * LANES, LANES)
+            power_ref[:, rows] = jnp.sum(jnp.transpose(sums_ref[rows, :]), axis=0, keepdims=True)
 
 
 def mix(by, last, part, state, rates, sums):
@@ -431,14 +427,7 @@
     width = tiles * LANES
     span = tokens // SUB
     total = (p0_ref[...] + p1_ref[...]) + (p2_ref[...] + p3_ref[...])
-    first = (lax.broadcasted_iota(jnp.int32, (SUB, LANES), 0) == 0).astype(F32)
-    power = lax.dot_general(
-        jnp.broadcast_to(total, (SUB, tokens)),
-        first,
-        (((0,), (0,)), ((), ())),
-        precision=lax.Precision.HIGHEST,
-        preferred_element_type=F32,
-    )
+    power = jnp.transpose(jnp.broadcast_to(total, (LANES, tokens)))
     runs_ref[...] = lax.rsqrt(power * (1.0 / D) + 1e-6)
     for i in range(span):
         scale_ref[pl.ds(i, SUB, stride=span), :] = runs_ref[pl.ds(i * SUB, SUB), :]
@@ -484,7 +473,7 @@
             pltpu.VMEM((tokens, LANES), F32),
             pltpu.VMEM((tokens, LANES), F32),
             pltpu.VMEM((OWNERS, tokens, width), BF16),
-            pltpu.SemaphoreType.DMA((OWNERS, 4)),
+            pltpu.SemaphoreType.DMA((OWNERS, 8)),
         ],
         compiler_params=PARAMS,
         cost_estimate=cost(1.7),
@@ -501,7 +490,7 @@
 
 
 def over_ch(x, by):
-    return lax.ppermute(x, "ch", [(i, (i + by) % 4) for i in range(4)])
+    return lax.ppermute(x, "ch", [(i, i ^ by) for i in range(4)])
 
 
 def body(gate, key, value, rates, residues, skip_gain, norm_gain):

time: 43.8 us -> 42.9 us (0.979)
  waiting for transfers between devices: 6.05 us -> 5.23 us
  starting transfers between devices: 19.3 us -> 19.8 us
    ppermute x3, waiting for transfers between devices: 3 us -> 2.17 us  [over_ch(): return lax.ppermute(x, 'ch', [(i, i ^ by) for i in range(4)])]
  transfers between devices with their start and end apart: 10 -> 10, of which waited for: 6 -> 5; matrix products, arithmetic and copies ran while one was open for 0% -> 0% of each run, Pallas kernels for 23% -> 23%
where the time goes in v4:
time: 42.9 us; the launch traced here: 42.8 us
  starting transfers between devices  19.8 us (46%)
  Pallas kernels  17.7 us (41%)
  waiting for transfers between devices  5.23 us (12%)
    ppermute x4, starting transfers between devices, with_partner(): return lax.ppermute(x, 'seq', [(i, i ^ by) for i in range(32)])  8.28 us
    ppermute x3, starting transfers between devices, over_ch(): return lax.ppermute(x, 'ch', [(i, i ^ by) for i in range(4)])  6.6 us
    pallas_call x2, Pallas kernels, local_part(): pl.pallas_call(lambda *refs: local_kernel(by, *refs), in_specs=[IN_VMEM,...  5.25 us
    ppermute x3, starting transfers between devices, over_x(): return lax.ppermute(x, 'seq', [(i, (i + 8 * by) % 32) for i in range(32)])  4.88 us
    pallas_call x2, Pallas kernels, mix(): pl.pallas_call(lambda *refs: mix_kernel(by, last, *refs), in_specs=[IN_VM...  4.4 us
    pallas_call x1, Pallas kernels, far_end(): pl.pallas_call(far_end_kernel, in_specs=[IN_HBM] * 3, out_specs=[IN_VMEM]...  3.79 us
    pallas_call x1, Pallas kernels, own_end(): pl.pallas_call(own_end_kernel, in_specs=[IN_VMEM, IN_VMEM, IN_HBM, IN_HBM...  2.62 us
    ppermute x3, waiting for transfers between devices, over_x(): return lax.ppermute(x, 'seq', [(i, (i + 8 * by) % 32) for i in range(32)])  2.26 us
  transfers between devices with their start and end apart: 10, of which 5 were waited for; matrix products, arithmetic and copies ran while one was open for 0% of the time, Pallas kernels for 23%

profile of v4, /device:TPU:1, one launch (start us, length us, event | category | flops | bytes accessed | tf_op | source)
XLA Modules:
  0.0 42.8 jit_solution(6718718206698537422)
XLA Ops:
  0.0 3.8 %far_end.1 = (f32[16,1024]{1,0:T(8,128)S(1)}, f32[384,1024]{1,0:T(8,128)S(1)}, f32[384,1024]{1,0:T(8,128)S(1)}, bf16[384,512]{1,0:T(8,128)(2,1)S(1)}, bf16[384,512]{1,0:T(8,128)(2,1)S(1)}) custom-call(bf16[384,2048]{1,0:T(8,128)(2,1)} %key_ref.3, bf16[384,2048]{1,0:T(8,128)(2,1)} %value_ref.3, f32[16,2048]{1,0:T(8,128)} %refs_6_.3), custom_call_target="tpu_custom_call" | custom-call | flops 3910000128 | bytes 12546000 | tf_op jit(solution)/shard_map/far_end/pallas_call | solution.py:151
  3.8 2.2 %collective-permute-start = (f32[16,1024]{1,0:T(8,128)S(1)}, f32[16,1024]{1,0:T(8,128)S(1)}, u32[]{:S(2)}, u32[]{:S(2)}) collective-permute-start(f32[16,1024]{1,0:T(8,128)S(1)} %get-tuple-element.53), channel_id=1, source_target_pairs={{0,1},{1,0},{2,3},{3,2},{4,5},{5,4},{6,7},{7,6},{8,9},{9,8},{10,11... | collective-permute-start | bytes 196616 | tf_op jit(solution)/shard_map/ppermute | solution.py:485
  6.0 2.6 %own_end.1 = (f32[16,1024]{1,0:T(8,128)S(1)}, f32[384,1024]{1,0:T(8,128)S(1)}, f32[384,1024]{1,0:T(8,128)S(1)}, f32[7,16,1024]{2,1,0:T(8,128)S(1)}) custom-call(bf16[384,512]{1,0:T(8,128)(2,1)S(1)} %get-tuple-element.48.key_first, bf16[384,512]{1,0:T(8,128)(2,1)S(1)} %get-tuple-element.49.value_first, bf16[384,2048]{1,0:T(8,128)(2,1)} %key_ref.3, ...), custom_call_target="tpu_custom_call" | custom-call | flops 3104999936 | bytes 9963000 | tf_op jit(solution)/shard_map/own_end/pallas_call | solution.py:214
  8.7 2.0 %collective-permute-start.1 = (f32[16,1024]{1,0:T(8,128)S(1)}, f32[16,1024]{1,0:T(8,128)S(1)}, u32[]{:S(2)}, u32[]{:S(2)}) collective-permute-start(f32[16,1024]{1,0:T(8,128)S(1)} %pair_kernel.1.own_ref), channel_id=1, source_target_pairs={{0,3},{1,2},{2,1},{3,0},{4,7},{5,6},{6,5},{7,4},{8,11},{9,10},{10,... | collective-permute-start | bytes 196616 | tf_op jit(solution)/shard_map/ppermute | solution.py:485
  10.7 2.6 %local_part.2 = (f32[384,1024]{1,0:T(8,128)S(1)}, f32[384,1024]{1,0:T(8,128)S(1)}, f32[128,1024]{1,0:T(8,128)S(1)}, f32[128,1024]{1,0:T(8,128)S(1)}, f32[256,1024]{1,0:T(8,128)S(1)}) custom-call(f32[384,1024]{1,0:T(8,128)S(1)} %get-tuple-element.56.refs_0_, f32[384,1024]{1,0:T(8,128)S(1)} %get-tuple-element.57.refs_1_, bf16[384,2048]{1,0:T(8,128)(2,1)} %refs_2_.3, ...), custom_call_target="tpu_custom_call" | custom-call | flops 2990000128 | bytes 9594000 | tf_op jit(solution)/shard_map/local_part/pallas_call | solution.py:350
  13.4 3.7 %collective-permute-start.2 = (f32[16,1024]{1,0:T(8,128)S(1)}, f32[16,1024]{1,0:T(8,128)S(1)}, u32[]{:S(2)}, u32[]{:S(2)}) collective-permute-start(f32[16,1024]{1,0:T(8,128)S(1)} %row_kernel.1.own_ref), channel_id=1, source_target_pairs={{0,4},{1,5},{2,6},{3,7},{4,0},{5,1},{6,2},{7,3},{8,12},{9,13},{10,... | collective-permute-start | bytes 196616 | tf_op jit(solution)/shard_map/ppermute | solution.py:485
  17.0 2.6 %local_part.3 = (f32[384,1024]{1,0:T(8,128)S(1)}, f32[384,1024]{1,0:T(8,128)S(1)}, f32[128,1024]{1,0:T(8,128)S(1)}, f32[128,1024]{1,0:T(8,128)S(1)}, f32[256,1024]{1,0:T(8,128)S(1)}) custom-call(f32[384,1024]{1,0:T(8,128)S(1)} %get-tuple-element.66.refs_0_, f32[384,1024]{1,0:T(8,128)S(1)} %get-tuple-element.67.refs_1_, bf16[384,2048]{1,0:T(8,128)(2,1)} %refs_2_.3, ...), custom_call_target="tpu_custom_call" | custom-call | flops 2990000128 | bytes 9594000 | tf_op jit(solution)/shard_map/local_part/pallas_call | solution.py:350
  19.7 1.3 %collective-permute-start.3 = (f32[16,1024]{1,0:T(8,128)S(1)}, f32[16,1024]{1,0:T(8,128)S(1)}, u32[]{:S(2)}, u32[]{:S(2)}) collective-permute-start(f32[16,1024]{1,0:T(8,128)S(1)} %plane_kernel.1), channel_id=1, source_target_pairs={{0,8},{1,9},{2,10},{3,11},{4,12},{5,13},{6,14},{7,15},{8,16},{9,17... | collective-permute-start | bytes 196616 | tf_op jit(solution)/shard_map/ppermute | solution.py:489
  21.0 2.5 %collective-permute-start.4 = (f32[16,1024]{1,0:T(8,128)S(1)}, f32[16,1024]{1,0:T(8,128)S(1)}, u32[]{:S(2)}, u32[]{:S(2)}) collective-permute-start(f32[16,1024]{1,0:T(8,128)S(1)} %plane_kernel.1), channel_id=1, source_target_pairs={{0,16},{1,17},{2,18},{3,19},{4,20},{5,21},{6,22},{7,23},{8,24},{9,... | collective-permute-start | bytes 196616 | tf_op jit(solution)/shard_map/ppermute | solution.py:489
  23.4 1.2 %collective-permute-start.5 = (f32[16,1024]{1,0:T(8,128)S(1)}, f32[16,1024]{1,0:T(8,128)S(1)}, u32[]{:S(2)}, u32[]{:S(2)}) collective-permute-start(f32[16,1024]{1,0:T(8,128)S(1)} %plane_kernel.1), channel_id=1, source_target_pairs={{0,24},{1,25},{2,26},{3,27},{4,28},{5,29},{6,30},{7,31},{8,0},{9,1... | collective-permute-start | bytes 196616 | tf_op jit(solution)/shard_map/ppermute | solution.py:489
  24.6 0.0 collective-permute-done.3.p1
  24.6 1.2 %collective-permute-done.4.p2 = f32[16,1024]{1,0:T(8,128)S(1)} collective-permute-done((f32[16,1024]{1,0:T(8,128)S(1)}, f32[16,1024]{1,0:T(8,128)S(1)}, u32[]{:S(2)}, u32[]{:S(2)}) %collective-permute-start.4) | collective-permute-done | bytes 65568 | tf_op jit(solution)/shard_map/ppermute | solution.py:489
  25.8 1.1 %collective-permute-done.5.p3 = f32[16,1024]{1,0:T(8,128)S(1)} collective-permute-done((f32[16,1024]{1,0:T(8,128)S(1)}, f32[16,1024]{1,0:T(8,128)S(1)}, u32[]{:S(2)}, u32[]{:S(2)}) %collective-permute-start.5) | collective-permute-done | bytes 65568 | tf_op jit(solution)/shard_map/ppermute | solution.py:489
  26.8 0.1 states_kernel.1
  26.9 0.4 collective-permute-start.6
  27.3 2.1 %mix.2 = (f32[8,400,128]{2,1,0:T(8,128)S(1)}, f32[384,128]{1,0:T(8,128)S(1)}) custom-call(f32[384,1024]{1,0:T(8,128)S(1)} %get-tuple-element.74.refs_0_, f32[384,1024]{1,0:T(8,128)S(1)} %get-tuple-element.75.refs_1_, f32[128,1024]{1,0:T(8,128)S(1)} %get-tuple-element.76.refs_2_, f32[128,1024]{1,0:T(8,128)S(1)} %get-tuple-element.77.refs_3_, ...), custom_call_target="tpu_custom_call" | custom-call | flops 2415000064 | bytes 7749000 | tf_op jit(solution)/shard_map/mix/pallas_call | solution.py:413
  29.5 0.8 %collective-permute-done.6.refs_5_ = f32[16,1024]{1,0:T(8,128)S(1)} collective-permute-done((f32[16,1024]{1,0:T(8,128)S(1)}, f32[16,1024]{1,0:T(8,128)S(1)}, u32[]{:S(2)}, u32[]{:S(2)}) %collective-permute-start.6) | collective-permute-done | bytes 65568 | tf_op jit(solution)/shard_map/ppermute | solution.py:485
  30.2 2.3 %mix.3 = (f32[1,384]{1,0:T(1,128)S(1)}, f32[8,400,128]{2,1,0:T(8,128)S(1)}) custom-call(f32[384,1024]{1,0:T(8,128)S(1)} %get-tuple-element.82.refs_0_, f32[384,1024]{1,0:T(8,128)S(1)} %get-tuple-element.83.refs_1_, f32[128,1024]{1,0:T(8,128)S(1)} %get-tuple-element.84.refs_2_, f32[128,1024]{1,0:T(8,128)S(1)} %get-tuple-element.85.refs_3_, ...), custom_call_target="tpu_custom_call" | custom-call | flops 2415000064 | bytes 7749000 | tf_op jit(solution)/shard_map/mix/pallas_call | solution.py:413
  32.5 4.9 %collective-permute-start.7 = (f32[1,384]{1,0:T(1,128)S(1)}, f32[1,384]{1,0:T(1,128)S(1)}, u32[]{:S(2)}, u32[]{:S(2)}) collective-permute-start(f32[1,384]{1,0:T(1,128)S(1)} %get-tuple-element.90.p0_ref), channel_id=1, source_target_pairs={{0,32},{32,0},{64,96},{96,64},{1,33},{33,1},{65,97},{97,65},{2,34}... | collective-permute-start | bytes 4616 | tf_op jit(solution)/shard_map/ppermute | solution.py:493
  37.4 0.9 %collective-permute-start.8 = (f32[1,384]{1,0:T(1,128)S(1)}, f32[1,384]{1,0:T(1,128)S(1)}, u32[]{:S(2)}, u32[]{:S(2)}) collective-permute-start(f32[1,384]{1,0:T(1,128)S(1)} %get-tuple-element.90.p0_ref), channel_id=1, source_target_pairs={{0,64},{32,96},{64,0},{96,32},{1,65},{33,97},{65,1},{97,33},{2,66}... | collective-permute-start | bytes 4616 | tf_op jit(solution)/shard_map/ppermute | solution.py:493
  38.3 0.8 %collective-permute-start.9 = (f32[1,384]{1,0:T(1,128)S(1)}, f32[1,384]{1,0:T(1,128)S(1)}, u32[]{:S(2)}, u32[]{:S(2)}) collective-permute-start(f32[1,384]{1,0:T(1,128)S(1)} %get-tuple-element.90.p0_ref), channel_id=1, source_target_pairs={{0,96},{32,64},{64,32},{96,0},{1,97},{33,65},{65,33},{97,1},{2,98}... | collective-permute-start | bytes 4616 | tf_op jit(solution)/shard_map/ppermute | solution.py:493
  39.1 0.7 %collective-permute-done.8.p2_ref = f32[1,384]{1,0:T(1,128)S(1)} collective-permute-done((f32[1,384]{1,0:T(1,128)S(1)}, f32[1,384]{1,0:T(1,128)S(1)}, u32[]{:S(2)}, u32[]{:S(2)}) %collective-permute-start.8) | collective-permute-done | bytes 1568 | tf_op jit(solution)/shard_map/ppermute | solution.py:493
  39.8 1.5 %collective-permute-done.9.p3_ref = f32[1,384]{1,0:T(1,128)S(1)} collective-permute-done((f32[1,384]{1,0:T(1,128)S(1)}, f32[1,384]{1,0:T(1,128)S(1)}, u32[]{:S(2)}, u32[]{:S(2)}) %collective-permute-start.9) | collective-permute-done | bytes 1568 | tf_op jit(solution)/shard_map/ppermute | solution.py:493
  41.3 1.5 %norm.1 = bf16[384,2048]{1,0:T(8,128)(2,1)} custom-call(f32[8,400,128]{2,1,0:T(8,128)S(1)} %get-tuple-element.81.g0, f32[8,400,128]{2,1,0:T(8,128)S(1)} %get-tuple-element.89.g1, f32[1,2048]{1,0:T(1,128)S(1)} %bitcast.4, f32[1,384]{1,0:T(1,128)S(1)} %get-tuple-element.90.p0_ref, f32[1,384]{1,0:T(1,128)S(1)} %collective-permute-done.7.p1_ref, ...), custom_call_target="tpu_custom_call" | custom-call | flops 1955000064 | bytes 6273000 | tf_op jit(solution)/shard_map/norm/pallas_call | solution.py:467
  (15 shorter events, 0.1 us)
Async XLA Ops:
  0.0 6.0 %copy-start.1 = (f32[16,2048]{1,0:T(8,128)S(1)}, f32[16,2048]{1,0:T(8,128)}, u32[]{:S(2)}) copy-start(f32[16,2048]{1,0:T(8,128)} %refs_6_.3) | copy-start | bytes 393220
  3.8 4.8 %collective-permute-start = (f32[16,1024]{1,0:T(8,128)S(1)}, f32[16,1024]{1,0:T(8,128)S(1)}, u32[]{:S(2)}, u32[]{:S(2)}) collective-permute-start(f32[16,1024]{1,0:T(8,128)S(1)} %get-tuple-element.53), channel_id=1, source_target_pairs={{0,1},{1,0},{2,3},{3,2},{4,5},{5,4},{6,7},{7,6},{8,9},{9,8},{10,11... | collective-permute-start | bytes 196616 | tf_op jit(solution)/shard_map/ppermute | solution.py:485
  6.0 4.7 %copy-start = (f32[16,2048]{1,0:T(8,128)S(1)}, f32[16,2048]{1,0:T(8,128)}, u32[]{:S(2)}) copy-start(f32[16,2048]{1,0:T(8,128)} %refs_4_.3) | copy-start | bytes 393220
  6.0 4.7 %copy-start.2 = (f32[2048]{0:T(1024)S(1)}, f32[2048]{0:T(1024)}, u32[]{:S(2)}) copy-start(f32[2048]{0:T(1024)} %param.12) | copy-start | bytes 24580
  8.7 4.6 %collective-permute-start.1 = (f32[16,1024]{1,0:T(8,128)S(1)}, f32[16,1024]{1,0:T(8,128)S(1)}, u32[]{:S(2)}, u32[]{:S(2)}) collective-permute-start(f32[16,1024]{1,0:T(8,128)S(1)} %pair_kernel.1.own_ref), channel_id=1, source_target_pairs={{0,3},{1,2},{2,1},{3,0},{4,7},{5,6},{6,5},{7,4},{8,11},{9,10},{10,... | collective-permute-start | bytes 196616 | tf_op jit(solution)/shard_map/ppermute | solution.py:485
  13.4 6.3 %collective-permute-start.2 = (f32[16,1024]{1,0:T(8,128)S(1)}, f32[16,1024]{1,0:T(8,128)S(1)}, u32[]{:S(2)}, u32[]{:S(2)}) collective-permute-start(f32[16,1024]{1,0:T(8,128)S(1)} %row_kernel.1.own_ref), channel_id=1, source_target_pairs={{0,4},{1,5},{2,6},{3,7},{4,0},{5,1},{6,2},{7,3},{8,12},{9,13},{10,... | collective-permute-start | bytes 196616 | tf_op jit(solution)/shard_map/ppermute | solution.py:485
  19.7 4.9 %collective-permute-start.3 = (f32[16,1024]{1,0:T(8,128)S(1)}, f32[16,1024]{1,0:T(8,128)S(1)}, u32[]{:S(2)}, u32[]{:S(2)}) collective-permute-start(f32[16,1024]{1,0:T(8,128)S(1)} %plane_kernel.1), channel_id=1, source_target_pairs={{0,8},{1,9},{2,10},{3,11},{4,12},{5,13},{6,14},{7,15},{8,16},{9,17... | collective-permute-start | bytes 196616 | tf_op jit(solution)/shard_map/ppermute | solution.py:489
  21.0 4.8 %collective-permute-start.4 = (f32[16,1024]{1,0:T(8,128)S(1)}, f32[16,1024]{1,0:T(8,128)S(1)}, u32[]{:S(2)}, u32[]{:S(2)}) collective-permute-start(f32[16,1024]{1,0:T(8,128)S(1)} %plane_kernel.1), channel_id=1, source_target_pairs={{0,16},{1,17},{2,18},{3,19},{4,20},{5,21},{6,22},{7,23},{8,24},{9,... | collective-permute-start | bytes 196616 | tf_op jit(solution)/shard_map/ppermute | solution.py:489
  23.4 3.4 %collective-permute-start.5 = (f32[16,1024]{1,0:T(8,128)S(1)}, f32[16,1024]{1,0:T(8,128)S(1)}, u32[]{:S(2)}, u32[]{:S(2)}) collective-permute-start(f32[16,1024]{1,0:T(8,128)S(1)} %plane_kernel.1), channel_id=1, source_target_pairs={{0,24},{1,25},{2,26},{3,27},{4,28},{5,29},{6,30},{7,31},{8,0},{9,1... | collective-permute-start | bytes 196616 | tf_op jit(solution)/shard_map/ppermute | solution.py:489
  26.9 3.3 %collective-permute-start.6 = (f32[16,1024]{1,0:T(8,128)S(1)}, f32[16,1024]{1,0:T(8,128)S(1)}, u32[]{:S(2)}, u32[]{:S(2)}) collective-permute-start(f32[16,1024]{1,0:T(8,128)S(1)} %get-tuple-element.87), channel_id=1, source_target_pairs={{0,1},{1,0},{2,3},{3,2},{4,5},{5,4},{6,7},{7,6},{8,9},{9,8},{10,11... | collective-permute-start | bytes 196616 | tf_op jit(solution)/shard_map/ppermute | solution.py:485
  30.2 11.0 %copy-start.3 = (f32[2048]{0:T(1024)S(1)}, f32[2048]{0:T(1024)}, u32[]{:S(2)}) copy-start(f32[2048]{0:T(1024)} %param.13) | copy-start | bytes 24580
  32.5 6.6 %collective-permute-start.7 = (f32[1,384]{1,0:T(1,128)S(1)}, f32[1,384]{1,0:T(1,128)S(1)}, u32[]{:S(2)}, u32[]{:S(2)}) collective-permute-start(f32[1,384]{1,0:T(1,128)S(1)} %get-tuple-element.90.p0_ref), channel_id=1, source_target_pairs={{0,32},{32,0},{64,96},{96,64},{1,33},{33,1},{65,97},{97,65},{2,34}... | collective-permute-start | bytes 4616 | tf_op jit(solution)/shard_map/ppermute | solution.py:493
  37.4 2.4 %collective-permute-start.8 = (f32[1,384]{1,0:T(1,128)S(1)}, f32[1,384]{1,0:T(1,128)S(1)}, u32[]{:S(2)}, u32[]{:S(2)}) collective-permute-start(f32[1,384]{1,0:T(1,128)S(1)} %get-tuple-element.90.p0_ref), channel_id=1, source_target_pairs={{0,64},{32,96},{64,0},{96,32},{1,65},{33,97},{65,1},{97,33},{2,66}... | collective-permute-start | bytes 4616 | tf_op jit(solution)/shard_map/ppermute | solution.py:493
  38.3 3.0 %collective-permute-start.9 = (f32[1,384]{1,0:T(1,128)S(1)}, f32[1,384]{1,0:T(1,128)S(1)}, u32[]{:S(2)}, u32[]{:S(2)}) collective-permute-start(f32[1,384]{1,0:T(1,128)S(1)} %get-tuple-element.90.p0_ref), channel_id=1, source_target_pairs={{0,96},{32,64},{64,32},{96,0},{1,97},{33,65},{65,33},{97,1},{2,98}... | collective-permute-start | bytes 4616 | tf_op jit(solution)/shard_map/ppermute | solution.py:493

commit v5 on v4

--- a/solution.py
+++ b/solution.py
@@ -55,9 +55,19 @@
     return jnp.where(place >= by, pltpu.roll(x, by, 0), 0.0)
 
 
-def end_of_tile(span, signal_ref, rates, sent_ref, ends_ref, here):
-    one = spread(jnp.exp(-rates))
-    run = spread(jnp.exp(rates * float(-RUN)))
+def fill_decays(span, rates_ref, first, decays_ref):
+    def tile(t, _):
+        rates = rates_ref[:, lanes_at(first + t * LANES)]
+        for i, length in enumerate((1, RUN, span, 2 * span, 4 * span)):
+            decays_ref[i, :, lanes_at(t * LANES)] = jnp.exp(rates * float(-length))
+        return 0
+
+    lax.fori_loop(0, decays_ref.shape[2] // LANES, tile, 0)
+
+
+def end_of_tile(span, signal_ref, decays_ref, sent_ref, ends_ref, here):
+    one = spread(decays_ref[0, :, here])
+    run = spread(decays_ref[1, :, here])
     total = None
     for g in range(span // RUN):
         acc = None
@@ -69,13 +79,13 @@
         for n in range(ORDER):
             ends_ref[pl.ds((g * ORDER + n) * SUB, SUB), here] = acc[n]
         total = acc if total is None else [t * r + a for t, r, a in zip(total, run, acc)]
-    for by in (1, 2, 4):
-        across = spread(jnp.exp(rates * float(-span * by)))
+    for i, by in enumerate((1, 2, 4)):
+        across = spread(decays_ref[2 + i, :, here])
         total = [t + pltpu.roll(t, by, 0) * a for t, a in zip(total, across)]
     return [t[SUB - 1 :, :] for t in total]
 
 
-def end_of_piece(key_ref, value_ref, rates_ref, first, signal_ref, sent_ref, ends_ref, end_ref, at):
+def end_of_piece(key_ref, value_ref, decays_ref, signal_ref, sent_ref, ends_ref, end_ref, at):
     span = key_ref.shape[0] // SUB
 
     def tile(t, _):
@@ -83,7 +93,7 @@
         for s in range(SUB):
             rows = pl.ds(s * span, span)
             signal_ref[pl.ds(s * PITCH, span), :] = key_ref[rows, there].astype(F32) * value_ref[rows, there].astype(F32)
-        ends = end_of_tile(span, signal_ref, rates_ref[:, lanes_at(first + t * LANES)], sent_ref, ends_ref, here)
+        ends = end_of_tile(span, signal_ref, decays_ref, sent_ref, ends_ref, here)
         for n in range(ORDER):
             end_ref[n : n + 1, here] = ends[n]
         return 0
@@ -108,7 +118,7 @@
 
 
 def far_end_kernel(key_ref, value_ref, rates_ref, end_ref, sent_ref, ends_ref, key_own, value_own,
-                   key_held, value_held, signal_ref, rates_here, sems, sem):
+                   key_held, value_held, signal_ref, rates_here, decays_ref, sems, sem):
     width = key_held.shape[1]
     cuts = 4
     step = width // cuts
@@ -122,6 +132,7 @@
         for c in pieces[i]:
             c.start()
     rates_copy.wait()
+    fill_decays(key_ref.shape[0] // SUB, rates_here, half_of(1) * width, decays_ref)
     for i in range(cuts):
         for c in pieces[i]:
             c.wait()
@@ -129,7 +140,7 @@
             for c in pieces[i + ahead]:
                 c.start()
         part = pl.ds(i * step, step)
-        end_of_piece(key_held.at[:, part], value_held.at[:, part], rates_here, half_of(1) * width + i * step,
+        end_of_piece(key_held.at[:, part], value_held.at[:, part], decays_ref,
                      signal_ref, sent_ref, ends_ref, end_ref, i * step)
     for p in pieces[cuts:]:
         for c in p:
@@ -158,6 +169,7 @@
             pltpu.VMEM((tokens, width), BF16),
             pltpu.VMEM((SUB * PITCH, LANES), F32),
             pltpu.VMEM((ORDER, channels), F32),
+            pltpu.VMEM((5, ORDER, width), F32),
             pltpu.SemaphoreType.DMA((2, 2, 4)),
             pltpu.SemaphoreType.DMA(()),
         ],
@@ -171,7 +183,7 @@
 
 
 def own_end_kernel(key_first, value_first, key_ref, value_ref, rates_ref, end_ref, sent_ref, ends_ref, tables_ref,
-                   key_held, value_held, signal_ref, sems):
+                   key_held, value_held, signal_ref, decays_ref, sems):
     tokens, width = key_held.shape
     x, z, _, _ = position()
     first = half_of(0) * width
@@ -196,6 +208,7 @@
         return 0
 
     lax.fori_loop(0, width // LANES, table, 0)
+    fill_decays(tokens // SUB, rates_ref, first, decays_ref)
     for i in range(cuts):
         part = pl.ds(i * step, step)
         if i < brought:
@@ -204,7 +217,7 @@
             key, value = key_held, value_held
             for c in pieces[i - brought]:
                 c.wait()
-        end_of_piece(key.at[:, part], value.at[:, part], rates_ref, first + i * step,
+        end_of_piece(key.at[:, part], value.at[:, part], decays_ref,
                      signal_ref, sent_ref, ends_ref, end_ref, i * step)
 
 
@@ -220,6 +233,7 @@
             pltpu.VMEM((tokens, width), BF16),
             pltpu.VMEM((tokens, width), BF16),
             pltpu.VMEM((SUB * PITCH, LANES), F32),
+            pltpu.VMEM((5, ORDER, width), F32),
             pltpu.SemaphoreType.DMA((2, 4)),
         ],
         compiler_params=PARAMS,
@@ -269,7 +283,7 @@
 
 
 def local_kernel(by, sent_ref, ends_ref, gate_ref, rates_ref, residues_ref, skip_ref,
-                 mixed_ref, gate_out, start_ref, reach_ref, enter_ref, gate_held, gate_f32, sems):
+                 mixed_ref, gate_out, start_ref, reach_ref, enter_ref, decay_ref, gate_held, gate_f32, sems):
     tokens, width = mixed_ref.shape
     span = tokens // SUB
     place = lax.broadcasted_iota(jnp.int32, (SUB, LANES), 0).astype(F32)
@@ -287,6 +301,7 @@
         rates = rates_ref[:, lanes]
         residues = residues_ref[:, lanes]
         decay = jnp.exp(-rates)
+        decay_ref[:, here] = decay
 
         taps, term = [], residues
         for k in range(RUN):
@@ -346,12 +361,13 @@
     token_part = jax.ShapeDtypeStruct((tokens, width), F32)
     mode_part = jax.ShapeDtypeStruct((ORDER * SUB, width), F32)
     enter_part = jax.ShapeDtypeStruct((2 * ORDER * SUB, width), F32)
+    decay_part = jax.ShapeDtypeStruct((ORDER, width), F32)
     gate = pltpu.with_memory_space_constraint(gate, pltpu.HBM)
     return pl.pallas_call(
         lambda *refs: local_kernel(by, *refs),
         in_specs=[IN_VMEM, IN_VMEM, IN_HBM, IN_VMEM, IN_VMEM, IN_VMEM],
-        out_specs=[IN_VMEM] * 5,
-        out_shape=[token_part, token_part, mode_part, mode_part, enter_part],
+        out_specs=[IN_VMEM] * 6,
+        out_shape=[token_part, token_part, mode_part, mode_part, enter_part, decay_part],
         scratch_shapes=[
             pltpu.VMEM((width // LANES, tokens, LANES), BF16),
             pltpu.VMEM((SUB * PITCH, LANES), F32),
@@ -363,7 +379,7 @@
     )(sent, ends, gate, rates, residues, skip)
 
 
-def mix_kernel(by, last, mixed_ref, gate_ref, start_ref, reach_ref, enter_ref, state_ref, rates_ref, *rest):
+def mix_kernel(by, last, mixed_ref, gate_ref, start_ref, reach_ref, enter_ref, decay_ref, state_ref, *rest):
     tokens, width = mixed_ref.shape
     span = tokens // SUB
     gated_ref, sums_ref = rest[-2], rest[-1]
@@ -376,7 +392,7 @@
 
     def tile(t, _):
         here = lanes_at(t * LANES)
-        step = spread(jnp.exp(-rates_ref[:, lanes_at(half_of(by) * width + t * LANES)]))
+        step = spread(decay_ref[:, here])
         state = state_ref[:, here]
         terms = []
         for n in range(ORDER):
@@ -401,11 +417,11 @@
             power_ref[:, rows] = jnp.sum(jnp.transpose(sums_ref[rows, :]), axis=0, keepdims=True)
 
 
-def mix(by, last, part, state, rates, sums):
+def mix(by, last, part, state, sums):
     tokens, width = part[0].shape
     out_sums = jax.ShapeDtypeStruct((tokens, LANES), F32)
     gated = jax.ShapeDtypeStruct((width // LANES, SUB * OUT_PITCH, LANES), F32)
-    args = [*part, state, rates] + ([] if sums is None else [sums])
+    args = [*part, state] + ([] if sums is None else [sums])
     if last:
         outs, scratch = [jax.ShapeDtypeStruct((1, tokens), F32), gated], [pltpu.VMEM((tokens, LANES), F32)]
     else:
@@ -519,8 +535,8 @@
     mine, theirs = small(states_kernel, 2, own, got, other_pair, other_row, *planes, tables)
 
     theirs = with_partner(theirs, 1)
-    own_gated, sums = mix(0, False, own_part, mine, rates, None)
-    power, far_gated = mix(1, True, far_part, theirs, rates, sums)
+    own_gated, sums = mix(0, False, own_part, mine, None)
+    power, far_gated = mix(1, True, far_part, theirs, sums)
     powers = [power] + [over_ch(power, k) for k in (1, 2, 3)]
     return norm([own_gated, far_gated], norm_gain[None, :], powers)
 

time: 42.9 us -> 42.7 us (level)
  no operation moved by 1% of the time
where the time goes in v5:
time: 42.7 us; the launch traced here: 42.5 us
  starting transfers between devices  19.8 us (46%)
  Pallas kernels  17.4 us (41%)
  waiting for transfers between devices  5.31 us (12%)
    ppermute x4, starting transfers between devices, with_partner(): return lax.ppermute(x, 'seq', [(i, i ^ by) for i in range(32)])  8.28 us
    ppermute x3, starting transfers between devices, over_ch(): return lax.ppermute(x, 'ch', [(i, i ^ by) for i in range(4)])  6.6 us
    pallas_call x2, Pallas kernels, local_part(): pl.pallas_call(lambda *refs: local_kernel(by, *refs), in_specs=[IN_VMEM,...  5.24 us
    ppermute x3, starting transfers between devices, over_x(): return lax.ppermute(x, 'seq', [(i, (i + 8 * by) % 32) for i in range(32)])  4.88 us
    pallas_call x2, Pallas kernels, mix(): pl.pallas_call(lambda *refs: mix_kernel(by, last, *refs), in_specs=[IN_VM...  4.14 us
    pallas_call x1, Pallas kernels, far_end(): pl.pallas_call(far_end_kernel, in_specs=[IN_HBM] * 3, out_specs=[IN_VMEM]...  3.7 us
    pallas_call x1, Pallas kernels, own_end(): pl.pallas_call(own_end_kernel, in_specs=[IN_VMEM, IN_VMEM, IN_HBM, IN_HBM...  2.68 us
    ppermute x3, waiting for transfers between devices, over_x(): return lax.ppermute(x, 'seq', [(i, (i + 8 * by) % 32) for i in range(32)])  2.26 us
  transfers between devices with their start and end apart: 10, of which 5 were waited for; matrix products, arithmetic and copies ran while one was open for 0% of the time, Pallas kernels for 23%

profile of v5, /device:TPU:1, one launch (start us, length us, event | category | flops | bytes accessed | tf_op | source)
XLA Modules:
  0.0 42.5 jit_solution(13273584830543458682)
XLA Ops:
  0.0 3.7 %far_end.1 = (f32[16,1024]{1,0:T(8,128)S(1)}, f32[384,1024]{1,0:T(8,128)S(1)}, f32[384,1024]{1,0:T(8,128)S(1)}, bf16[384,512]{1,0:T(8,128)(2,1)S(1)}, bf16[384,512]{1,0:T(8,128)(2,1)S(1)}) custom-call(bf16[384,2048]{1,0:T(8,128)(2,1)} %key_ref.3, bf16[384,2048]{1,0:T(8,128)(2,1)} %value_ref.3, f32[16,2048]{1,0:T(8,128)} %refs_3_.1), custom_call_target="tpu_custom_call" | custom-call | flops 3910000128 | bytes 12546000 | tf_op jit(solution)/shard_map/far_end/pallas_call | solution.py:162
  3.7 2.2 %collective-permute-start = (f32[16,1024]{1,0:T(8,128)S(1)}, f32[16,1024]{1,0:T(8,128)S(1)}, u32[]{:S(2)}, u32[]{:S(2)}) collective-permute-start(f32[16,1024]{1,0:T(8,128)S(1)} %get-tuple-element.57), channel_id=1, source_target_pairs={{0,1},{1,0},{2,3},{3,2},{4,5},{5,4},{6,7},{7,6},{8,9},{9,8},{10,11... | collective-permute-start | bytes 196616 | tf_op jit(solution)/shard_map/ppermute | solution.py:501
  5.9 2.7 %own_end.1 = (f32[16,1024]{1,0:T(8,128)S(1)}, f32[384,1024]{1,0:T(8,128)S(1)}, f32[384,1024]{1,0:T(8,128)S(1)}, f32[7,16,1024]{2,1,0:T(8,128)S(1)}) custom-call(bf16[384,512]{1,0:T(8,128)(2,1)S(1)} %get-tuple-element.52.key_first, bf16[384,512]{1,0:T(8,128)(2,1)S(1)} %get-tuple-element.53.value_first, bf16[384,2048]{1,0:T(8,128)(2,1)} %key_ref.3, ...), custom_call_target="tpu_custom_call" | custom-call | flops 3104999936 | bytes 9963000 | tf_op jit(solution)/shard_map/own_end/pallas_call | solution.py:227
  8.7 2.0 %collective-permute-start.1 = (f32[16,1024]{1,0:T(8,128)S(1)}, f32[16,1024]{1,0:T(8,128)S(1)}, u32[]{:S(2)}, u32[]{:S(2)}) collective-permute-start(f32[16,1024]{1,0:T(8,128)S(1)} %pair_kernel.1.own_ref), channel_id=1, source_target_pairs={{0,3},{1,2},{2,1},{3,0},{4,7},{5,6},{6,5},{7,4},{8,11},{9,10},{10,... | collective-permute-start | bytes 196616 | tf_op jit(solution)/shard_map/ppermute | solution.py:501
  10.6 2.6 %local_part.2 = (f32[384,1024]{1,0:T(8,128)S(1)}, f32[384,1024]{1,0:T(8,128)S(1)}, f32[128,1024]{1,0:T(8,128)S(1)}, f32[128,1024]{1,0:T(8,128)S(1)}, f32[256,1024]{1,0:T(8,128)S(1)}, /*index=5*/f32[16,1024]{1,0:T(8,128)S(1)}) custom-call(f32[384,1024]{1,0:T(8,128)S(1)} %get-tuple-element.60.refs_0_, f32[384,1024]{1,0:T(8,128)S(1)} %get-tuple-element.61.refs_1_, ...), custom_call_target="tpu_custom_call" | custom-call | flops 2990000128 | bytes 9594000 | tf_op jit(solution)/shard_map/local_part/pallas_call | solution.py:366
  13.3 0.0 collective-permute-done.1.got_ref.pair_ref
  13.3 3.7 %collective-permute-start.2 = (f32[16,1024]{1,0:T(8,128)S(1)}, f32[16,1024]{1,0:T(8,128)S(1)}, u32[]{:S(2)}, u32[]{:S(2)}) collective-permute-start(f32[16,1024]{1,0:T(8,128)S(1)} %row_kernel.1.own_ref), channel_id=1, source_target_pairs={{0,4},{1,5},{2,6},{3,7},{4,0},{5,1},{6,2},{7,3},{8,12},{9,13},{10,... | collective-permute-start | bytes 196616 | tf_op jit(solution)/shard_map/ppermute | solution.py:501
  17.0 2.6 %local_part.3 = (f32[384,1024]{1,0:T(8,128)S(1)}, f32[384,1024]{1,0:T(8,128)S(1)}, f32[128,1024]{1,0:T(8,128)S(1)}, f32[128,1024]{1,0:T(8,128)S(1)}, f32[256,1024]{1,0:T(8,128)S(1)}, /*index=5*/f32[16,1024]{1,0:T(8,128)S(1)}) custom-call(f32[384,1024]{1,0:T(8,128)S(1)} %get-tuple-element.71.refs_0_, f32[384,1024]{1,0:T(8,128)S(1)} %get-tuple-element.72.refs_1_, ...), custom_call_target="tpu_custom_call" | custom-call | flops 2990000128 | bytes 9594000 | tf_op jit(solution)/shard_map/local_part/pallas_call | solution.py:366
  19.7 1.3 %collective-permute-start.3 = (f32[16,1024]{1,0:T(8,128)S(1)}, f32[16,1024]{1,0:T(8,128)S(1)}, u32[]{:S(2)}, u32[]{:S(2)}) collective-permute-start(f32[16,1024]{1,0:T(8,128)S(1)} %plane_kernel.1), channel_id=1, source_target_pairs={{0,8},{1,9},{2,10},{3,11},{4,12},{5,13},{6,14},{7,15},{8,16},{9,17... | collective-permute-start | bytes 196616 | tf_op jit(solution)/shard_map/ppermute | solution.py:505
  20.9 2.5 %collective-permute-start.4 = (f32[16,1024]{1,0:T(8,128)S(1)}, f32[16,1024]{1,0:T(8,128)S(1)}, u32[]{:S(2)}, u32[]{:S(2)}) collective-permute-start(f32[16,1024]{1,0:T(8,128)S(1)} %plane_kernel.1), channel_id=1, source_target_pairs={{0,16},{1,17},{2,18},{3,19},{4,20},{5,21},{6,22},{7,23},{8,24},{9,... | collective-permute-start | bytes 196616 | tf_op jit(solution)/shard_map/ppermute | solution.py:505
  23.4 1.2 %collective-permute-start.5 = (f32[16,1024]{1,0:T(8,128)S(1)}, f32[16,1024]{1,0:T(8,128)S(1)}, u32[]{:S(2)}, u32[]{:S(2)}) collective-permute-start(f32[16,1024]{1,0:T(8,128)S(1)} %plane_kernel.1), channel_id=1, source_target_pairs={{0,24},{1,25},{2,26},{3,27},{4,28},{5,29},{6,30},{7,31},{8,0},{9,1... | collective-permute-start | bytes 196616 | tf_op jit(solution)/shard_map/ppermute | solution.py:505
  24.5 1.2 %collective-permute-done.4.p2 = f32[16,1024]{1,0:T(8,128)S(1)} collective-permute-done((f32[16,1024]{1,0:T(8,128)S(1)}, f32[16,1024]{1,0:T(8,128)S(1)}, u32[]{:S(2)}, u32[]{:S(2)}) %collective-permute-start.4) | collective-permute-done | bytes 65568 | tf_op jit(solution)/shard_map/ppermute | solution.py:505
  25.7 1.1 %collective-permute-done.5.p3 = f32[16,1024]{1,0:T(8,128)S(1)} collective-permute-done((f32[16,1024]{1,0:T(8,128)S(1)}, f32[16,1024]{1,0:T(8,128)S(1)}, u32[]{:S(2)}, u32[]{:S(2)}) %collective-permute-start.5) | collective-permute-done | bytes 65568 | tf_op jit(solution)/shard_map/ppermute | solution.py:505
  26.8 0.1 states_kernel.1
  26.9 0.4 collective-permute-start.6
  27.3 2.0 %mix.2 = (f32[8,400,128]{2,1,0:T(8,128)S(1)}, f32[384,128]{1,0:T(8,128)S(1)}) custom-call(f32[384,1024]{1,0:T(8,128)S(1)} %get-tuple-element.80.refs_0_, f32[384,1024]{1,0:T(8,128)S(1)} %get-tuple-element.81.refs_1_, f32[128,1024]{1,0:T(8,128)S(1)} %get-tuple-element.82.refs_2_, f32[128,1024]{1,0:T(8,128)S(1)} %get-tuple-element.83.refs_3_, ...), custom_call_target="tpu_custom_call" | custom-call | flops 2415000064 | bytes 7749000 | tf_op jit(solution)/shard_map/mix/pallas_call | solution.py:429
  29.3 0.9 %collective-permute-done.6.refs_6_ = f32[16,1024]{1,0:T(8,128)S(1)} collective-permute-done((f32[16,1024]{1,0:T(8,128)S(1)}, f32[16,1024]{1,0:T(8,128)S(1)}, u32[]{:S(2)}, u32[]{:S(2)}) %collective-permute-start.6) | collective-permute-done | bytes 65568 | tf_op jit(solution)/shard_map/ppermute | solution.py:501
  30.1 2.1 %mix.3 = (f32[1,384]{1,0:T(1,128)S(1)}, f32[8,400,128]{2,1,0:T(8,128)S(1)}) custom-call(f32[384,1024]{1,0:T(8,128)S(1)} %get-tuple-element.89.refs_0_, f32[384,1024]{1,0:T(8,128)S(1)} %get-tuple-element.90.refs_1_, f32[128,1024]{1,0:T(8,128)S(1)} %get-tuple-element.91.refs_2_, f32[128,1024]{1,0:T(8,128)S(1)} %get-tuple-element.92.refs_3_, ...), custom_call_target="tpu_custom_call" | custom-call | flops 2415000064 | bytes 7749000 | tf_op jit(solution)/shard_map/mix/pallas_call | solution.py:429
  32.3 4.9 %collective-permute-start.7 = (f32[1,384]{1,0:T(1,128)S(1)}, f32[1,384]{1,0:T(1,128)S(1)}, u32[]{:S(2)}, u32[]{:S(2)}) collective-permute-start(f32[1,384]{1,0:T(1,128)S(1)} %get-tuple-element.98.p0_ref), channel_id=1, source_target_pairs={{0,32},{32,0},{64,96},{96,64},{1,33},{33,1},{65,97},{97,65},{2,34}... | collective-permute-start | bytes 4616 | tf_op jit(solution)/shard_map/ppermute | solution.py:509
  37.2 0.9 %collective-permute-start.8 = (f32[1,384]{1,0:T(1,128)S(1)}, f32[1,384]{1,0:T(1,128)S(1)}, u32[]{:S(2)}, u32[]{:S(2)}) collective-permute-start(f32[1,384]{1,0:T(1,128)S(1)} %get-tuple-element.98.p0_ref), channel_id=1, source_target_pairs={{0,64},{32,96},{64,0},{96,32},{1,65},{33,97},{65,1},{97,33},{2,66}... | collective-permute-start | bytes 4616 | tf_op jit(solution)/shard_map/ppermute | solution.py:509
  38.1 0.8 %collective-permute-start.9 = (f32[1,384]{1,0:T(1,128)S(1)}, f32[1,384]{1,0:T(1,128)S(1)}, u32[]{:S(2)}, u32[]{:S(2)}) collective-permute-start(f32[1,384]{1,0:T(1,128)S(1)} %get-tuple-element.98.p0_ref), channel_id=1, source_target_pairs={{0,96},{32,64},{64,32},{96,0},{1,97},{33,65},{65,33},{97,1},{2,98}... | collective-permute-start | bytes 4616 | tf_op jit(solution)/shard_map/ppermute | solution.py:509
  38.9 0.7 %collective-permute-done.8.p2_ref = f32[1,384]{1,0:T(1,128)S(1)} collective-permute-done((f32[1,384]{1,0:T(1,128)S(1)}, f32[1,384]{1,0:T(1,128)S(1)}, u32[]{:S(2)}, u32[]{:S(2)}) %collective-permute-start.8) | collective-permute-done | bytes 1568 | tf_op jit(solution)/shard_map/ppermute | solution.py:509
  39.6 1.5 %collective-permute-done.9.p3_ref = f32[1,384]{1,0:T(1,128)S(1)} collective-permute-done((f32[1,384]{1,0:T(1,128)S(1)}, f32[1,384]{1,0:T(1,128)S(1)}, u32[]{:S(2)}, u32[]{:S(2)}) %collective-permute-start.9) | collective-permute-done | bytes 1568 | tf_op jit(solution)/shard_map/ppermute | solution.py:509
  41.1 1.5 %norm.1 = bf16[384,2048]{1,0:T(8,128)(2,1)} custom-call(f32[8,400,128]{2,1,0:T(8,128)S(1)} %get-tuple-element.88.g0, f32[8,400,128]{2,1,0:T(8,128)S(1)} %get-tuple-element.97.g1, f32[1,2048]{1,0:T(1,128)S(1)} %bitcast.4, f32[1,384]{1,0:T(1,128)S(1)} %get-tuple-element.98.p0_ref, f32[1,384]{1,0:T(1,128)S(1)} %collective-permute-done.7.p1_ref, ...), custom_call_target="tpu_custom_call" | custom-call | flops 1955000064 | bytes 6273000 | tf_op jit(solution)/shard_map/norm/pallas_call | solution.py:483
  (15 shorter events, 0.1 us)
Async XLA Ops:
  0.0 5.9 %copy-start = (f32[16,2048]{1,0:T(8,128)S(1)}, f32[16,2048]{1,0:T(8,128)}, u32[]{:S(2)}) copy-start(f32[16,2048]{1,0:T(8,128)} %refs_3_.1) | copy-start | bytes 393220
  3.7 4.9 %collective-permute-start = (f32[16,1024]{1,0:T(8,128)S(1)}, f32[16,1024]{1,0:T(8,128)S(1)}, u32[]{:S(2)}, u32[]{:S(2)}) collective-permute-start(f32[16,1024]{1,0:T(8,128)S(1)} %get-tuple-element.57), channel_id=1, source_target_pairs={{0,1},{1,0},{2,3},{3,2},{4,5},{5,4},{6,7},{7,6},{8,9},{9,8},{10,11... | collective-permute-start | bytes 196616 | tf_op jit(solution)/shard_map/ppermute | solution.py:501
  5.9 4.7 %copy-start.1 = (f32[16,2048]{1,0:T(8,128)S(1)}, f32[16,2048]{1,0:T(8,128)}, u32[]{:S(2)}) copy-start(f32[16,2048]{1,0:T(8,128)} %refs_4_.3) | copy-start | bytes 393220
  5.9 4.7 %copy-start.2 = (f32[2048]{0:T(1024)S(1)}, f32[2048]{0:T(1024)}, u32[]{:S(2)}) copy-start(f32[2048]{0:T(1024)} %param.12) | copy-start | bytes 24580
  8.7 4.6 %collective-permute-start.1 = (f32[16,1024]{1,0:T(8,128)S(1)}, f32[16,1024]{1,0:T(8,128)S(1)}, u32[]{:S(2)}, u32[]{:S(2)}) collective-permute-start(f32[16,1024]{1,0:T(8,128)S(1)} %pair_kernel.1.own_ref), channel_id=1, source_target_pairs={{0,3},{1,2},{2,1},{3,0},{4,7},{5,6},{6,5},{7,4},{8,11},{9,10},{10,... | collective-permute-start | bytes 196616 | tf_op jit(solution)/shard_map/ppermute | solution.py:501
  13.3 6.3 %collective-permute-start.2 = (f32[16,1024]{1,0:T(8,128)S(1)}, f32[16,1024]{1,0:T(8,128)S(1)}, u32[]{:S(2)}, u32[]{:S(2)}) collective-permute-start(f32[16,1024]{1,0:T(8,128)S(1)} %row_kernel.1.own_ref), channel_id=1, source_target_pairs={{0,4},{1,5},{2,6},{3,7},{4,0},{5,1},{6,2},{7,3},{8,12},{9,13},{10,... | collective-permute-start | bytes 196616 | tf_op jit(solution)/shard_map/ppermute | solution.py:501
  19.7 4.9 %collective-permute-start.3 = (f32[16,1024]{1,0:T(8,128)S(1)}, f32[16,1024]{1,0:T(8,128)S(1)}, u32[]{:S(2)}, u32[]{:S(2)}) collective-permute-start(f32[16,1024]{1,0:T(8,128)S(1)} %plane_kernel.1), channel_id=1, source_target_pairs={{0,8},{1,9},{2,10},{3,11},{4,12},{5,13},{6,14},{7,15},{8,16},{9,17... | collective-permute-start | bytes 196616 | tf_op jit(solution)/shard_map/ppermute | solution.py:505
  20.9 4.8 %collective-permute-start.4 = (f32[16,1024]{1,0:T(8,128)S(1)}, f32[16,1024]{1,0:T(8,128)S(1)}, u32[]{:S(2)}, u32[]{:S(2)}) collective-permute-start(f32[16,1024]{1,0:T(8,128)S(1)} %plane_kernel.1), channel_id=1, source_target_pairs={{0,16},{1,17},{2,18},{3,19},{4,20},{5,21},{6,22},{7,23},{8,24},{9,... | collective-permute-start | bytes 196616 | tf_op jit(solution)/shard_map/ppermute | solution.py:505
  23.4 3.4 %collective-permute-start.5 = (f32[16,1024]{1,0:T(8,128)S(1)}, f32[16,1024]{1,0:T(8,128)S(1)}, u32[]{:S(2)}, u32[]{:S(2)}) collective-permute-start(f32[16,1024]{1,0:T(8,128)S(1)} %plane_kernel.1), channel_id=1, source_target_pairs={{0,24},{1,25},{2,26},{3,27},{4,28},{5,29},{6,30},{7,31},{8,0},{9,1... | collective-permute-start | bytes 196616 | tf_op jit(solution)/shard_map/ppermute | solution.py:505
  26.9 3.3 %collective-permute-start.6 = (f32[16,1024]{1,0:T(8,128)S(1)}, f32[16,1024]{1,0:T(8,128)S(1)}, u32[]{:S(2)}, u32[]{:S(2)}) collective-permute-start(f32[16,1024]{1,0:T(8,128)S(1)} %get-tuple-element.95), channel_id=1, source_target_pairs={{0,1},{1,0},{2,3},{3,2},{4,5},{5,4},{6,7},{7,6},{8,9},{9,8},{10,11... | collective-permute-start | bytes 196616 | tf_op jit(solution)/shard_map/ppermute | solution.py:501
  30.1 10.9 %copy-start.3 = (f32[2048]{0:T(1024)S(1)}, f32[2048]{0:T(1024)}, u32[]{:S(2)}) copy-start(f32[2048]{0:T(1024)} %param.13) | copy-start | bytes 24580
  32.3 6.6 %collective-permute-start.7 = (f32[1,384]{1,0:T(1,128)S(1)}, f32[1,384]{1,0:T(1,128)S(1)}, u32[]{:S(2)}, u32[]{:S(2)}) collective-permute-start(f32[1,384]{1,0:T(1,128)S(1)} %get-tuple-element.98.p0_ref), channel_id=1, source_target_pairs={{0,32},{32,0},{64,96},{96,64},{1,33},{33,1},{65,97},{97,65},{2,34}... | collective-permute-start | bytes 4616 | tf_op jit(solution)/shard_map/ppermute | solution.py:509
  37.2 2.4 %collective-permute-start.8 = (f32[1,384]{1,0:T(1,128)S(1)}, f32[1,384]{1,0:T(1,128)S(1)}, u32[]{:S(2)}, u32[]{:S(2)}) collective-permute-start(f32[1,384]{1,0:T(1,128)S(1)} %get-tuple-element.98.p0_ref), channel_id=1, source_target_pairs={{0,64},{32,96},{64,0},{96,32},{1,65},{33,97},{65,1},{97,33},{2,66}... | collective-permute-start | bytes 4616 | tf_op jit(solution)/shard_map/ppermute | solution.py:509
  38.1 3.0 %collective-permute-start.9 = (f32[1,384]{1,0:T(1,128)S(1)}, f32[1,384]{1,0:T(1,128)S(1)}, u32[]{:S(2)}, u32[]{:S(2)}) collective-permute-start(f32[1,384]{1,0:T(1,128)S(1)} %get-tuple-element.98.p0_ref), channel_id=1, source_target_pairs={{0,96},{32,64},{64,32},{96,0},{1,97},{33,65},{65,33},{97,1},{2,98}... | collective-permute-start | bytes 4616 | tf_op jit(solution)/shard_map/ppermute | solution.py:509

commit v6 on v5

--- a/solution.py
+++ b/solution.py
@@ -98,7 +98,7 @@
             end_ref[n : n + 1, here] = ends[n]
         return 0
 
-    lax.fori_loop(0, key_ref.shape[1] // LANES, tile, 0)
+    lax.fori_loop(0, key_ref.shape[1] // LANES, tile, 0, unroll=2)
 
 
 def half_copies(by, sources, targets, sems, cuts, which):
@@ -410,7 +410,7 @@
             sums_ref[rows, :] += gated * gated
         return 0
 
-    lax.fori_loop(0, width // LANES, tile, 0)
+    lax.fori_loop(0, width // LANES, tile, 0, unroll=2)
     if last:
         for block in range(tokens // LANES):
             rows = pl.ds(block * LANES, LANES)

time: 42.7 us -> 42.6 us (level)
  no operation moved by 1% of the time
where the time goes in v6:
time: 42.6 us; the launch traced here: 42.4 us
  starting transfers between devices  19.8 us (46%)
  Pallas kernels  17.2 us (40%)
  waiting for transfers between devices  5.41 us (13%)
    ppermute x4, starting transfers between devices, with_partner(): return lax.ppermute(x, 'seq', [(i, i ^ by) for i in range(32)])  8.28 us
    ppermute x3, starting transfers between devices, over_ch(): return lax.ppermute(x, 'ch', [(i, i ^ by) for i in range(4)])  6.6 us
    pallas_call x2, Pallas kernels, local_part(): pl.pallas_call(lambda *refs: local_kernel(by, *refs), in_specs=[IN_VMEM,...  5.24 us
    ppermute x3, starting transfers between devices, over_x(): return lax.ppermute(x, 'seq', [(i, (i + 8 * by) % 32) for i in range(32)])  4.88 us
    pallas_call x2, Pallas kernels, mix(): pl.pallas_call(lambda *refs: mix_kernel(by, last, *refs), in_specs=[IN_VM...  4.05 us
    pallas_call x1, Pallas kernels, far_end(): pl.pallas_call(far_end_kernel, in_specs=[IN_HBM] * 3, out_specs=[IN_VMEM]...  3.66 us
    pallas_call x1, Pallas kernels, own_end(): pl.pallas_call(own_end_kernel, in_specs=[IN_VMEM, IN_VMEM, IN_HBM, IN_HBM...  2.63 us
    ppermute x3, waiting for transfers between devices, over_x(): return lax.ppermute(x, 'seq', [(i, (i + 8 * by) % 32) for i in range(32)])  2.26 us
  transfers between devices with their start and end apart: 10, of which 5 were waited for; matrix products, arithmetic and copies ran while one was open for 0% of the time, Pallas kernels for 23%

profile of v6, /device:TPU:1, one launch (start us, length us, event | category | flops | bytes accessed | tf_op | source)
XLA Modules:
  0.0 42.4 jit_solution(14820778418150744260)
XLA Ops:
  0.0 3.7 %far_end.1 = (f32[16,1024]{1,0:T(8,128)S(1)}, f32[384,1024]{1,0:T(8,128)S(1)}, f32[384,1024]{1,0:T(8,128)S(1)}, bf16[384,512]{1,0:T(8,128)(2,1)S(1)}, bf16[384,512]{1,0:T(8,128)(2,1)S(1)}) custom-call(bf16[384,2048]{1,0:T(8,128)(2,1)} %key_ref.3, bf16[384,2048]{1,0:T(8,128)(2,1)} %value_ref.3, f32[16,2048]{1,0:T(8,128)} %refs_3_.1), custom_call_target="tpu_custom_call" | custom-call | flops 3910000128 | bytes 12546000 | tf_op jit(solution)/shard_map/far_end/pallas_call | solution.py:162
  3.7 2.2 %collective-permute-start = (f32[16,1024]{1,0:T(8,128)S(1)}, f32[16,1024]{1,0:T(8,128)S(1)}, u32[]{:S(2)}, u32[]{:S(2)}) collective-permute-start(f32[16,1024]{1,0:T(8,128)S(1)} %get-tuple-element.57), channel_id=1, source_target_pairs={{0,1},{1,0},{2,3},{3,2},{4,5},{5,4},{6,7},{7,6},{8,9},{9,8},{10,11... | collective-permute-start | bytes 196616 | tf_op jit(solution)/shard_map/ppermute | solution.py:501
  5.9 2.6 %own_end.1 = (f32[16,1024]{1,0:T(8,128)S(1)}, f32[384,1024]{1,0:T(8,128)S(1)}, f32[384,1024]{1,0:T(8,128)S(1)}, f32[7,16,1024]{2,1,0:T(8,128)S(1)}) custom-call(bf16[384,512]{1,0:T(8,128)(2,1)S(1)} %get-tuple-element.52.key_first, bf16[384,512]{1,0:T(8,128)(2,1)S(1)} %get-tuple-element.53.value_first, bf16[384,2048]{1,0:T(8,128)(2,1)} %key_ref.3, ...), custom_call_target="tpu_custom_call" | custom-call | flops 3104999936 | bytes 9963000 | tf_op jit(solution)/shard_map/own_end/pallas_call | solution.py:227
  8.5 0.0 collective-permute-done.got_ref
  8.6 2.0 %collective-permute-start.1 = (f32[16,1024]{1,0:T(8,128)S(1)}, f32[16,1024]{1,0:T(8,128)S(1)}, u32[]{:S(2)}, u32[]{:S(2)}) collective-permute-start(f32[16,1024]{1,0:T(8,128)S(1)} %pair_kernel.1.own_ref), channel_id=1, source_target_pairs={{0,3},{1,2},{2,1},{3,0},{4,7},{5,6},{6,5},{7,4},{8,11},{9,10},{10,... | collective-permute-start | bytes 196616 | tf_op jit(solution)/shard_map/ppermute | solution.py:501
  10.5 2.6 %local_part.2 = (f32[384,1024]{1,0:T(8,128)S(1)}, f32[384,1024]{1,0:T(8,128)S(1)}, f32[128,1024]{1,0:T(8,128)S(1)}, f32[128,1024]{1,0:T(8,128)S(1)}, f32[256,1024]{1,0:T(8,128)S(1)}, /*index=5*/f32[16,1024]{1,0:T(8,128)S(1)}) custom-call(f32[384,1024]{1,0:T(8,128)S(1)} %get-tuple-element.60.refs_0_, f32[384,1024]{1,0:T(8,128)S(1)} %get-tuple-element.61.refs_1_, ...), custom_call_target="tpu_custom_call" | custom-call | flops 2990000128 | bytes 9594000 | tf_op jit(solution)/shard_map/local_part/pallas_call | solution.py:366
  13.2 3.7 %collective-permute-start.2 = (f32[16,1024]{1,0:T(8,128)S(1)}, f32[16,1024]{1,0:T(8,128)S(1)}, u32[]{:S(2)}, u32[]{:S(2)}) collective-permute-start(f32[16,1024]{1,0:T(8,128)S(1)} %row_kernel.1.own_ref), channel_id=1, source_target_pairs={{0,4},{1,5},{2,6},{3,7},{4,0},{5,1},{6,2},{7,3},{8,12},{9,13},{10,... | collective-permute-start | bytes 196616 | tf_op jit(solution)/shard_map/ppermute | solution.py:501
  16.9 2.6 %local_part.3 = (f32[384,1024]{1,0:T(8,128)S(1)}, f32[384,1024]{1,0:T(8,128)S(1)}, f32[128,1024]{1,0:T(8,128)S(1)}, f32[128,1024]{1,0:T(8,128)S(1)}, f32[256,1024]{1,0:T(8,128)S(1)}, /*index=5*/f32[16,1024]{1,0:T(8,128)S(1)}) custom-call(f32[384,1024]{1,0:T(8,128)S(1)} %get-tuple-element.71.refs_0_, f32[384,1024]{1,0:T(8,128)S(1)} %get-tuple-element.72.refs_1_, ...), custom_call_target="tpu_custom_call" | custom-call | flops 2990000128 | bytes 9594000 | tf_op jit(solution)/shard_map/local_part/pallas_call | solution.py:366
  19.6 1.3 %collective-permute-start.3 = (f32[16,1024]{1,0:T(8,128)S(1)}, f32[16,1024]{1,0:T(8,128)S(1)}, u32[]{:S(2)}, u32[]{:S(2)}) collective-permute-start(f32[16,1024]{1,0:T(8,128)S(1)} %plane_kernel.1), channel_id=1, source_target_pairs={{0,8},{1,9},{2,10},{3,11},{4,12},{5,13},{6,14},{7,15},{8,16},{9,17... | collective-permute-start | bytes 196616 | tf_op jit(solution)/shard_map/ppermute | solution.py:505
  20.8 2.5 %collective-permute-start.4 = (f32[16,1024]{1,0:T(8,128)S(1)}, f32[16,1024]{1,0:T(8,128)S(1)}, u32[]{:S(2)}, u32[]{:S(2)}) collective-permute-start(f32[16,1024]{1,0:T(8,128)S(1)} %plane_kernel.1), channel_id=1, source_target_pairs={{0,16},{1,17},{2,18},{3,19},{4,20},{5,21},{6,22},{7,23},{8,24},{9,... | collective-permute-start | bytes 196616 | tf_op jit(solution)/shard_map/ppermute | solution.py:505
  23.3 1.2 %collective-permute-start.5 = (f32[16,1024]{1,0:T(8,128)S(1)}, f32[16,1024]{1,0:T(8,128)S(1)}, u32[]{:S(2)}, u32[]{:S(2)}) collective-permute-start(f32[16,1024]{1,0:T(8,128)S(1)} %plane_kernel.1), channel_id=1, source_target_pairs={{0,24},{1,25},{2,26},{3,27},{4,28},{5,29},{6,30},{7,31},{8,0},{9,1... | collective-permute-start | bytes 196616 | tf_op jit(solution)/shard_map/ppermute | solution.py:505
  24.5 1.2 %collective-permute-done.4.p2 = f32[16,1024]{1,0:T(8,128)S(1)} collective-permute-done((f32[16,1024]{1,0:T(8,128)S(1)}, f32[16,1024]{1,0:T(8,128)S(1)}, u32[]{:S(2)}, u32[]{:S(2)}) %collective-permute-start.4) | collective-permute-done | bytes 65568 | tf_op jit(solution)/shard_map/ppermute | solution.py:505
  25.6 1.1 %collective-permute-done.5.p3 = f32[16,1024]{1,0:T(8,128)S(1)} collective-permute-done((f32[16,1024]{1,0:T(8,128)S(1)}, f32[16,1024]{1,0:T(8,128)S(1)}, u32[]{:S(2)}, u32[]{:S(2)}) %collective-permute-start.5) | collective-permute-done | bytes 65568 | tf_op jit(solution)/shard_map/ppermute | solution.py:505
  26.7 0.1 states_kernel.1
  26.8 0.4 collective-permute-start.6
  27.2 2.0 %mix.2 = (f32[8,400,128]{2,1,0:T(8,128)S(1)}, f32[384,128]{1,0:T(8,128)S(1)}) custom-call(f32[384,1024]{1,0:T(8,128)S(1)} %get-tuple-element.80.refs_0_, f32[384,1024]{1,0:T(8,128)S(1)} %get-tuple-element.81.refs_1_, f32[128,1024]{1,0:T(8,128)S(1)} %get-tuple-element.82.refs_2_, f32[128,1024]{1,0:T(8,128)S(1)} %get-tuple-element.83.refs_3_, ...), custom_call_target="tpu_custom_call" | custom-call | flops 2415000064 | bytes 7749000 | tf_op jit(solution)/shard_map/mix/pallas_call | solution.py:429
  29.1 1.0 %collective-permute-done.6.refs_6_ = f32[16,1024]{1,0:T(8,128)S(1)} collective-permute-done((f32[16,1024]{1,0:T(8,128)S(1)}, f32[16,1024]{1,0:T(8,128)S(1)}, u32[]{:S(2)}, u32[]{:S(2)}) %collective-permute-start.6) | collective-permute-done | bytes 65568 | tf_op jit(solution)/shard_map/ppermute | solution.py:501
  30.1 2.1 %mix.3 = (f32[1,384]{1,0:T(1,128)S(1)}, f32[8,400,128]{2,1,0:T(8,128)S(1)}) custom-call(f32[384,1024]{1,0:T(8,128)S(1)} %get-tuple-element.89.refs_0_, f32[384,1024]{1,0:T(8,128)S(1)} %get-tuple-element.90.refs_1_, f32[128,1024]{1,0:T(8,128)S(1)} %get-tuple-element.91.refs_2_, f32[128,1024]{1,0:T(8,128)S(1)} %get-tuple-element.92.refs_3_, ...), custom_call_target="tpu_custom_call" | custom-call | flops 2415000064 | bytes 7749000 | tf_op jit(solution)/shard_map/mix/pallas_call | solution.py:429
  32.2 4.9 %collective-permute-start.7 = (f32[1,384]{1,0:T(1,128)S(1)}, f32[1,384]{1,0:T(1,128)S(1)}, u32[]{:S(2)}, u32[]{:S(2)}) collective-permute-start(f32[1,384]{1,0:T(1,128)S(1)} %get-tuple-element.98.p0_ref), channel_id=1, source_target_pairs={{0,32},{32,0},{64,96},{96,64},{1,33},{33,1},{65,97},{97,65},{2,34}... | collective-permute-start | bytes 4616 | tf_op jit(solution)/shard_map/ppermute | solution.py:509
  37.1 0.9 %collective-permute-start.8 = (f32[1,384]{1,0:T(1,128)S(1)}, f32[1,384]{1,0:T(1,128)S(1)}, u32[]{:S(2)}, u32[]{:S(2)}) collective-permute-start(f32[1,384]{1,0:T(1,128)S(1)} %get-tuple-element.98.p0_ref), channel_id=1, source_target_pairs={{0,64},{32,96},{64,0},{96,32},{1,65},{33,97},{65,1},{97,33},{2,66}... | collective-permute-start | bytes 4616 | tf_op jit(solution)/shard_map/ppermute | solution.py:509
  38.0 0.8 %collective-permute-start.9 = (f32[1,384]{1,0:T(1,128)S(1)}, f32[1,384]{1,0:T(1,128)S(1)}, u32[]{:S(2)}, u32[]{:S(2)}) collective-permute-start(f32[1,384]{1,0:T(1,128)S(1)} %get-tuple-element.98.p0_ref), channel_id=1, source_target_pairs={{0,96},{32,64},{64,32},{96,0},{1,97},{33,65},{65,33},{97,1},{2,98}... | collective-permute-start | bytes 4616 | tf_op jit(solution)/shard_map/ppermute | solution.py:509
  38.8 0.7 %collective-permute-done.8.p2_ref = f32[1,384]{1,0:T(1,128)S(1)} collective-permute-done((f32[1,384]{1,0:T(1,128)S(1)}, f32[1,384]{1,0:T(1,128)S(1)}, u32[]{:S(2)}, u32[]{:S(2)}) %collective-permute-start.8) | collective-permute-done | bytes 1568 | tf_op jit(solution)/shard_map/ppermute | solution.py:509
  39.5 1.5 %collective-permute-done.9.p3_ref = f32[1,384]{1,0:T(1,128)S(1)} collective-permute-done((f32[1,384]{1,0:T(1,128)S(1)}, f32[1,384]{1,0:T(1,128)S(1)}, u32[]{:S(2)}, u32[]{:S(2)}) %collective-permute-start.9) | collective-permute-done | bytes 1568 | tf_op jit(solution)/shard_map/ppermute | solution.py:509
  41.0 1.5 %norm.1 = bf16[384,2048]{1,0:T(8,128)(2,1)} custom-call(f32[8,400,128]{2,1,0:T(8,128)S(1)} %get-tuple-element.88.g0, f32[8,400,128]{2,1,0:T(8,128)S(1)} %get-tuple-element.97.g1, f32[1,2048]{1,0:T(1,128)S(1)} %bitcast.4, f32[1,384]{1,0:T(1,128)S(1)} %get-tuple-element.98.p0_ref, f32[1,384]{1,0:T(1,128)S(1)} %collective-permute-done.7.p1_ref, ...), custom_call_target="tpu_custom_call" | custom-call | flops 1955000064 | bytes 6273000 | tf_op jit(solution)/shard_map/norm/pallas_call | solution.py:483
  (15 shorter events, 0.1 us)
Async XLA Ops:
  0.0 5.9 %copy-start = (f32[16,2048]{1,0:T(8,128)S(1)}, f32[16,2048]{1,0:T(8,128)}, u32[]{:S(2)}) copy-start(f32[16,2048]{1,0:T(8,128)} %refs_3_.1) | copy-start | bytes 393220
  3.7 4.8 %collective-permute-start = (f32[16,1024]{1,0:T(8,128)S(1)}, f32[16,1024]{1,0:T(8,128)S(1)}, u32[]{:S(2)}, u32[]{:S(2)}) collective-permute-start(f32[16,1024]{1,0:T(8,128)S(1)} %get-tuple-element.57), channel_id=1, source_target_pairs={{0,1},{1,0},{2,3},{3,2},{4,5},{5,4},{6,7},{7,6},{8,9},{9,8},{10,11... | collective-permute-start | bytes 196616 | tf_op jit(solution)/shard_map/ppermute | solution.py:501
  5.9 4.7 %copy-start.1 = (f32[16,2048]{1,0:T(8,128)S(1)}, f32[16,2048]{1,0:T(8,128)}, u32[]{:S(2)}) copy-start(f32[16,2048]{1,0:T(8,128)} %refs_4_.3) | copy-start | bytes 393220
  5.9 4.7 %copy-start.2 = (f32[2048]{0:T(1024)S(1)}, f32[2048]{0:T(1024)}, u32[]{:S(2)}) copy-start(f32[2048]{0:T(1024)} %param.12) | copy-start | bytes 24580
  8.6 4.6 %collective-permute-start.1 = (f32[16,1024]{1,0:T(8,128)S(1)}, f32[16,1024]{1,0:T(8,128)S(1)}, u32[]{:S(2)}, u32[]{:S(2)}) collective-permute-start(f32[16,1024]{1,0:T(8,128)S(1)} %pair_kernel.1.own_ref), channel_id=1, source_target_pairs={{0,3},{1,2},{2,1},{3,0},{4,7},{5,6},{6,5},{7,4},{8,11},{9,10},{10,... | collective-permute-start | bytes 196616 | tf_op jit(solution)/shard_map/ppermute | solution.py:501
  13.2 6.3 %collective-permute-start.2 = (f32[16,1024]{1,0:T(8,128)S(1)}, f32[16,1024]{1,0:T(8,128)S(1)}, u32[]{:S(2)}, u32[]{:S(2)}) collective-permute-start(f32[16,1024]{1,0:T(8,128)S(1)} %row_kernel.1.own_ref), channel_id=1, source_target_pairs={{0,4},{1,5},{2,6},{3,7},{4,0},{5,1},{6,2},{7,3},{8,12},{9,13},{10,... | collective-permute-start | bytes 196616 | tf_op jit(solution)/shard_map/ppermute | solution.py:501
  19.6 4.9 %collective-permute-start.3 = (f32[16,1024]{1,0:T(8,128)S(1)}, f32[16,1024]{1,0:T(8,128)S(1)}, u32[]{:S(2)}, u32[]{:S(2)}) collective-permute-start(f32[16,1024]{1,0:T(8,128)S(1)} %plane_kernel.1), channel_id=1, source_target_pairs={{0,8},{1,9},{2,10},{3,11},{4,12},{5,13},{6,14},{7,15},{8,16},{9,17... | collective-permute-start | bytes 196616 | tf_op jit(solution)/shard_map/ppermute | solution.py:505
  20.8 4.8 %collective-permute-start.4 = (f32[16,1024]{1,0:T(8,128)S(1)}, f32[16,1024]{1,0:T(8,128)S(1)}, u32[]{:S(2)}, u32[]{:S(2)}) collective-permute-start(f32[16,1024]{1,0:T(8,128)S(1)} %plane_kernel.1), channel_id=1, source_target_pairs={{0,16},{1,17},{2,18},{3,19},{4,20},{5,21},{6,22},{7,23},{8,24},{9,... | collective-permute-start | bytes 196616 | tf_op jit(solution)/shard_map/ppermute | solution.py:505
  23.3 3.4 %collective-permute-start.5 = (f32[16,1024]{1,0:T(8,128)S(1)}, f32[16,1024]{1,0:T(8,128)S(1)}, u32[]{:S(2)}, u32[]{:S(2)}) collective-permute-start(f32[16,1024]{1,0:T(8,128)S(1)} %plane_kernel.1), channel_id=1, source_target_pairs={{0,24},{1,25},{2,26},{3,27},{4,28},{5,29},{6,30},{7,31},{8,0},{9,1... | collective-permute-start | bytes 196616 | tf_op jit(solution)/shard_map/ppermute | solution.py:505
  26.8 3.3 %collective-permute-start.6 = (f32[16,1024]{1,0:T(8,128)S(1)}, f32[16,1024]{1,0:T(8,128)S(1)}, u32[]{:S(2)}, u32[]{:S(2)}) collective-permute-start(f32[16,1024]{1,0:T(8,128)S(1)} %get-tuple-element.95), channel_id=1, source_target_pairs={{0,1},{1,0},{2,3},{3,2},{4,5},{5,4},{6,7},{7,6},{8,9},{9,8},{10,11... | collective-permute-start | bytes 196616 | tf_op jit(solution)/shard_map/ppermute | solution.py:501
  30.1 10.9 %copy-start.3 = (f32[2048]{0:T(1024)S(1)}, f32[2048]{0:T(1024)}, u32[]{:S(2)}) copy-start(f32[2048]{0:T(1024)} %param.13) | copy-start | bytes 24580
  32.2 6.6 %collective-permute-start.7 = (f32[1,384]{1,0:T(1,128)S(1)}, f32[1,384]{1,0:T(1,128)S(1)}, u32[]{:S(2)}, u32[]{:S(2)}) collective-permute-start(f32[1,384]{1,0:T(1,128)S(1)} %get-tuple-element.98.p0_ref), channel_id=1, source_target_pairs={{0,32},{32,0},{64,96},{96,64},{1,33},{33,1},{65,97},{97,65},{2,34}... | collective-permute-start | bytes 4616 | tf_op jit(solution)/shard_map/ppermute | solution.py:509
  37.1 2.4 %collective-permute-start.8 = (f32[1,384]{1,0:T(1,128)S(1)}, f32[1,384]{1,0:T(1,128)S(1)}, u32[]{:S(2)}, u32[]{:S(2)}) collective-permute-start(f32[1,384]{1,0:T(1,128)S(1)} %get-tuple-element.98.p0_ref), channel_id=1, source_target_pairs={{0,64},{32,96},{64,0},{96,32},{1,65},{33,97},{65,1},{97,33},{2,66}... | collective-permute-start | bytes 4616 | tf_op jit(solution)/shard_map/ppermute | solution.py:509
  38.0 3.0 %collective-permute-start.9 = (f32[1,384]{1,0:T(1,128)S(1)}, f32[1,384]{1,0:T(1,128)S(1)}, u32[]{:S(2)}, u32[]{:S(2)}) collective-permute-start(f32[1,384]{1,0:T(1,128)S(1)} %get-tuple-element.98.p0_ref), channel_id=1, source_target_pairs={{0,96},{32,64},{64,32},{96,0},{1,97},{33,65},{65,33},{97,1},{2,98}... | collective-permute-start | bytes 4616 | tf_op jit(solution)/shard_map/ppermute | solution.py:509
